TPU v7x, 256 devices: a whole 4x4x8 slice. The times are simulated.
256 devices in a mesh: row: 4 (over y_hi, core), col: 8 (over z), aux: 8 (over x, y_lo).
Axes of the slice: x: 4, y: 4 (y_hi: 2, y_lo: 2; y = y_hi * 2 + y_lo), z: 8, core: 2. Of those that a mesh axis runs over, the one named last changes fastest.
Arguments:
- integrals: bfloat16 [8, 256, 64, 3072], P('aux', ('row', 'col')), may hold values from -0.75 to 0.75
- block_mask: int32 [8, 64, 64], P('aux', ('row', 'col')), may hold values from 0 to 1, as said below
- block_slots: int32 [8, 64, 64], P('aux', ('row', 'col')), may hold values from -1 to 7, as said below
- orbitals: bfloat16 [64, 4096], replicated, may hold values from -0.107910156 to 0.107910156
Outputs:
- exchange_matrix: float32 [4096, 4, 1024], P(('row', 'aux'), None, 'col')
Inputs may be any that keep to these rules, and one draw needn't show every extreme that they name: `block_mask`: within one device's tile (one auxiliary batch, the mu blocks of one row and col index pair, all lambda blocks) between 1 and 8 blocks survive, and in some tile exactly 8. `block_slots`: the surviving blocks of a tile are numbered 0, 1, 2, ... in row-major order of (mu block, lambda block); blocks that did not survive hold -1, and packed slots past a tile's count hold data that is never read.
All inputs are finite; a program needn't handle non-finite values.
Results may differ from a plain program's by a relative error of at most 0.0017.
Values may be sent and summed in bfloat16 or wider, within the bound.
No kernel may reach another device: no remote copies, remote signals or barrier semaphores. Data moves between devices by JAX's collectives and lax.ppermute only.
A program may use at most 128 MiB of HBM per device.

v0:
```python
import jax
import jax.numpy as jnp
from jax import lax
from jax.sharding import PartitionSpec as P


def half_transform(mask_tile, slot_tile, packed_tile, orbitals):
    capacity = packed_tile.shape[0]
    block_size = packed_tile.shape[1]
    row_blocks, block_count = mask_tile.shape
    occ_count = orbitals.shape[0]
    aux_count = packed_tile.shape[2] // block_size
    mask_flat = mask_tile.reshape(-1)
    slot_flat = slot_tile.reshape(-1)
    positions = jnp.arange(mask_flat.shape[0], dtype=jnp.int32)
    slot_ids = jnp.arange(capacity, dtype=jnp.int32)
    select = ((mask_flat[None, :] == 1) & (slot_flat[None, :] == slot_ids[:, None])).astype(
        jnp.int32
    )
    block_row = jnp.sum(select * (positions // block_count)[None, :], axis=1)
    lam_block = jnp.sum(select * (positions % block_count)[None, :], axis=1)
    present = jnp.sum(select, axis=1).astype(jnp.float32)
    weights = (block_row[:, None] == jnp.arange(row_blocks, dtype=jnp.int32)[None, :]).astype(
        jnp.float32
    ) * present[:, None]
    orbital_blocks = jnp.take(
        orbitals.reshape(occ_count, block_count, block_size), lam_block, axis=1
    )
    products = jnp.einsum(
        "isx,sxy->siy", orbital_blocks, packed_tile, preferred_element_type=jnp.float32
    )
    products = products.reshape(capacity, occ_count, aux_count, block_size)
    half_block = jnp.einsum("sb,siqm->iqbm", weights, products, precision=lax.Precision.HIGHEST)
    return half_block.reshape(occ_count, aux_count, row_blocks * block_size).astype(jnp.bfloat16)


def local(integrals, block_mask, block_slots, orbitals):
    half_local = half_transform(block_mask[0], block_slots[0], integrals[0], orbitals)
    occ_count, aux_count, local_rows = half_local.shape
    row_index = lax.axis_index("row")
    col_index = lax.axis_index("col")
    row_count = lax.axis_size("row")
    col_count = lax.axis_size("col")
    contract = (((0, 1), (0, 1)), ((), ()))
    gathered = lax.all_gather(half_local, ("row", "col"), axis=2, tiled=True)
    rows_panel = lax.dynamic_slice_in_dim(
        gathered, row_index * col_count * local_rows, col_count * local_rows, 2
    )
    grid_view = gathered.reshape(occ_count, aux_count, row_count, col_count, local_rows)
    column_panel = lax.dynamic_index_in_dim(grid_view, col_index, 3, keepdims=False)
    exchange_tile = lax.dot_general(
        rows_panel, column_panel, contract, preferred_element_type=jnp.float32
    )
    return lax.psum_scatter(exchange_tile, "aux", scatter_dimension=0, tiled=True)


def solution(mesh):
    placed = (
        P("aux", ("row", "col"), None, None),
        P("aux", ("row", "col"), None),
        P("aux", ("row", "col"), None),
        P(),
    )
    return jax.shard_map(
        local, mesh=mesh, in_specs=placed, out_specs=P(("row", "aux"), None, "col"), check_vma=False
    )
```

profile of v0, /device:TPU:16, one launch (start us, length us, event | category | flops | bytes accessed | tf_op | source)
XLA Modules:
  0.0 344.4 jit_solution(12587228098716600738)
XLA Ops:
  6.5 0.0 copy-start
  6.5 0.0 all-gather.2.cloned.1.call-start
  6.5 0.8 broadcast_compare_fusion
  7.4 0.1 eq.48
  7.5 0.8 eq.49
  8.3 0.1 select_reduce_fusion
  8.5 2.8 reshape.65
  11.2 2.9 copy.18
  14.2 1.8 gather_fusion
  16.0 0.0 copy-done
  16.0 3.6 %fusion.5 = f32[8,64,3072]{2,1,0:T(8,128)} fusion(bf16[1,8,64,3072]{3,2,1,0:T(8,128)(2,1)S(1)} %copy-done, bf16[8,64,64]{2,1,0:T(8,128)(2,1)S(1)} %gather_fusion, pred[8]{0:T(512)(128)(4,1)S(1)} %compare_and_fusion), kind=kOutput, calls=%fused_computation.7 | convolution fusion | flops 201359360 | bytes 9502728 | tf_op jit(solution)/shard_map/isx,sxy->siy/dot_general | solution.py:29
  19.6 10.0 %reshape.66 = f32[8,64,48,64]{3,2,1,0:T(8,128)} reshape(f32[8,64,3072]{2,1,0:T(8,128)} %fusion.5) | data formatting | bytes 12582912 | tf_op jit(solution)/shard_map/reshape | solution.py:32
  29.6 21.8 %fusion.13 = bf16[64,48,2,64]{3,2,1,0:T(2,128)(2,1)S(1)} fusion(f32[8,64,48,64]{3,2,1,0:T(8,128)} %reshape.66, f32[8]{0:T(128)S(1)} %convert_element_type.21, s32[8]{0:T(128)S(1)} %get-tuple-element.5), kind=kOutput, calls=%fused_computation.11 | convolution fusion | flops 38141984 | bytes 7077952 | tf_op jit(solution)/shard_map/sb,siqm->iqbm/dot_general | solution.py:33
  51.4 0.7 convert_element_type.24
  52.1 1.1 copy.20
  53.3 0.0 all-gather.2.cloned.1.call-update
  53.3 0.0 reduce-scatter.2.cloned.1.call-start
  53.4 200.5 %all-gather.2.cloned.1.call-done = bf16[64,48,4096]{2,0,1:T(8,128)(2,1)} async-done(((bf16[64,48,128]{2,0,1:T(8,128)(2,1)}), bf16[64,48,4096]{2,0,1:T(8,128)(2,1)}) %all-gather.2.cloned.1.call-update) | async-done | bytes 25165840 | tf_op jit(solution)/shard_map/all_gather | solution.py:45
  253.8 14.2 %copy.26 = bf16[384,8,32,128]{3,2,1,0:T(8,128)(2,1)S(1)} copy(bf16[384,8,32,128]{3,1,2,0:T(8,128)(2,1)} %bitcast.37) | data formatting | bytes 50331648
  268.1 6.7 %constant_dynamic-slice_fusion = bf16[64,48,4,1,128]{4,3,2,0,1:T(2,128)(2,1)S(1)} fusion(bf16[64,48,4,8,128]{4,3,2,0,1:T(8,128)(2,1)S(1)} %bitcast.36, s32[]{:T(128)S(6)} %select_n.53), kind=kLoop, calls=%fused_computation.37 | loop fusion | bytes 6291460 | tf_op jit(solution)/shard_map/jit(dynamic_index_in_dim)/dynamic_slice | solution.py:50
  274.8 0.0 copy-start.1
  274.8 7.8 %fusion.10 = f32[1024,4,128]{2,0,1:T(8,128)} fusion(bf16[64,48,4,1,128]{4,3,2,0,1:T(2,128)(2,1)S(1)} %constant_dynamic-slice_fusion, bf16[64,48,4096]{2,0,1:T(8,128)(2,1)} %all-gather.2.cloned.1.call-done, s32[]{:T(128)S(6)} %select_n.52), kind=kOutput, calls=%fused_computation.10 | convolution fusion | flops 3221225472 | bytes 11534340 | tf_op jit(solution)/shard_map/dot_general | solution.py:51
  282.6 0.0 reduce-scatter.2.cloned.1.call-update
  282.6 53.1 %reduce-scatter.2.cloned.1.call-done = f32[128,4,128]{2,0,1:T(8,128)} async-done(((f32[1024,4,128]{2,0,1:T(8,128)}), f32[128,4,128]{2,0,1:T(8,128)}) %reduce-scatter.2.cloned.1.call-update) | async-done | bytes 262160 | tf_op jit(solution)/shard_map/reduce_scatter | solution.py:54
  335.7 1.8 copy.22
  337.6 0.0 copy-done.1
  (5 shorter events, 0.0 us)
Async XLA Ops:
  6.5 9.4 %copy-start = (bf16[1,8,64,3072]{3,2,1,0:T(8,128)(2,1)S(1)}, bf16[1,8,64,3072]{3,2,1,0:T(8,128)(2,1)}, u32[]{:S(2)}) copy-start(bf16[1,8,64,3072]{3,2,1,0:T(8,128)(2,1)} %param.4) | copy-start | bytes 9437188
  6.5 247.3 %all-gather.2.cloned.1.call-start = ((), (), s32[]{:S(2)}) async-start(), calls=%async_computation.1 | async-start | bytes 25952256 | tf_op jit(solution)/shard_map/all_gather | solution.py:45
  53.3 282.4 %reduce-scatter.2.cloned.1.call-start = ((), (), s32[]{:S(2)}) async-start(), calls=%async_computation.2 | async-start | bytes 2359296 | tf_op jit(solution)/shard_map/reduce_scatter | solution.py:54
  274.8 62.8 %copy-start.1 = (bf16[1,8,64,3072]{3,2,1,0:T(8,128)(2,1)S(1)}, bf16[1,8,64,3072]{3,2,1,0:T(8,128)(2,1)}, u32[]{:S(2)}) copy-start(bf16[1,8,64,3072]{3,2,1,0:T(8,128)(2,1)} %param.4) | copy-start | bytes 9437188
Sparse Core Ops, SparseCore 0:
  53.4 200.3 all-gather.1
  282.7 52.9 reduce-scatter.1
where the time goes:
time: 345 us; the launch traced here: 344 us
  waiting for transfers between devices  254 us (74%)
  local copies, waits for them, and re-layouts  43 us (12%)
  matrix products  33.2 us (10%)
  between operations  13.5 us (4%)
    all_gather x1, waiting for transfers between devices, local(): gathered = lax.all_gather(half_local, ('row', 'col'), axis=2, tiled=True)  200 us
    reduce_scatter x1, waiting for transfers between devices, local(): lax.psum_scatter(exchange_tile, 'aux', scatter_dimension=0, tiled=True)  53.1 us
    dot_general x1, matrix products, half_transform(): jnp.einsum('sb,siqm->iqbm', weights, products, precision=lax.Precision.HI...  21.8 us
    unnamed x5, local copies, waits for them, and re-layouts  14.2 us
    reshape x1, local copies, waits for them, and re-layouts, half_transform(): products = products.reshape(capacity, occ_count, aux_count, block_size)  9.96 us
    dot_general x1, matrix products, local(): lax.dot_general(rows_panel, column_panel, contract, preferred_element_typ...  7.78 us
  transfers between devices with their start and end apart: 2, of which 2 were waited for; matrix products, arithmetic and copies ran while one was open for 0% of the time, Pallas kernels for 0%

commit v1 on v0

v1 whole, which is shorter than its diff:
```python
import functools

import jax
import jax.numpy as jnp
from jax import lax
from jax.experimental import pallas as pl
from jax.experimental.pallas import tpu as pltpu
from jax.sharding import PartitionSpec as P

VMEM_LIMIT = 48 * 1024 * 1024
CHUNKS = 4


def half_kernel(swap_ref, mask_ref, slot_ref, orb_ref, int_ref, whole_ref, a0_ref, a1_ref, b0_ref, b1_ref, place_ref, weight_ref):
    step = pl.program_id(0)
    occ = orb_ref.shape[0]
    capacity, block, lanes = int_ref.shape
    row_blocks, block_count = mask_ref.shape
    low = lax.broadcasted_iota(jnp.int32, (occ, 2 * block), 1) < block

    @pl.when(step == 0)
    def _():
        for s in range(capacity):
            place_ref[s] = -1
        for b in range(row_blocks):
            for l in range(block_count):
                slot = slot_ref[b, l]
                valid = (mask_ref[b, l] == 1) & (slot >= 0) & (slot < capacity)
                place_ref[jnp.where(valid, slot, capacity)] = b * block_count + l
        for pair in range(capacity // 2):
            parts = []
            for s in (2 * pair, 2 * pair + 1):
                place = place_ref[s]
                at = jnp.maximum(place, 0)
                b = at // block_count
                l = at % block_count
                columns = orb_ref[:, pl.ds(pl.multiple_of((l // 2) * (2 * block), 2 * block), 2 * block)].astype(jnp.float32)
                turned = pltpu.roll(columns, block, 1)
                value = jnp.where((l % 2) == (s % 2), columns, turned)
                parts.append((place, b, value))
            for b in range(row_blocks):
                chosen = [
                    jnp.where((place >= 0) & (home == b), value, 0.0) for place, home, value in parts
                ]
                weight_ref[b * occ : (b + 1) * occ, pair * 2 * block : (pair + 1) * 2 * block] = jnp.where(
                    low, chosen[0], chosen[1]
                ).astype(weight_ref.dtype)

    packed = int_ref[...].reshape(capacity * block, lanes)
    product = jnp.dot(weight_ref[...], packed, preferred_element_type=jnp.float32)
    pieces = []
    for pair in range(lanes // (2 * block)):
        first = product[:occ, pair * 2 * block : (pair + 1) * 2 * block]
        second = product[occ:, pair * 2 * block : (pair + 1) * 2 * block]
        pieces.append(jnp.where(low, first, pltpu.roll(second, block, 1)))
        pieces.append(jnp.where(low, pltpu.roll(first, block, 1), second))
    result = jnp.concatenate(pieces, axis=0).astype(whole_ref.dtype)
    whole_ref[...] = result
    swap = swap_ref[0]
    for target, out_ref in enumerate((a0_ref, a1_ref, b0_ref, b1_ref)):
        @pl.when(step == (target // 2) * 2 + ((target % 2) ^ swap))
        def _(out_ref=out_ref):
            out_ref[...] = result


def half_transform(swap, mask, slots, packed, orbitals):
    capacity, block, width = packed.shape
    occ = orbitals.shape[0]
    lanes = width // CHUNKS
    rows = lanes // block * occ
    chunk = jax.ShapeDtypeStruct((rows, 2 * block), jnp.bfloat16)
    smem = pl.BlockSpec(memory_space=pltpu.SMEM)
    fixed = pl.BlockSpec((rows, 2 * block), lambda g: (0, 0))
    return pl.pallas_call(
        half_kernel,
        grid=(CHUNKS,),
        out_shape=(jax.ShapeDtypeStruct((rows * CHUNKS, 2 * block), jnp.bfloat16),) + (chunk,) * 4,
        in_specs=[
            smem,
            smem,
            smem,
            pl.BlockSpec(orbitals.shape, lambda g: (0, 0)),
            pl.BlockSpec((capacity, block, lanes), lambda g: (0, 0, g)),
        ],
        out_specs=(pl.BlockSpec((rows, 2 * block), lambda g: (g, 0)),) + (fixed,) * 4,
        scratch_shapes=[
            pltpu.SMEM((capacity + 1,), jnp.int32),
            pltpu.VMEM((2 * occ, capacity * block), jnp.bfloat16),
        ],
        compiler_params=pltpu.CompilerParams(vmem_limit_bytes=VMEM_LIMIT),
        cost_estimate=pl.CostEstimate(flops=2 * 2 * occ * capacity * block * width, bytes_accessed=5 << 20, transcendentals=0),
    )(swap, mask, slots, orbitals, packed)


def columns_at(col_refs, start, rows):
    return jnp.concatenate([ref[pl.ds(start, rows), :] for ref in col_refs], axis=1)


CONTRACT = (((0,), (0,)), ((), ()))


def tiles_kernel(pos_ref, *refs):
    col_refs = refs[:4]
    moved = refs[4:16]
    out_ref = refs[16]
    col = pos_ref[0]
    rows = moved[0].shape[0]
    ring = out_ref.shape[0]
    own = None
    for part in range(4):
        term = lax.dot_general(
            col_refs[0][part * rows : (part + 1) * rows, :],
            columns_at(col_refs, part * rows, rows),
            CONTRACT,
            preferred_element_type=jnp.float32,
        )
        own = term if own is None else own + term
    out_ref[col] = own.astype(out_ref.dtype)
    for d in range(1, 4):
        for side in range(2):
            origin = lax.rem(col + (d if side == 0 else ring - d), ring)
            swap = (origin < ring // 2).astype(jnp.int32)
            total = None
            for part in range(2):
                start = pl.multiple_of((2 * side + (part ^ swap)) * rows, rows)
                term = lax.dot_general(
                    moved[(d - 1) * 4 + side * 2 + part][...],
                    columns_at(col_refs, start, rows),
                    CONTRACT,
                    preferred_element_type=jnp.float32,
                )
                total = term if total is None else total + term
            out_ref[origin] = total.astype(out_ref.dtype)


def tiles(pos, col_panels, moved, ring):
    rows, width = moved[0].shape
    return pl.pallas_call(
        tiles_kernel,
        out_shape=jax.ShapeDtypeStruct((ring, width, 4 * width), jnp.bfloat16),
        in_specs=[pl.BlockSpec(memory_space=pltpu.SMEM)] + [pl.BlockSpec(memory_space=pltpu.VMEM)] * 16,
        out_specs=pl.BlockSpec(memory_space=pltpu.VMEM),
        compiler_params=pltpu.CompilerParams(vmem_limit_bytes=VMEM_LIMIT),
        cost_estimate=pl.CostEstimate(flops=2 * width * 4 * width * rows * 16, bytes_accessed=7 << 20, transcendentals=0),
    )(pos, *col_panels, *moved)


def last_tile_kernel(pos_ref, old_ref, a_ref, b_ref, *refs):
    col_refs, out_ref = refs[:8], refs[8]
    total = None
    for side, ref in enumerate((a_ref, b_ref)):
        term = lax.dot_general(
            ref[...],
            jnp.concatenate([c[...] for c in col_refs[side * 4 : side * 4 + 4]], axis=1),
            CONTRACT,
            preferred_element_type=jnp.float32,
        )
        total = term if total is None else total + term
    out_ref[0] = total.astype(out_ref.dtype)


def last_tile(pos, sums, a_far, b_far, col_panels):
    ring, width, wide = sums.shape
    rows = a_far.shape[0]
    far = lambda pos: lax.rem(pos[0] + ring // 2, ring)
    swapped = lambda pos: (far(pos) < ring // 2).astype(jnp.int32)
    full = pl.BlockSpec((rows, width), lambda g, pos: (0, 0))
    col_specs = [
        pl.BlockSpec((rows, width), lambda g, pos, side=side: (2 * side + swapped(pos), 0))
        for side in range(2)
        for _ in range(4)
    ]
    return pl.pallas_call(
        last_tile_kernel,
        grid_spec=pltpu.PrefetchScalarGridSpec(
            num_scalar_prefetch=1,
            grid=(1,),
            in_specs=[pl.BlockSpec(memory_space=pl.ANY), full, full] + col_specs,
            out_specs=pl.BlockSpec((1, width, wide), lambda g, pos: (far(pos), 0, 0)),
        ),
        out_shape=jax.ShapeDtypeStruct(sums.shape, sums.dtype),
        input_output_aliases={1: 0},
        compiler_params=pltpu.CompilerParams(vmem_limit_bytes=VMEM_LIMIT),
        cost_estimate=pl.CostEstimate(flops=4 * width * wide * rows, bytes_accessed=2 << 20, transcendentals=0),
    )(pos, sums, a_far, b_far, *col_panels, *col_panels)


def sum_kernel(in_ref, *out_refs):
    total = in_ref[0].astype(jnp.float32)
    for a in range(1, in_ref.shape[0]):
        total = total + in_ref[a].astype(jnp.float32)
    width = out_refs[0].shape[1]
    for rho, ref in enumerate(out_refs):
        ref[...] = total[:, rho * width : (rho + 1) * width]


def sum_parts(received):
    count, width, wide = received.shape
    return pl.pallas_call(
        sum_kernel,
        out_shape=(jax.ShapeDtypeStruct((width, width), jnp.float32),) * (wide // width),
        compiler_params=pltpu.CompilerParams(vmem_limit_bytes=VMEM_LIMIT),
        cost_estimate=pl.CostEstimate(flops=count * width * wide, bytes_accessed=2 * count * width * wide, transcendentals=0),
    )(received)


def finish_kernel(pos_ref, *refs):
    own, other, out_ref = refs[:4], refs[4:8], refs[8]
    row = pos_ref[1]
    diagonal = pos_ref[0] == pos_ref[2]
    for rho in range(4):
        back = jnp.where(diagonal, 0.0, other[rho][...].T)
        out_ref[:, row ^ rho, :] = own[rho][...] + back


def finish(pos, own, other):
    width = own[0].shape[0]
    return pl.pallas_call(
        finish_kernel,
        out_shape=jax.ShapeDtypeStruct((width, 4, width), jnp.float32),
        in_specs=[pl.BlockSpec(memory_space=pltpu.SMEM)] + [pl.BlockSpec(memory_space=pltpu.VMEM)] * 8,
        out_specs=pl.BlockSpec(memory_space=pltpu.VMEM),
        compiler_params=pltpu.CompilerParams(vmem_limit_bytes=VMEM_LIMIT),
    )(pos, *own, *other)


def local(integrals, block_mask, block_slots, orbitals):
    row, col, aux = lax.axis_index("row"), lax.axis_index("col"), lax.axis_index("aux")
    ring, rows_n, aux_n = lax.axis_size("col"), lax.axis_size("row"), lax.axis_size("aux")
    pos = jnp.stack([col, row, aux]).astype(jnp.int32)
    swap = (col < ring // 2).astype(jnp.int32).reshape(1)
    whole, a0, a1, b0, b1 = half_transform(swap, block_mask[0], block_slots[0], integrals[0], orbitals)

    down = [(i, (i - 1) % ring) for i in range(ring)]
    up = [(i, (i + 1) % ring) for i in range(ring)]
    core = [(i, i ^ 1) for i in range(rows_n)]
    across = [(i, i ^ 2) for i in range(rows_n)]

    moved = []
    held = [a0, a1, b0, b1]
    for _ in range(3):
        held = [
            lax.ppermute(held[0], "col", down),
            lax.ppermute(held[1], "col", down),
            lax.ppermute(held[2], "col", up),
            lax.ppermute(held[3], "col", up),
        ]
        moved += held
    a_far = lax.ppermute(held[0], "col", down)
    b_far = lax.ppermute(held[2], "col", up)

    beside = lax.ppermute(whole, "row", core)
    over = lax.ppermute(whole, "row", across)
    diagonal = lax.ppermute(over, "row", core)
    col_panels = [whole, beside, over, diagonal]

    sums = tiles(pos, col_panels, moved, ring)
    sums = last_tile(pos, sums, a_far, b_far, col_panels)
    received = lax.all_to_all(sums, "aux", 0, 0, tiled=True)
    own = sum_parts(received)

    def flip(rho):
        return [
            ((r * ring + z) * aux_n + a, ((r ^ rho) * ring + a) * aux_n + z)
            for r in range(rows_n)
            for z in range(ring)
            for a in range(aux_n)
        ]

    other = [lax.ppermute(own[rho], ("row", "col", "aux"), flip(rho)) for rho in range(rows_n)]
    return finish(pos, own, other)


def solution(mesh):
    placed = (
        P("aux", ("row", "col"), None, None),
        P("aux", ("row", "col"), None),
        P("aux", ("row", "col"), None),
        P(),
    )
    return jax.shard_map(
        local, mesh=mesh, in_specs=placed, out_specs=P(("row", "aux"), None, "col"), check_vma=False
    )
```

time: 345 us -> 119 us (0.34)
  the two profiles are of different devices: /device:TPU:16 before, /device:TPU:5 now
where the time goes in v1:
time: 119 us
  starting transfers between devices  49.2 us (41%)
  waiting for transfers between devices  33.4 us (28%)
  blocking collectives  14.1 us (12%)
  local copies, waits for them, and re-layouts  11.9 us (10%)
  Pallas kernels  9.93 us (8%)
    ppermute x4, starting transfers between devices, local(): lax.ppermute(own[rho], ('row', 'col', 'aux'), flip(rho))  23.8 us
    all_to_all x1, blocking collectives, local(): received = lax.all_to_all(sums, 'aux', 0, 0, tiled=True)  14.1 us
    ppermute x4, waiting for transfers between devices, local(): lax.ppermute(own[rho], ('row', 'col', 'aux'), flip(rho))  12 us
    unnamed x26, local copies, waits for them, and re-layouts  11.9 us
    ppermute x3, starting transfers between devices, local(): lax.ppermute(held[0], 'col', down)  10.9 us
    ppermute x3, waiting for transfers between devices, local(): lax.ppermute(held[3], 'col', up)  10.3 us
    ppermute x1, waiting for transfers between devices, local(): over = lax.ppermute(whole, 'row', across)  6.95 us
    ppermute x3, starting transfers between devices, local(): lax.ppermute(held[1], 'col', down)  4.67 us
  transfers between devices with their start and end apart: 21, of which 9 were waited for; matrix products, arithmetic and copies ran while one was open for 0% of the time, Pallas kernels for 4%

profile of v1, /device:TPU:5, one launch (start us, length us, event | category | flops | bytes accessed | tf_op | source)
XLA Modules:
  0.0 118.7 jit_solution(2329497234767431831)
XLA Ops:
  0.0 1.9 %copy-done.1 = bf16[1,8,64,3072]{3,2,1,0:T(8,128)(2,1)S(1)} copy-done((bf16[1,8,64,3072]{3,2,1,0:T(8,128)(2,1)S(1)}, bf16[1,8,64,3072]{3,2,1,0:T(8,128)(2,1)}, u32[]{:S(2)}) %copy-start.1) | copy-done | bytes 3145752
  1.9 1.0 copy-done.2
  2.9 0.7 copy-done.11
  3.6 0.7 copy-done.12
  4.3 3.0 %shard_map.46 = (bf16[3072,128]{1,0:T(8,128)(2,1)S(1)}, bf16[768,128]{1,0:T(8,128)(2,1)S(1)}, bf16[768,128]{1,0:T(8,128)(2,1)S(1)}, bf16[768,128]{1,0:T(8,128)(2,1)S(1)}, bf16[768,128]{1,0:T(8,128)(2,1)S(1)}) custom-call(s32[1]{0:T(128)} %bitcast.3.swap_ref, s32[2,64]{1,0:T(2,128)S(1)} %bitcast.8, s32[2,64]{1,0:T(2,128)S(1)} %bitcast.9, ...), custom_call_target="tpu_custom_call" | custom-call | flops 402653184 | bytes 5242880 | tf_op jit(solution)/shard_map/pallas_call | solution.py:74
  7.3 3.0 %collective-permute-start.1 = (bf16[3072,128]{1,0:T(8,128)(2,1)S(1)}, bf16[3072,128]{1,0:T(8,128)(2,1)S(1)}, u32[]{:S(2)}, u32[]{:S(2)}) collective-permute-start(bf16[3072,128]{1,0:T(8,128)(2,1)S(1)} %get-tuple-element.14.refs_0_.refs_4_), channel_id=1, source_target_pairs={{0,128},{64,192},{128,0},{192,64},{1,129},{65,193},{129,1},{193,65... | collective-permute-start | bytes 2359304 | tf_op jit(solution)/shard_map/ppermute | solution.py:253
  10.3 5.6 %collective-permute-start.3 = (bf16[768,128]{1,0:T(8,128)(2,1)S(1)}, bf16[768,128]{1,0:T(8,128)(2,1)S(1)}, u32[]{:S(2)}, u32[]{:S(2)}) collective-permute-start(bf16[768,128]{1,0:T(8,128)(2,1)S(1)} %get-tuple-element.15), channel_id=1, source_target_pairs={{0,56},{8,0},{16,8},{24,16},{32,24},{40,32},{48,40},{56,48},{1,57}... | collective-permute-start | bytes 589832 | tf_op jit(solution)/shard_map/ppermute | solution.py:243
  15.8 0.0 collective-permute-start.5
  15.8 2.7 %collective-permute-start.4 = (bf16[768,128]{1,0:T(8,128)(2,1)S(1)}, bf16[768,128]{1,0:T(8,128)(2,1)S(1)}, u32[]{:S(2)}, u32[]{:S(2)}) collective-permute-start(bf16[768,128]{1,0:T(8,128)(2,1)S(1)} %get-tuple-element.16), channel_id=1, source_target_pairs={{0,56},{8,0},{16,8},{24,16},{32,24},{40,32},{48,40},{56,48},{1,57}... | collective-permute-start | bytes 589832 | tf_op jit(solution)/shard_map/ppermute | solution.py:244
  18.5 1.8 %collective-permute-start = (bf16[3072,128]{1,0:T(8,128)(2,1)S(1)}, bf16[3072,128]{1,0:T(8,128)(2,1)S(1)}, u32[]{:S(2)}, u32[]{:S(2)}) collective-permute-start(bf16[3072,128]{1,0:T(8,128)(2,1)S(1)} %get-tuple-element.14.refs_0_.refs_4_), channel_id=1, source_target_pairs={{0,64},{64,0},{128,192},{192,128},{1,65},{65,1},{129,193},{193,129... | collective-permute-start | bytes 2359304 | tf_op jit(solution)/shard_map/ppermute | solution.py:252
  20.3 6.9 %collective-permute-done.1.refs_2_.refs_6_ = bf16[3072,128]{1,0:T(8,128)(2,1)S(1)} collective-permute-done((bf16[3072,128]{1,0:T(8,128)(2,1)S(1)}, bf16[3072,128]{1,0:T(8,128)(2,1)S(1)}, u32[]{:S(2)}, u32[]{:S(2)}) %collective-permute-start.1) | collective-permute-done | bytes 786464 | tf_op jit(solution)/shard_map/ppermute | solution.py:253
  27.3 1.5 %collective-permute-start.2 = (bf16[3072,128]{1,0:T(8,128)(2,1)S(1)}, bf16[3072,128]{1,0:T(8,128)(2,1)S(1)}, u32[]{:S(2)}, u32[]{:S(2)}) collective-permute-start(bf16[3072,128]{1,0:T(8,128)(2,1)S(1)} %collective-permute-done.1.refs_2_.refs_6_), channel_id=1, source_target_pairs={{0,64},{64,0},{128,192},{192,128},{1,65},{65,1},{129,193},{193,129... | collective-permute-start | bytes 2359304 | tf_op jit(solution)/shard_map/ppermute | solution.py:254
  28.8 1.6 %collective-permute-start.6 = (bf16[768,128]{1,0:T(8,128)(2,1)S(1)}, bf16[768,128]{1,0:T(8,128)(2,1)S(1)}, u32[]{:S(2)}, u32[]{:S(2)}) collective-permute-start(bf16[768,128]{1,0:T(8,128)(2,1)S(1)} %get-tuple-element.18), channel_id=1, source_target_pairs={{0,8},{8,16},{16,24},{24,32},{32,40},{40,48},{48,56},{56,0},{1,9},... | collective-permute-start | bytes 589832 | tf_op jit(solution)/shard_map/ppermute | solution.py:246
  30.5 4.0 %collective-permute-start.7 = (bf16[768,128]{1,0:T(8,128)(2,1)S(1)}, bf16[768,128]{1,0:T(8,128)(2,1)S(1)}, u32[]{:S(2)}, u32[]{:S(2)}) collective-permute-start(bf16[768,128]{1,0:T(8,128)(2,1)S(1)} %collective-permute-done.3.refs_4_), channel_id=1, source_target_pairs={{0,56},{8,0},{16,8},{24,16},{32,24},{40,32},{48,40},{56,48},{1,57}... | collective-permute-start | bytes 589832 | tf_op jit(solution)/shard_map/ppermute | solution.py:243
  34.5 5.2 %collective-permute-done.6.refs_7_ = bf16[768,128]{1,0:T(8,128)(2,1)S(1)} collective-permute-done((bf16[768,128]{1,0:T(8,128)(2,1)S(1)}, bf16[768,128]{1,0:T(8,128)(2,1)S(1)}, u32[]{:S(2)}, u32[]{:S(2)}) %collective-permute-start.6) | collective-permute-done | bytes 196640 | tf_op jit(solution)/shard_map/ppermute | solution.py:246
  39.7 1.3 %collective-permute-start.8 = (bf16[768,128]{1,0:T(8,128)(2,1)S(1)}, bf16[768,128]{1,0:T(8,128)(2,1)}, u32[]{:S(2)}, u32[]{:S(2)}) collective-permute-start(bf16[768,128]{1,0:T(8,128)(2,1)S(1)} %collective-permute-done.4.refs_5_), channel_id=1, source_target_pairs={{0,56},{8,0},{16,8},{24,16},{32,24},{40,32},{48,40},{56,48},{1,57}... | collective-permute-start | bytes 589832 | tf_op jit(solution)/shard_map/ppermute | solution.py:244
  40.9 0.7 copy-done.3
  41.6 0.2 collective-permute-start.10
  41.8 0.7 copy-done.5
  42.5 1.5 %collective-permute-done.9.refs_10_ = bf16[768,128]{1,0:T(8,128)(2,1)} collective-permute-done((bf16[768,128]{1,0:T(8,128)(2,1)S(1)}, bf16[768,128]{1,0:T(8,128)(2,1)}, u32[]{:S(2)}, u32[]{:S(2)}) %collective-permute-start.9) | collective-permute-done | bytes 196640 | tf_op jit(solution)/shard_map/ppermute | solution.py:245
  44.0 1.3 %collective-permute-start.11 = (bf16[768,128]{1,0:T(8,128)(2,1)S(1)}, bf16[768,128]{1,0:T(8,128)(2,1)S(1)}, u32[]{:S(2)}, u32[]{:S(2)}) collective-permute-start(bf16[768,128]{1,0:T(8,128)(2,1)S(1)} %collective-permute-done.7.refs_8_), channel_id=1, source_target_pairs={{0,56},{8,0},{16,8},{24,16},{32,24},{40,32},{48,40},{56,48},{1,57}... | collective-permute-start | bytes 589832 | tf_op jit(solution)/shard_map/ppermute | solution.py:243
  45.3 0.7 copy-done.7
  45.9 0.2 collective-permute-start.13
  46.1 1.7 %collective-permute-done.10.refs_11_ = bf16[768,128]{1,0:T(8,128)(2,1)} collective-permute-done((bf16[768,128]{1,0:T(8,128)(2,1)S(1)}, bf16[768,128]{1,0:T(8,128)(2,1)}, u32[]{:S(2)}, u32[]{:S(2)}) %collective-permute-start.10) | collective-permute-done | bytes 196640 | tf_op jit(solution)/shard_map/ppermute | solution.py:246
  47.9 0.7 collective-permute-start.12
  48.6 1.3 %collective-permute-done.11.refs_12_ = bf16[768,128]{1,0:T(8,128)(2,1)S(1)} collective-permute-done((bf16[768,128]{1,0:T(8,128)(2,1)S(1)}, bf16[768,128]{1,0:T(8,128)(2,1)S(1)}, u32[]{:S(2)}, u32[]{:S(2)}) %collective-permute-start.11) | collective-permute-done | bytes 196640 | tf_op jit(solution)/shard_map/ppermute | solution.py:243
  49.9 0.7 copy-done.9
  50.6 1.4 %collective-permute-done.13.refs_14_ = bf16[768,128]{1,0:T(8,128)(2,1)} collective-permute-done((bf16[768,128]{1,0:T(8,128)(2,1)}, bf16[768,128]{1,0:T(8,128)(2,1)}, u32[]{:S(2)}, u32[]{:S(2)}) %collective-permute-start.13) | collective-permute-done | bytes 196640 | tf_op jit(solution)/shard_map/ppermute | solution.py:245
  52.0 1.2 %collective-permute-start.15 = (bf16[768,128]{1,0:T(8,128)(2,1)}, bf16[768,128]{1,0:T(8,128)(2,1)S(1)}, u32[]{:S(2)}, u32[]{:S(2)}) collective-permute-start(bf16[768,128]{1,0:T(8,128)(2,1)} %copy-done.9), channel_id=1, source_target_pairs={{0,56},{8,0},{16,8},{24,16},{32,24},{40,32},{48,40},{56,48},{1,57}... | collective-permute-start | bytes 589832 | tf_op jit(solution)/shard_map/ppermute | solution.py:249
  53.2 0.2 collective-permute-start.16
  53.5 0.1 pad_add_fusion.pos_ref
  53.5 3.4 %collective-permute-done.14.refs_15_ = bf16[768,128]{1,0:T(8,128)(2,1)} collective-permute-done((bf16[768,128]{1,0:T(8,128)(2,1)}, bf16[768,128]{1,0:T(8,128)(2,1)}, u32[]{:S(2)}, u32[]{:S(2)}) %collective-permute-start.14) | collective-permute-done | bytes 196640 | tf_op jit(solution)/shard_map/ppermute | solution.py:246
  56.9 0.9 copy-done.4
  57.9 0.9 copy-done.6
  58.8 0.9 copy-done.8
  59.7 0.9 copy-done.10
  60.7 4.3 %shard_map.47.old_ref = bf16[8,128,512]{2,1,0:T(8,128)(2,1)} custom-call(s32[3]{0:T(128)S(1)} %pad_add_fusion.pos_ref, bf16[3072,128]{1,0:T(8,128)(2,1)S(1)} %get-tuple-element.14.refs_0_.refs_4_, bf16[3072,128]{1,0:T(8,128)(2,1)S(1)} %collective-permute-done.refs_1_.refs_5_, bf16[3072,128]{1,0:T(8,128)(2,1)S(1)} %collective-permute-done.1.refs_2_.refs_6_, ...), custom_call_target="tpu_custom_call" | custom-call | flops 1610612736 | bytes 7340032 | tf_op jit(solution)/shard_map/pallas_call | solution.py:138
  65.0 1.2 %copy-done = bf16[8,128,512]{2,1,0:T(8,128)(2,1)S(1)} copy-done((bf16[8,128,512]{2,1,0:T(8,128)(2,1)S(1)}, bf16[8,128,512]{2,1,0:T(8,128)(2,1)}, u32[]{:S(2)}) %copy-start) | copy-done | bytes 1048600
  66.2 1.0 shard_map.48
  67.2 14.1 %all_to_all.5.in_ref = bf16[8,128,512]{2,1,0:T(8,128)(2,1)S(1)} all-to-all(bf16[8,128,512]{2,1,0:T(8,128)(2,1)S(1)} %shard_map.48), channel_id=1, replica_groups=mesh['row'=4,'col'=8,'aux'=8] {'aux'}, dimensions={0} | all-to-all | bytes 2097152 | tf_op jit(solution)/shard_map/all_to_all | solution.py:259
  81.3 0.1 shard_map.49
  81.4 5.9 %collective-permute-start.17 = (f32[128,128]{1,0:T(8,128)S(1)}, f32[128,128]{1,0:T(8,128)S(1)}, u32[]{:S(2)}, u32[]{:S(2)}) collective-permute-start(f32[128,128]{1,0:T(8,128)S(1)} %get-tuple-element.19.refs_0_), channel_id=1, source_target_pairs={{0,0},{1,8},{2,16},{3,24},{4,32},{5,40},{6,48},{7,56},{8,1},{9,9},... | collective-permute-start | bytes 196616 | tf_op jit(solution)/shard_map/ppermute | solution.py:270
  87.3 9.5 %collective-permute-start.18 = (f32[128,128]{1,0:T(8,128)S(1)}, f32[128,128]{1,0:T(8,128)S(1)}, u32[]{:S(2)}, u32[]{:S(2)}) collective-permute-start(f32[128,128]{1,0:T(8,128)S(1)} %get-tuple-element.20.refs_1_), channel_id=1, source_target_pairs={{0,64},{1,72},{2,80},{3,88},{4,96},{5,104},{6,112},{7,120},{8,65},... | collective-permute-start | bytes 196616 | tf_op jit(solution)/shard_map/ppermute | solution.py:270
  96.8 7.9 %collective-permute-start.19 = (f32[128,128]{1,0:T(8,128)S(1)}, f32[128,128]{1,0:T(8,128)S(1)}, u32[]{:S(2)}, u32[]{:S(2)}) collective-permute-start(f32[128,128]{1,0:T(8,128)S(1)} %get-tuple-element.21.refs_2_), channel_id=1, source_target_pairs={{0,128},{1,136},{2,144},{3,152},{4,160},{5,168},{6,176},{7,184},{8... | collective-permute-start | bytes 196616 | tf_op jit(solution)/shard_map/ppermute | solution.py:270
  104.8 0.5 collective-permute-start.20
  105.2 6.7 %collective-permute-done.19.refs_6_ = f32[128,128]{1,0:T(8,128)S(1)} collective-permute-done((f32[128,128]{1,0:T(8,128)S(1)}, f32[128,128]{1,0:T(8,128)S(1)}, u32[]{:S(2)}, u32[]{:S(2)}) %collective-permute-start.19) | collective-permute-done | bytes 65568 | tf_op jit(solution)/shard_map/ppermute | solution.py:270
  112.0 5.2 %collective-permute-done.20.refs_7_ = f32[128,128]{1,0:T(8,128)S(1)} collective-permute-done((f32[128,128]{1,0:T(8,128)S(1)}, f32[128,128]{1,0:T(8,128)S(1)}, u32[]{:S(2)}, u32[]{:S(2)}) %collective-permute-start.20) | collective-permute-done | bytes 65568 | tf_op jit(solution)/shard_map/ppermute | solution.py:270
  117.2 1.5 %shard_map.50 = f32[128,4,128]{2,1,0:T(4,128)} custom-call(s32[3]{0:T(128)S(1)} %pad_add_fusion.pos_ref, f32[128,128]{1,0:T(8,128)S(1)} %get-tuple-element.19.refs_0_, f32[128,128]{1,0:T(8,128)S(1)} %get-tuple-element.20.refs_1_, f32[128,128]{1,0:T(8,128)S(1)} %get-tuple-element.21.refs_2_, f32[128,128]{1,0:T(8,128)S(1)} %get-tuple-element.22.refs_3_, ...), custom_call_target="tpu_custom_call" | custom-call | tf_op jit(solution)/shard_map/pallas_call | solution.py:218
  (27 shorter events, 0.1 us)
Async XLA Ops:
  0.0 1.9 %copy-start.1 = (bf16[1,8,64,3072]{3,2,1,0:T(8,128)(2,1)S(1)}, bf16[1,8,64,3072]{3,2,1,0:T(8,128)(2,1)}, u32[]{:S(2)}) copy-start(bf16[1,8,64,3072]{3,2,1,0:T(8,128)(2,1)} %param.4) | copy-start | bytes 9437188
  1.9 1.0 copy-start.2
  2.9 0.7 copy-start.11
  3.6 0.7 copy-start.12
  7.3 20.0 %collective-permute-start.1 = (bf16[3072,128]{1,0:T(8,128)(2,1)S(1)}, bf16[3072,128]{1,0:T(8,128)(2,1)S(1)}, u32[]{:S(2)}, u32[]{:S(2)}) collective-permute-start(bf16[3072,128]{1,0:T(8,128)(2,1)S(1)} %get-tuple-element.14.refs_0_.refs_4_), channel_id=1, source_target_pairs={{0,128},{64,192},{128,0},{192,64},{1,129},{65,193},{129,1},{193,65... | collective-permute-start | bytes 2359304 | tf_op jit(solution)/shard_map/ppermute | solution.py:253
  10.3 18.5 %collective-permute-start.3 = (bf16[768,128]{1,0:T(8,128)(2,1)S(1)}, bf16[768,128]{1,0:T(8,128)(2,1)S(1)}, u32[]{:S(2)}, u32[]{:S(2)}) collective-permute-start(bf16[768,128]{1,0:T(8,128)(2,1)S(1)} %get-tuple-element.15), channel_id=1, source_target_pairs={{0,56},{8,0},{16,8},{24,16},{32,24},{40,32},{48,40},{56,48},{1,57}... | collective-permute-start | bytes 589832 | tf_op jit(solution)/shard_map/ppermute | solution.py:243
  15.8 14.6 %collective-permute-start.5 = (bf16[768,128]{1,0:T(8,128)(2,1)S(1)}, bf16[768,128]{1,0:T(8,128)(2,1)S(1)}, u32[]{:S(2)}, u32[]{:S(2)}) collective-permute-start(bf16[768,128]{1,0:T(8,128)(2,1)S(1)} %get-tuple-element.17), channel_id=1, source_target_pairs={{0,8},{8,16},{16,24},{24,32},{32,40},{40,48},{48,56},{56,0},{1,9},... | collective-permute-start | bytes 589832 | tf_op jit(solution)/shard_map/ppermute | solution.py:245
  15.8 18.6 %collective-permute-start.4 = (bf16[768,128]{1,0:T(8,128)(2,1)S(1)}, bf16[768,128]{1,0:T(8,128)(2,1)S(1)}, u32[]{:S(2)}, u32[]{:S(2)}) collective-permute-start(bf16[768,128]{1,0:T(8,128)(2,1)S(1)} %get-tuple-element.16), channel_id=1, source_target_pairs={{0,56},{8,0},{16,8},{24,16},{32,24},{40,32},{48,40},{56,48},{1,57}... | collective-permute-start | bytes 589832 | tf_op jit(solution)/shard_map/ppermute | solution.py:244
  18.5 38.4 %collective-permute-start = (bf16[3072,128]{1,0:T(8,128)(2,1)S(1)}, bf16[3072,128]{1,0:T(8,128)(2,1)S(1)}, u32[]{:S(2)}, u32[]{:S(2)}) collective-permute-start(bf16[3072,128]{1,0:T(8,128)(2,1)S(1)} %get-tuple-element.14.refs_0_.refs_4_), channel_id=1, source_target_pairs={{0,64},{64,0},{128,192},{192,128},{1,65},{65,1},{129,193},{193,129... | collective-permute-start | bytes 2359304 | tf_op jit(solution)/shard_map/ppermute | solution.py:252
  27.3 29.7 %collective-permute-start.2 = (bf16[3072,128]{1,0:T(8,128)(2,1)S(1)}, bf16[3072,128]{1,0:T(8,128)(2,1)S(1)}, u32[]{:S(2)}, u32[]{:S(2)}) collective-permute-start(bf16[3072,128]{1,0:T(8,128)(2,1)S(1)} %collective-permute-done.1.refs_2_.refs_6_), channel_id=1, source_target_pairs={{0,64},{64,0},{128,192},{192,128},{1,65},{65,1},{129,193},{193,129... | collective-permute-start | bytes 2359304 | tf_op jit(solution)/shard_map/ppermute | solution.py:254
  28.8 10.9 %collective-permute-start.6 = (bf16[768,128]{1,0:T(8,128)(2,1)S(1)}, bf16[768,128]{1,0:T(8,128)(2,1)S(1)}, u32[]{:S(2)}, u32[]{:S(2)}) collective-permute-start(bf16[768,128]{1,0:T(8,128)(2,1)S(1)} %get-tuple-element.18), channel_id=1, source_target_pairs={{0,8},{8,16},{16,24},{24,32},{32,40},{40,48},{48,56},{56,0},{1,9},... | collective-permute-start | bytes 589832 | tf_op jit(solution)/shard_map/ppermute | solution.py:246
  30.5 11.2 %collective-permute-start.7 = (bf16[768,128]{1,0:T(8,128)(2,1)S(1)}, bf16[768,128]{1,0:T(8,128)(2,1)S(1)}, u32[]{:S(2)}, u32[]{:S(2)}) collective-permute-start(bf16[768,128]{1,0:T(8,128)(2,1)S(1)} %collective-permute-done.3.refs_4_), channel_id=1, source_target_pairs={{0,56},{8,0},{16,8},{24,16},{32,24},{40,32},{48,40},{56,48},{1,57}... | collective-permute-start | bytes 589832 | tf_op jit(solution)/shard_map/ppermute | solution.py:243
  34.5 9.5 %collective-permute-start.9 = (bf16[768,128]{1,0:T(8,128)(2,1)S(1)}, bf16[768,128]{1,0:T(8,128)(2,1)}, u32[]{:S(2)}, u32[]{:S(2)}) collective-permute-start(bf16[768,128]{1,0:T(8,128)(2,1)S(1)} %collective-permute-done.5.refs_6_), channel_id=1, source_target_pairs={{0,8},{8,16},{16,24},{24,32},{32,40},{40,48},{48,56},{56,0},{1,9},... | collective-permute-start | bytes 589832 | tf_op jit(solution)/shard_map/ppermute | solution.py:245
  39.7 6.3 %collective-permute-start.8 = (bf16[768,128]{1,0:T(8,128)(2,1)S(1)}, bf16[768,128]{1,0:T(8,128)(2,1)}, u32[]{:S(2)}, u32[]{:S(2)}) collective-permute-start(bf16[768,128]{1,0:T(8,128)(2,1)S(1)} %collective-permute-done.4.refs_5_), channel_id=1, source_target_pairs={{0,56},{8,0},{16,8},{24,16},{32,24},{40,32},{48,40},{56,48},{1,57}... | collective-permute-start | bytes 589832 | tf_op jit(solution)/shard_map/ppermute | solution.py:244
  40.9 0.7 copy-start.3
  41.6 6.3 %collective-permute-start.10 = (bf16[768,128]{1,0:T(8,128)(2,1)S(1)}, bf16[768,128]{1,0:T(8,128)(2,1)}, u32[]{:S(2)}, u32[]{:S(2)}) collective-permute-start(bf16[768,128]{1,0:T(8,128)(2,1)S(1)} %collective-permute-done.6.refs_7_), channel_id=1, source_target_pairs={{0,8},{8,16},{16,24},{24,32},{32,40},{40,48},{48,56},{56,0},{1,9},... | collective-permute-start | bytes 589832 | tf_op jit(solution)/shard_map/ppermute | solution.py:246
  41.8 0.7 copy-start.5
  44.0 5.9 %collective-permute-start.11 = (bf16[768,128]{1,0:T(8,128)(2,1)S(1)}, bf16[768,128]{1,0:T(8,128)(2,1)S(1)}, u32[]{:S(2)}, u32[]{:S(2)}) collective-permute-start(bf16[768,128]{1,0:T(8,128)(2,1)S(1)} %collective-permute-done.7.refs_8_), channel_id=1, source_target_pairs={{0,56},{8,0},{16,8},{24,16},{32,24},{40,32},{48,40},{56,48},{1,57}... | collective-permute-start | bytes 589832 | tf_op jit(solution)/shard_map/ppermute | solution.py:243
  45.3 0.7 copy-start.7
  45.9 6.0 %collective-permute-start.13 = (bf16[768,128]{1,0:T(8,128)(2,1)}, bf16[768,128]{1,0:T(8,128)(2,1)}, u32[]{:S(2)}, u32[]{:S(2)}) collective-permute-start(bf16[768,128]{1,0:T(8,128)(2,1)} %collective-permute-done.9.refs_10_), channel_id=1, source_target_pairs={{0,8},{8,16},{16,24},{24,32},{32,40},{40,48},{48,56},{56,0},{1,9},... | collective-permute-start | bytes 589832 | tf_op jit(solution)/shard_map/ppermute | solution.py:245
  47.9 5.4 %collective-permute-start.12 = (bf16[768,128]{1,0:T(8,128)(2,1)}, bf16[768,128]{1,0:T(8,128)(2,1)}, u32[]{:S(2)}, u32[]{:S(2)}) collective-permute-start(bf16[768,128]{1,0:T(8,128)(2,1)} %collective-permute-done.8.refs_9_), channel_id=1, source_target_pairs={{0,56},{8,0},{16,8},{24,16},{32,24},{40,32},{48,40},{56,48},{1,57}... | collective-permute-start | bytes 589832 | tf_op jit(solution)/shard_map/ppermute | solution.py:244
  49.9 0.7 copy-start.9
  50.6 6.4 %collective-permute-start.14 = (bf16[768,128]{1,0:T(8,128)(2,1)}, bf16[768,128]{1,0:T(8,128)(2,1)}, u32[]{:S(2)}, u32[]{:S(2)}) collective-permute-start(bf16[768,128]{1,0:T(8,128)(2,1)} %collective-permute-done.10.refs_11_), channel_id=1, source_target_pairs={{0,8},{8,16},{16,24},{24,32},{32,40},{40,48},{48,56},{56,0},{1,9},... | collective-permute-start | bytes 589832 | tf_op jit(solution)/shard_map/ppermute | solution.py:246
  52.0 13.0 %collective-permute-start.15 = (bf16[768,128]{1,0:T(8,128)(2,1)}, bf16[768,128]{1,0:T(8,128)(2,1)S(1)}, u32[]{:S(2)}, u32[]{:S(2)}) collective-permute-start(bf16[768,128]{1,0:T(8,128)(2,1)} %copy-done.9), channel_id=1, source_target_pairs={{0,56},{8,0},{16,8},{24,16},{32,24},{40,32},{48,40},{56,48},{1,57}... | collective-permute-start | bytes 589832 | tf_op jit(solution)/shard_map/ppermute | solution.py:249
  53.2 11.8 %collective-permute-start.16 = (bf16[768,128]{1,0:T(8,128)(2,1)}, bf16[768,128]{1,0:T(8,128)(2,1)S(1)}, u32[]{:S(2)}, u32[]{:S(2)}) collective-permute-start(bf16[768,128]{1,0:T(8,128)(2,1)} %collective-permute-done.13.refs_14_), channel_id=1, source_target_pairs={{0,8},{8,16},{16,24},{24,32},{32,40},{40,48},{48,56},{56,0},{1,9},... | collective-permute-start | bytes 589832 | tf_op jit(solution)/shard_map/ppermute | solution.py:250
  56.9 0.9 copy-start.4
  57.9 0.9 copy-start.6
  58.8 0.9 copy-start.8
  59.7 0.9 copy-start.10
  65.0 1.2 %copy-start = (bf16[8,128,512]{2,1,0:T(8,128)(2,1)S(1)}, bf16[8,128,512]{2,1,0:T(8,128)(2,1)}, u32[]{:S(2)}) copy-start(bf16[8,128,512]{2,1,0:T(8,128)(2,1)} %shard_map.47.old_ref) | copy-start | bytes 3145732
  81.4 23.8 %collective-permute-start.17 = (f32[128,128]{1,0:T(8,128)S(1)}, f32[128,128]{1,0:T(8,128)S(1)}, u32[]{:S(2)}, u32[]{:S(2)}) collective-permute-start(f32[128,128]{1,0:T(8,128)S(1)} %get-tuple-element.19.refs_0_), channel_id=1, source_target_pairs={{0,0},{1,8},{2,16},{3,24},{4,32},{5,40},{6,48},{7,56},{8,1},{9,9},... | collective-permute-start | bytes 196616 | tf_op jit(solution)/shard_map/ppermute | solution.py:270
  87.3 17.9 %collective-permute-start.18 = (f32[128,128]{1,0:T(8,128)S(1)}, f32[128,128]{1,0:T(8,128)S(1)}, u32[]{:S(2)}, u32[]{:S(2)}) collective-permute-start(f32[128,128]{1,0:T(8,128)S(1)} %get-tuple-element.20.refs_1_), channel_id=1, source_target_pairs={{0,64},{1,72},{2,80},{3,88},{4,96},{5,104},{6,112},{7,120},{8,65},... | collective-permute-start | bytes 196616 | tf_op jit(solution)/shard_map/ppermute | solution.py:270
  96.8 15.1 %collective-permute-start.19 = (f32[128,128]{1,0:T(8,128)S(1)}, f32[128,128]{1,0:T(8,128)S(1)}, u32[]{:S(2)}, u32[]{:S(2)}) collective-permute-start(f32[128,128]{1,0:T(8,128)S(1)} %get-tuple-element.21.refs_2_), channel_id=1, source_target_pairs={{0,128},{1,136},{2,144},{3,152},{4,160},{5,168},{6,176},{7,184},{8... | collective-permute-start | bytes 196616 | tf_op jit(solution)/shard_map/ppermute | solution.py:270
  104.8 12.4 %collective-permute-start.20 = (f32[128,128]{1,0:T(8,128)S(1)}, f32[128,128]{1,0:T(8,128)S(1)}, u32[]{:S(2)}, u32[]{:S(2)}) collective-permute-start(f32[128,128]{1,0:T(8,128)S(1)} %get-tuple-element.22.refs_3_), channel_id=1, source_target_pairs={{0,192},{1,200},{2,208},{3,216},{4,224},{5,232},{6,240},{7,248},{8... | collective-permute-start | bytes 196616 | tf_op jit(solution)/shard_map/ppermute | solution.py:270

commit v2 on v0

v2 whole, which is shorter than its diff:
```python
import functools

import jax
import jax.numpy as jnp
from jax import lax
from jax.experimental import pallas as pl
from jax.experimental.pallas import tpu as pltpu
from jax.sharding import PartitionSpec as P

WIDE_LIMIT = 60 * 1024 * 1024
VMEM_LIMIT = 16 * 1024 * 1024
CHUNKS = 4


def half_kernel(mask_ref, slot_ref, orb_ref, int_ref, whole_ref, lower_ref, upper_ref,
                place_ref, weight_ref, orb_buf, int_buf, out_buf, int_sem, orb_sem, out_sem, part_sem):
    chunks, capacity, block, lanes = int_buf.shape
    rows = out_buf.shape[1]
    occ = orb_buf.shape[0]
    row_blocks, block_count = mask_ref.shape
    low = lax.broadcasted_iota(jnp.int32, (occ, 2 * block), 1) < block

    def load(c):
        return pltpu.make_async_copy(int_ref.at[:, :, pl.ds(c * lanes, lanes)], int_buf.at[c], int_sem.at[c])

    orb_load = pltpu.make_async_copy(orb_ref, orb_buf, orb_sem)
    orb_load.start()
    for c in range(chunks):
        load(c).start()

    for s in range(capacity):
        place_ref[s] = -1
    for b in range(row_blocks):
        for l in range(block_count):
            slot = slot_ref[b, l]
            valid = (mask_ref[b, l] == 1) & (slot >= 0) & (slot < capacity)
            place_ref[jnp.where(valid, slot, capacity)] = b * block_count + l

    orb_load.wait()
    for pair in range(capacity // 2):
        parts = []
        for s in (2 * pair, 2 * pair + 1):
            place = place_ref[s]
            at = jnp.maximum(place, 0)
            home = at // block_count
            parity = lax.rem(at, 2)
            start = pl.multiple_of((lax.rem(at, block_count) // 2) * (2 * block), 2 * block)
            columns = orb_buf[:, pl.ds(start, 2 * block)].astype(jnp.float32)
            turned = pltpu.roll(columns, block, 1)
            value = jnp.where(parity == (s % 2), columns, turned)
            parts.append((place, home, value))
        for b in range(row_blocks):
            chosen = [jnp.where((place >= 0) & (home == b), value, 0.0) for place, home, value in parts]
            weight_ref[b * occ : (b + 1) * occ, pair * 2 * block : (pair + 1) * 2 * block] = jnp.where(
                low, chosen[0], chosen[1]
            ).astype(weight_ref.dtype)

    def store(c):
        return pltpu.make_async_copy(out_buf.at[c], whole_ref.at[pl.ds(c * rows, rows)], out_sem.at[c])

    def store_part(c):
        target = (lower_ref, upper_ref)[c // 2]
        return pltpu.make_async_copy(out_buf.at[c], target.at[pl.ds((c % 2) * rows, rows)], part_sem.at[c])

    for c in range(chunks):
        load(c).wait()
        packed = int_buf[c].reshape(capacity * block, lanes)
        product = jnp.dot(weight_ref[...], packed, preferred_element_type=jnp.float32)
        for pair in range(lanes // (2 * block)):
            first = product[:occ, pair * 2 * block : (pair + 1) * 2 * block]
            second = product[occ:, pair * 2 * block : (pair + 1) * 2 * block]
            out_buf[c, 2 * pair * occ : (2 * pair + 1) * occ, :] = jnp.where(
                low, first, pltpu.roll(second, block, 1)
            ).astype(out_buf.dtype)
            out_buf[c, (2 * pair + 1) * occ : (2 * pair + 2) * occ, :] = jnp.where(
                low, pltpu.roll(first, block, 1), second
            ).astype(out_buf.dtype)
        store_part(c).start()
        store(c).start()
    for c in range(chunks):
        store_part(c).wait()
        store(c).wait()


def half_transform(mask, slots, packed, orbitals):
    capacity, block, width = packed.shape
    occ = orbitals.shape[0]
    lanes = width // CHUNKS
    rows = lanes // block * occ
    smem = pl.BlockSpec(memory_space=pltpu.SMEM)
    anywhere = pl.BlockSpec(memory_space=pl.ANY)
    return pl.pallas_call(
        half_kernel,
        out_shape=(jax.ShapeDtypeStruct((rows * CHUNKS, 2 * block), jnp.bfloat16),)
        + (jax.ShapeDtypeStruct((rows * CHUNKS // 2, 2 * block), jnp.bfloat16),) * 2,
        in_specs=[smem, smem, anywhere, anywhere],
        out_specs=(anywhere,) * 3,
        scratch_shapes=[
            pltpu.SMEM((capacity + 1,), jnp.int32),
            pltpu.VMEM((2 * occ, capacity * block), jnp.bfloat16),
            pltpu.VMEM(orbitals.shape, jnp.bfloat16),
            pltpu.VMEM((CHUNKS, capacity, block, lanes), jnp.bfloat16),
            pltpu.VMEM((CHUNKS, rows, 2 * block), jnp.bfloat16),
            pltpu.SemaphoreType.DMA((CHUNKS,)),
            pltpu.SemaphoreType.DMA,
            pltpu.SemaphoreType.DMA((CHUNKS,)),
            pltpu.SemaphoreType.DMA((CHUNKS,)),
        ],
        compiler_params=pltpu.CompilerParams(vmem_limit_bytes=WIDE_LIMIT),
        cost_estimate=pl.CostEstimate(flops=2 * 2 * occ * capacity * block * width, bytes_accessed=5 << 20, transcendentals=0),
    )(mask, slots, orbitals, packed)


CONTRACT = (((0,), (0,)), ((), ()))


def tile_of(parts, col_refs):
    total, start = None, 0
    for ref in parts:
        rows = ref.shape[0]
        columns = jnp.concatenate([c[start : start + rows, :] for c in col_refs], axis=1)
        term = lax.dot_general(ref[...], columns, CONTRACT, preferred_element_type=jnp.float32)
        total = term if total is None else total + term
        start += rows
    return total


def early_kernel(count, *refs):
    col_refs, moved = refs[:4], refs[4 : 4 + 2 * count]
    out_ref, held, sems = refs[4 + 2 * count :]
    copies = [pltpu.make_async_copy(ref, held.at[n], sems.at[n]) for n, ref in enumerate(moved)]
    for copy in copies:
        copy.start()
    for n in range(count):
        copies[2 * n].wait()
        copies[2 * n + 1].wait()
        out_ref[n] = tile_of([held.at[2 * n], held.at[2 * n + 1]], col_refs).astype(out_ref.dtype)


def early_tiles(col_panels, moved):
    depth, width = col_panels[0].shape
    count = len(moved) // 2
    vmem = pl.BlockSpec(memory_space=pltpu.VMEM)
    return pl.pallas_call(
        functools.partial(early_kernel, count),
        out_shape=jax.ShapeDtypeStruct((count, width, 4 * width), jnp.bfloat16),
        in_specs=[vmem] * 4 + [pl.BlockSpec(memory_space=pltpu.HBM)] * (2 * count),
        out_specs=vmem,
        scratch_shapes=[
            pltpu.VMEM((2 * count,) + moved[0].shape, jnp.bfloat16),
            pltpu.SemaphoreType.DMA((2 * count,)),
        ],
        compiler_params=pltpu.CompilerParams(vmem_limit_bytes=VMEM_LIMIT),
        cost_estimate=pl.CostEstimate(flops=2 * width * 4 * width * depth * count, bytes_accessed=7 << 20, transcendentals=0),
    )(*col_panels, *moved)


def last_kernel(ring, pos_ref, *refs):
    done_refs, col_refs, parts, out_ref = refs[:3], refs[3:7], refs[7:9], refs[9]
    col = pos_ref[0]

    def origin(d):
        return lax.rem(col + d, ring)

    for ref, distances in zip(done_refs, ((0, 1, ring - 1), (2, ring - 2), (3, ring - 3))):
        for n, d in enumerate(distances):
            out_ref[origin(d)] = ref[n]
    out_ref[origin(4)] = tile_of(parts, col_refs).astype(out_ref.dtype)


def last_tile(pos, done, col_panels, parts, ring):
    depth, width = col_panels[0].shape
    return pl.pallas_call(
        functools.partial(last_kernel, ring),
        out_shape=jax.ShapeDtypeStruct((ring, width, 4 * width), jnp.bfloat16),
        in_specs=[pl.BlockSpec(memory_space=pltpu.SMEM)] + [pl.BlockSpec(memory_space=pltpu.VMEM)] * 9,
        out_specs=pl.BlockSpec(memory_space=pltpu.VMEM),
        compiler_params=pltpu.CompilerParams(vmem_limit_bytes=VMEM_LIMIT),
        cost_estimate=pl.CostEstimate(flops=2 * width * 4 * width * depth, bytes_accessed=6 << 20, transcendentals=0),
    )(pos, *done, *col_panels, *parts)


def sum_kernel(pos_ref, in_ref, out_ref):
    width = out_ref.shape[2]
    for rho in range(out_ref.shape[1]):
        total = None
        for a in range(in_ref.shape[0]):
            term = in_ref[a, :, rho * width : (rho + 1) * width].astype(jnp.float32)
            total = term if total is None else total + term
        out_ref[:, pos_ref[1] ^ rho, :] = total


def sum_parts(pos, received):
    count, width, wide = received.shape
    return pl.pallas_call(
        sum_kernel,
        out_shape=jax.ShapeDtypeStruct((width, wide // width, width), jnp.float32),
        in_specs=[pl.BlockSpec(memory_space=pltpu.SMEM), pl.BlockSpec(memory_space=pltpu.VMEM)],
        out_specs=pl.BlockSpec(memory_space=pltpu.VMEM),
        compiler_params=pltpu.CompilerParams(vmem_limit_bytes=VMEM_LIMIT),
        cost_estimate=pl.CostEstimate(flops=count * width * wide, bytes_accessed=2 * count * width * wide, transcendentals=0),
    )(pos, received)


def local(integrals, block_mask, block_slots, orbitals):
    row, col = lax.axis_index("row"), lax.axis_index("col")
    ring, rows_n = lax.axis_size("col"), lax.axis_size("row")
    pos = jnp.stack([col, row]).astype(jnp.int32)
    whole, lower, upper = half_transform(block_mask[0], block_slots[0], integrals[0], orbitals)

    down = [(i, (i - 1) % ring) for i in range(ring)]
    up = [(i, (i + 1) % ring) for i in range(ring)]

    def hop(held):
        return [
            lax.ppermute(held[0], "col", down),
            lax.ppermute(held[1], "col", down),
            lax.ppermute(held[2], "col", up),
            lax.ppermute(held[3], "col", up),
        ]

    beside = lax.ppermute(whole, "row", [(i, i ^ 1) for i in range(rows_n)])
    over = lax.ppermute(whole, "row", [(i, i ^ 2) for i in range(rows_n)])
    first = hop([lower, upper, lower, upper])
    over, first[1] = lax.optimization_barrier((over, first[1]))
    second = hop(first)
    diagonal = lax.ppermute(over, "row", [(i, i ^ 1) for i in range(rows_n)])
    col_panels = [whole, beside, over, diagonal]
    near = early_tiles(col_panels, [lower, upper] + first)
    near, second[2] = lax.optimization_barrier((near, second[2]))
    third = hop(second)
    middle = early_tiles(col_panels, second)
    middle, third[0] = lax.optimization_barrier((middle, third[0]))
    parts = [lax.ppermute(third[0], "col", down), lax.ppermute(third[3], "col", up)]
    outer = early_tiles(col_panels, third)
    sums = last_tile(pos, [near, middle, outer], col_panels, parts, ring)
    received = lax.all_to_all(sums, "aux", 0, 0, tiled=True)
    return sum_parts(pos, received)


def solution(mesh):
    placed = (
        P("aux", ("row", "col"), None, None),
        P("aux", ("row", "col"), None),
        P("aux", ("row", "col"), None),
        P(),
    )
    return jax.shard_map(
        local, mesh=mesh, in_specs=placed, out_specs=P(("row", "aux"), None, "col"), check_vma=False
    )
```

time: 345 us -> 99.6 us (0.29)
  waiting for transfers between devices: 254 us -> 33.4 us
  local copies, waits for them, and re-layouts: 43 us -> 3.82 us
  matrix products: 33.2 us -> 0 us
  starting transfers between devices: 0.04 us -> 26.3 us
  blocking collectives: 0 us -> 19.3 us
  Pallas kernels: 0 us -> 16.3 us
  between operations: 13.5 us -> 0.13 us
    all_gather x1 -> x0, waiting for transfers between devices: 200 us -> none  [local(): gathered = lax.all_gather(half_local, ('row', 'col'), axis=2, tiled=True)]
    reduce_scatter x1 -> x0, waiting for transfers between devices: 53.1 us -> none  [local(): lax.psum_scatter(exchange_tile, 'aux', scatter_dimension=0, tiled=True)]
    ppermute x0 -> x17, waiting for transfers between devices: none -> 33.4 us  [the longest x3 11.8 us: hop(): lax.ppermute(held[1], 'col', down)]
    dot_general x3 -> x0, matrix products: 33.2 us -> none  [the longest x1 21.8 us: half_transform(): jnp.einsum('sb,siqm->iqbm', weights, products, precision=lax.Precision.HI...]
    ppermute x0 -> x17, starting transfers between devices: none -> 26.3 us  [the longest x3 10.7 us: hop(): lax.ppermute(held[0], 'col', down)]
    all_to_all x0 -> x1, blocking collectives: none -> 19.3 us  [local(): received = lax.all_to_all(sums, 'aux', 0, 0, tiled=True)]
    pallas_call x0 -> x6, Pallas kernels: none -> 16.3 us  [the longest x3 7.83 us: early_tiles(): pl.pallas_call(functools.partial(early_kernel, count), out_shape=jax.Shap...]
    reshape x3 -> x0, local copies, waits for them, and re-layouts: 15.7 us -> none  [the longest x1 9.96 us: half_transform(): products = products.reshape(capacity, occ_count, aux_count, block_size)]
  transfers between devices with their start and end apart: 2 -> 17, of which waited for: 2 -> 10; matrix products, arithmetic and copies ran while one was open for 0% -> 0% of each run, Pallas kernels for 0% -> 8%
where the time goes in v2:
time: 99.6 us; the launch traced here: 99.3 us
  waiting for transfers between devices  33.4 us (34%)
  starting transfers between devices  26.3 us (26%)
  blocking collectives  19.3 us (19%)
  Pallas kernels  16.3 us (16%)
  local copies, waits for them, and re-layouts  3.82 us (4%)
    all_to_all x1, blocking collectives, local(): received = lax.all_to_all(sums, 'aux', 0, 0, tiled=True)  19.3 us
    ppermute x3, waiting for transfers between devices, hop(): lax.ppermute(held[1], 'col', down)  11.8 us
    ppermute x3, starting transfers between devices, hop(): lax.ppermute(held[0], 'col', down)  10.7 us
    ppermute x3, waiting for transfers between devices, hop(): lax.ppermute(held[2], 'col', up)  10.4 us
    ppermute x3, starting transfers between devices, hop(): lax.ppermute(held[1], 'col', down)  9.94 us
    pallas_call x3, Pallas kernels, early_tiles(): pl.pallas_call(functools.partial(early_kernel, count), out_shape=jax.Shap...  7.83 us
    pallas_call x1, Pallas kernels, half_transform(): pl.pallas_call(half_kernel, out_shape=(jax.ShapeDtypeStruct((rows * CHUNK...  5.21 us
    ppermute x3, waiting for transfers between devices, hop(): lax.ppermute(held[3], 'col', up)  4.79 us
  transfers between devices with their start and end apart: 17, of which 10 were waited for; matrix products, arithmetic and copies ran while one was open for 0% of the time, Pallas kernels for 8%

profile of v2, /device:TPU:16, one launch (start us, length us, event | category | flops | bytes accessed | tf_op | source)
XLA Modules:
  0.0 99.3 jit_solution(9656334959391712418)
XLA Ops:
  0.0 5.2 %shard_map.46 = (bf16[3072,128]{1,0:T(8,128)(2,1)}, bf16[1536,128]{1,0:T(8,128)(2,1)}, bf16[1536,128]{1,0:T(8,128)(2,1)}) custom-call(s32[2,64]{1,0:T(2,128)} %bitcast.6, s32[2,64]{1,0:T(2,128)} %bitcast.7, bf16[64,4096]{1,0:T(8,128)(2,1)} %orb_ref.1, bf16[8,64,3072]{2,1,0:T(8,128)(2,1)} %bitcast.5), custom_call_target="tpu_custom_call" | custom-call | flops 402653184 | bytes 5242880 | tf_op jit(solution)/shard_map/pallas_call | solution.py:92
  5.2 2.2 %collective-permute-start.1 = (bf16[3072,128]{1,0:T(8,128)(2,1)}, bf16[3072,128]{1,0:T(8,128)(2,1)S(1)}, u32[]{:S(2)}, u32[]{:S(2)}) collective-permute-start(bf16[3072,128]{1,0:T(8,128)(2,1)} %get-tuple-element.14.refs_0_.refs_3_), channel_id=1, source_target_pairs={{0,128},{64,192},{128,0},{192,64},{1,129},{65,193},{129,1},{193,65... | collective-permute-start | bytes 2359304 | tf_op jit(solution)/shard_map/ppermute | solution.py:223
  7.4 4.1 %collective-permute-start.2 = (bf16[1536,128]{1,0:T(8,128)(2,1)}, bf16[1536,128]{1,0:T(8,128)(2,1)S(1)}, u32[]{:S(2)}, u32[]{:S(2)}) collective-permute-start(bf16[1536,128]{1,0:T(8,128)(2,1)} %get-tuple-element.15.refs_5_), channel_id=1, source_target_pairs={{0,56},{8,0},{16,8},{24,16},{32,24},{40,32},{48,40},{56,48},{1,57}... | collective-permute-start | bytes 1179656 | tf_op jit(solution)/shard_map/ppermute | solution.py:217
  11.5 0.0 collective-permute-start.6
  11.5 0.0 collective-permute-start
  11.5 3.2 %collective-permute-start.4 = (bf16[1536,128]{1,0:T(8,128)(2,1)}, bf16[1536,128]{1,0:T(8,128)(2,1)S(1)}, u32[]{:S(2)}, u32[]{:S(2)}) collective-permute-start(bf16[1536,128]{1,0:T(8,128)(2,1)} %get-tuple-element.17.refs_4_), channel_id=1, source_target_pairs={{0,56},{8,0},{16,8},{24,16},{32,24},{40,32},{48,40},{56,48},{1,57}... | collective-permute-start | bytes 1179656 | tf_op jit(solution)/shard_map/ppermute | solution.py:216
  14.7 6.6 %collective-permute-done.2.refs_7_ = bf16[1536,128]{1,0:T(8,128)(2,1)S(1)} collective-permute-done((bf16[1536,128]{1,0:T(8,128)(2,1)}, bf16[1536,128]{1,0:T(8,128)(2,1)S(1)}, u32[]{:S(2)}, u32[]{:S(2)}) %collective-permute-start.2) | collective-permute-done | bytes 393248 | tf_op jit(solution)/shard_map/ppermute | solution.py:217
  21.4 0.0 collective-permute-start.5
  21.4 1.9 %collective-permute-done.6.refs_9_ = bf16[1536,128]{1,0:T(8,128)(2,1)S(1)} collective-permute-done((bf16[1536,128]{1,0:T(8,128)(2,1)}, bf16[1536,128]{1,0:T(8,128)(2,1)S(1)}, u32[]{:S(2)}, u32[]{:S(2)}) %collective-permute-start.6) | collective-permute-done | bytes 393248 | tf_op jit(solution)/shard_map/ppermute | solution.py:219
  23.2 0.0 collective-permute-start.10
  23.2 3.0 %collective-permute-done.1.refs_2_.refs_5_ = bf16[3072,128]{1,0:T(8,128)(2,1)S(1)} collective-permute-done((bf16[3072,128]{1,0:T(8,128)(2,1)}, bf16[3072,128]{1,0:T(8,128)(2,1)S(1)}, u32[]{:S(2)}, u32[]{:S(2)}) %collective-permute-start.1) | collective-permute-done | bytes 786464 | tf_op jit(solution)/shard_map/ppermute | solution.py:223
  26.3 0.0 collective-permute-start.3
  26.3 2.1 %collective-permute-done.4.refs_6_ = bf16[1536,128]{1,0:T(8,128)(2,1)S(1)} collective-permute-done((bf16[1536,128]{1,0:T(8,128)(2,1)}, bf16[1536,128]{1,0:T(8,128)(2,1)S(1)}, u32[]{:S(2)}, u32[]{:S(2)}) %collective-permute-start.4) | collective-permute-done | bytes 393248 | tf_op jit(solution)/shard_map/ppermute | solution.py:216
  28.4 3.8 %collective-permute-start.8 = (bf16[1536,128]{1,0:T(8,128)(2,1)S(1)}, bf16[1536,128]{1,0:T(8,128)(2,1)S(1)}, u32[]{:S(2)}, u32[]{:S(2)}) collective-permute-start(bf16[1536,128]{1,0:T(8,128)(2,1)S(1)} %collective-permute-done.4.refs_6_), channel_id=1, source_target_pairs={{0,56},{8,0},{16,8},{24,16},{32,24},{40,32},{48,40},{56,48},{1,57}... | collective-permute-start | bytes 1179656 | tf_op jit(solution)/shard_map/ppermute | solution.py:216
  32.2 3.0 %collective-permute-done.5.refs_8_ = bf16[1536,128]{1,0:T(8,128)(2,1)S(1)} collective-permute-done((bf16[1536,128]{1,0:T(8,128)(2,1)}, bf16[1536,128]{1,0:T(8,128)(2,1)S(1)}, u32[]{:S(2)}, u32[]{:S(2)}) %collective-permute-start.5) | collective-permute-done | bytes 393248 | tf_op jit(solution)/shard_map/ppermute | solution.py:218
  35.2 2.0 %collective-permute-start.9 = (bf16[1536,128]{1,0:T(8,128)(2,1)S(1)}, bf16[1536,128]{1,0:T(8,128)(2,1)}, u32[]{:S(2)}, u32[]{:S(2)}) collective-permute-start(bf16[1536,128]{1,0:T(8,128)(2,1)S(1)} %collective-permute-done.2.refs_7_), channel_id=1, source_target_pairs={{0,56},{8,0},{16,8},{24,16},{32,24},{40,32},{48,40},{56,48},{1,57}... | collective-permute-start | bytes 1179656 | tf_op jit(solution)/shard_map/ppermute | solution.py:217
  37.2 2.9 %collective-permute-done.10.refs_7_ = bf16[1536,128]{1,0:T(8,128)(2,1)S(1)} collective-permute-done((bf16[1536,128]{1,0:T(8,128)(2,1)S(1)}, bf16[1536,128]{1,0:T(8,128)(2,1)S(1)}, u32[]{:S(2)}, u32[]{:S(2)}) %collective-permute-start.10) | collective-permute-done | bytes 393248 | tf_op jit(solution)/shard_map/ppermute | solution.py:219
  40.1 0.0 collective-permute-start.14
  40.1 0.0 collective-permute-done.refs_1_.refs_4_
  40.1 0.1 collective-permute-start.7
  40.3 1.3 %collective-permute-done.8.refs_4_ = bf16[1536,128]{1,0:T(8,128)(2,1)S(1)} collective-permute-done((bf16[1536,128]{1,0:T(8,128)(2,1)S(1)}, bf16[1536,128]{1,0:T(8,128)(2,1)S(1)}, u32[]{:S(2)}, u32[]{:S(2)}) %collective-permute-start.8) | collective-permute-done | bytes 393248 | tf_op jit(solution)/shard_map/ppermute | solution.py:216
  41.6 3.7 %collective-permute-start.11 = (bf16[1536,128]{1,0:T(8,128)(2,1)S(1)}, bf16[1536,128]{1,0:T(8,128)(2,1)}, u32[]{:S(2)}, u32[]{:S(2)}) collective-permute-start(bf16[1536,128]{1,0:T(8,128)(2,1)S(1)} %collective-permute-done.8.refs_4_), channel_id=1, source_target_pairs={{0,56},{8,0},{16,8},{24,16},{32,24},{40,32},{48,40},{56,48},{1,57}... | collective-permute-start | bytes 1179656 | tf_op jit(solution)/shard_map/ppermute | solution.py:216
  45.3 4.7 %collective-permute-done.9.refs_5_ = bf16[1536,128]{1,0:T(8,128)(2,1)} collective-permute-done((bf16[1536,128]{1,0:T(8,128)(2,1)S(1)}, bf16[1536,128]{1,0:T(8,128)(2,1)}, u32[]{:S(2)}, u32[]{:S(2)}) %collective-permute-start.9) | collective-permute-done | bytes 393248 | tf_op jit(solution)/shard_map/ppermute | solution.py:217
  50.0 3.8 %collective-permute-start.12 = (bf16[1536,128]{1,0:T(8,128)(2,1)}, bf16[1536,128]{1,0:T(8,128)(2,1)}, u32[]{:S(2)}, u32[]{:S(2)}) collective-permute-start(bf16[1536,128]{1,0:T(8,128)(2,1)} %collective-permute-done.9.refs_5_), channel_id=1, source_target_pairs={{0,56},{8,0},{16,8},{24,16},{32,24},{40,32},{48,40},{56,48},{1,57}... | collective-permute-start | bytes 1179656 | tf_op jit(solution)/shard_map/ppermute | solution.py:217
  53.8 0.0 collective-permute-done.14.refs_7_
  53.8 0.0 collective-permute-start.16
  53.8 0.0 collective-permute-done.3.refs_3_.refs_6_
  53.8 1.1 %copy-done = bf16[3072,128]{1,0:T(8,128)(2,1)S(1)} copy-done((bf16[3072,128]{1,0:T(8,128)(2,1)S(1)}, bf16[3072,128]{1,0:T(8,128)(2,1)}, u32[]{:S(2)}) %copy-start) | copy-done | bytes 786456
  55.0 1.0 %copy-done.4 = bf16[1536,128]{1,0:T(8,128)(2,1)S(1)} copy-done((bf16[1536,128]{1,0:T(8,128)(2,1)S(1)}, bf16[1536,128]{1,0:T(8,128)(2,1)}, u32[]{:S(2)}) %copy-start.4) | copy-done | bytes 393240
  56.0 1.0 %copy-done.5 = bf16[1536,128]{1,0:T(8,128)(2,1)S(1)} copy-done((bf16[1536,128]{1,0:T(8,128)(2,1)S(1)}, bf16[1536,128]{1,0:T(8,128)(2,1)}, u32[]{:S(2)}) %copy-start.5) | copy-done | bytes 393240
  57.0 3.0 %shard_map.47.refs_0_ = bf16[3,128,512]{2,1,0:T(8,128)(2,1)S(1)} custom-call(bf16[3072,128]{1,0:T(8,128)(2,1)S(1)} %copy-done, bf16[3072,128]{1,0:T(8,128)(2,1)S(1)} %collective-permute-done.refs_1_.refs_4_, bf16[3072,128]{1,0:T(8,128)(2,1)S(1)} %collective-permute-done.1.refs_2_.refs_5_, bf16[3072,128]{1,0:T(8,128)(2,1)S(1)} %collective-permute-done.3.refs_3_.refs_6_, ...), custom_call_target="tpu_custom_call" | custom-call | flops 1207959552 | bytes 7340032 | tf_op jit(solution)/shard_map/pallas_call | solution.py:144
  60.0 0.0 collective-permute-done.7.refs_6_
  60.0 0.1 collective-permute-start.13
  60.1 2.4 %shard_map.48.refs_1_ = bf16[2,128,512]{2,1,0:T(8,128)(2,1)S(1)} custom-call(bf16[3072,128]{1,0:T(8,128)(2,1)S(1)} %copy-done, bf16[3072,128]{1,0:T(8,128)(2,1)S(1)} %collective-permute-done.refs_1_.refs_4_, bf16[3072,128]{1,0:T(8,128)(2,1)S(1)} %collective-permute-done.1.refs_2_.refs_5_, bf16[3072,128]{1,0:T(8,128)(2,1)S(1)} %collective-permute-done.3.refs_3_.refs_6_, ...), custom_call_target="tpu_custom_call" | custom-call | flops 805306368 | bytes 7340032 | tf_op jit(solution)/shard_map/pallas_call | solution.py:144
  62.5 0.0 copy-start.2
  62.6 0.7 copy-done.2
  63.2 0.0 collective-permute-done.11.refs_4_
  63.3 3.2 %collective-permute-start.15 = (bf16[1536,128]{1,0:T(8,128)(2,1)}, bf16[1536,128]{1,0:T(8,128)(2,1)}, u32[]{:S(2)}, u32[]{:S(2)}) collective-permute-start(bf16[1536,128]{1,0:T(8,128)(2,1)} %collective-permute-done.11.refs_4_), channel_id=1, source_target_pairs={{0,56},{8,0},{16,8},{24,16},{32,24},{40,32},{48,40},{56,48},{1,57}... | collective-permute-start | bytes 1179656 | tf_op jit(solution)/shard_map/ppermute | solution.py:234
  66.5 0.1 pad_add_fusion.pos_ref
  66.6 0.4 collective-permute-done.12.refs_5_
  67.0 7.4 %collective-permute-done.13.refs_6_ = bf16[1536,128]{1,0:T(8,128)(2,1)} collective-permute-done((bf16[1536,128]{1,0:T(8,128)(2,1)}, bf16[1536,128]{1,0:T(8,128)(2,1)}, u32[]{:S(2)}, u32[]{:S(2)}) %collective-permute-start.13) | collective-permute-done | bytes 393248 | tf_op jit(solution)/shard_map/ppermute | solution.py:218
  74.4 0.0 copy-done.1
  74.4 2.4 %shard_map.49.refs_2_ = bf16[2,128,512]{2,1,0:T(8,128)(2,1)S(1)} custom-call(bf16[3072,128]{1,0:T(8,128)(2,1)S(1)} %copy-done.1, bf16[3072,128]{1,0:T(8,128)(2,1)S(1)} %collective-permute-done.refs_1_.refs_4_, bf16[3072,128]{1,0:T(8,128)(2,1)S(1)} %collective-permute-done.1.refs_2_.refs_5_, bf16[3072,128]{1,0:T(8,128)(2,1)S(1)} %collective-permute-done.3.refs_3_.refs_6_, ...), custom_call_target="tpu_custom_call" | custom-call | flops 805306368 | bytes 7340032 | tf_op jit(solution)/shard_map/pallas_call | solution.py:144
  76.7 0.0 collective-permute-done.16.refs_8_
  76.7 0.0 collective-permute-done.15.refs_7_
  76.8 1.7 %shard_map.50 = bf16[8,128,512]{2,1,0:T(8,128)(2,1)S(1)} custom-call(s32[2]{0:T(128)S(1)} %pad_add_fusion.pos_ref, bf16[3,128,512]{2,1,0:T(8,128)(2,1)S(1)} %shard_map.47.refs_0_, bf16[2,128,512]{2,1,0:T(8,128)(2,1)S(1)} %copy-done.3, bf16[2,128,512]{2,1,0:T(8,128)(2,1)S(1)} %shard_map.49.refs_2_, bf16[3072,128]{1,0:T(8,128)(2,1)S(1)} %copy-done.1, ...), custom_call_target="tpu_custom_call" | custom-call | flops 402653184 | bytes 6291456 | tf_op jit(solution)/shard_map/pallas_call | solution.py:173
  78.5 19.3 %all_to_all.5.in_ref = bf16[8,128,512]{2,1,0:T(8,128)(2,1)S(1)} all-to-all(bf16[8,128,512]{2,1,0:T(8,128)(2,1)S(1)} %shard_map.50), channel_id=1, replica_groups=mesh['row'=4,'col'=8,'aux'=8] {'aux'}, dimensions={0} | all-to-all | bytes 2097152 | tf_op jit(solution)/shard_map/all_to_all | solution.py:237
  97.8 1.5 %shard_map.51 = f32[128,4,128]{2,1,0:T(4,128)} custom-call(s32[2]{0:T(128)S(1)} %pad_add_fusion.pos_ref, bf16[8,128,512]{2,1,0:T(8,128)(2,1)S(1)} %all_to_all.5.in_ref), custom_call_target="tpu_custom_call" | custom-call | flops 524288 | bytes 1048576 | tf_op jit(solution)/shard_map/pallas_call | solution.py:195
  (6 shorter events, 0.0 us)
Async XLA Ops:
  5.2 21.1 %collective-permute-start.1 = (bf16[3072,128]{1,0:T(8,128)(2,1)}, bf16[3072,128]{1,0:T(8,128)(2,1)S(1)}, u32[]{:S(2)}, u32[]{:S(2)}) collective-permute-start(bf16[3072,128]{1,0:T(8,128)(2,1)} %get-tuple-element.14.refs_0_.refs_3_), channel_id=1, source_target_pairs={{0,128},{64,192},{128,0},{192,64},{1,129},{65,193},{129,1},{193,65... | collective-permute-start | bytes 2359304 | tf_op jit(solution)/shard_map/ppermute | solution.py:223
  7.4 14.0 %collective-permute-start.2 = (bf16[1536,128]{1,0:T(8,128)(2,1)}, bf16[1536,128]{1,0:T(8,128)(2,1)S(1)}, u32[]{:S(2)}, u32[]{:S(2)}) collective-permute-start(bf16[1536,128]{1,0:T(8,128)(2,1)} %get-tuple-element.15.refs_5_), channel_id=1, source_target_pairs={{0,56},{8,0},{16,8},{24,16},{32,24},{40,32},{48,40},{56,48},{1,57}... | collective-permute-start | bytes 1179656 | tf_op jit(solution)/shard_map/ppermute | solution.py:217
  11.5 11.8 %collective-permute-start.6 = (bf16[1536,128]{1,0:T(8,128)(2,1)}, bf16[1536,128]{1,0:T(8,128)(2,1)S(1)}, u32[]{:S(2)}, u32[]{:S(2)}) collective-permute-start(bf16[1536,128]{1,0:T(8,128)(2,1)} %get-tuple-element.15.refs_5_), channel_id=1, source_target_pairs={{0,8},{8,16},{16,24},{24,32},{32,40},{40,48},{48,56},{56,0},{1,9},... | collective-permute-start | bytes 1179656 | tf_op jit(solution)/shard_map/ppermute | solution.py:219
  11.5 28.6 %collective-permute-start = (bf16[3072,128]{1,0:T(8,128)(2,1)}, bf16[3072,128]{1,0:T(8,128)(2,1)S(1)}, u32[]{:S(2)}, u32[]{:S(2)}) collective-permute-start(bf16[3072,128]{1,0:T(8,128)(2,1)} %get-tuple-element.14.refs_0_.refs_3_), channel_id=1, source_target_pairs={{0,64},{64,0},{128,192},{192,128},{1,65},{65,1},{129,193},{193,129... | collective-permute-start | bytes 2359304 | tf_op jit(solution)/shard_map/ppermute | solution.py:222
  11.5 16.9 %collective-permute-start.4 = (bf16[1536,128]{1,0:T(8,128)(2,1)}, bf16[1536,128]{1,0:T(8,128)(2,1)S(1)}, u32[]{:S(2)}, u32[]{:S(2)}) collective-permute-start(bf16[1536,128]{1,0:T(8,128)(2,1)} %get-tuple-element.17.refs_4_), channel_id=1, source_target_pairs={{0,56},{8,0},{16,8},{24,16},{32,24},{40,32},{48,40},{56,48},{1,57}... | collective-permute-start | bytes 1179656 | tf_op jit(solution)/shard_map/ppermute | solution.py:216
  21.4 13.8 %collective-permute-start.5 = (bf16[1536,128]{1,0:T(8,128)(2,1)}, bf16[1536,128]{1,0:T(8,128)(2,1)S(1)}, u32[]{:S(2)}, u32[]{:S(2)}) collective-permute-start(bf16[1536,128]{1,0:T(8,128)(2,1)} %get-tuple-element.17.refs_4_), channel_id=1, source_target_pairs={{0,8},{8,16},{16,24},{24,32},{32,40},{40,48},{48,56},{56,0},{1,9},... | collective-permute-start | bytes 1179656 | tf_op jit(solution)/shard_map/ppermute | solution.py:218
  23.2 16.9 %collective-permute-start.10 = (bf16[1536,128]{1,0:T(8,128)(2,1)S(1)}, bf16[1536,128]{1,0:T(8,128)(2,1)S(1)}, u32[]{:S(2)}, u32[]{:S(2)}) collective-permute-start(bf16[1536,128]{1,0:T(8,128)(2,1)S(1)} %collective-permute-done.6.refs_9_), channel_id=1, source_target_pairs={{0,8},{8,16},{16,24},{24,32},{32,40},{40,48},{48,56},{56,0},{1,9},... | collective-permute-start | bytes 1179656 | tf_op jit(solution)/shard_map/ppermute | solution.py:219
  26.3 27.5 %collective-permute-start.3 = (bf16[3072,128]{1,0:T(8,128)(2,1)S(1)}, bf16[3072,128]{1,0:T(8,128)(2,1)S(1)}, u32[]{:S(2)}, u32[]{:S(2)}) collective-permute-start(bf16[3072,128]{1,0:T(8,128)(2,1)S(1)} %collective-permute-done.1.refs_2_.refs_5_), channel_id=1, source_target_pairs={{0,64},{64,0},{128,192},{192,128},{1,65},{65,1},{129,193},{193,129... | collective-permute-start | bytes 2359304 | tf_op jit(solution)/shard_map/ppermute | solution.py:227
  28.4 13.2 %collective-permute-start.8 = (bf16[1536,128]{1,0:T(8,128)(2,1)S(1)}, bf16[1536,128]{1,0:T(8,128)(2,1)S(1)}, u32[]{:S(2)}, u32[]{:S(2)}) collective-permute-start(bf16[1536,128]{1,0:T(8,128)(2,1)S(1)} %collective-permute-done.4.refs_6_), channel_id=1, source_target_pairs={{0,56},{8,0},{16,8},{24,16},{32,24},{40,32},{48,40},{56,48},{1,57}... | collective-permute-start | bytes 1179656 | tf_op jit(solution)/shard_map/ppermute | solution.py:216
  35.2 14.8 %collective-permute-start.9 = (bf16[1536,128]{1,0:T(8,128)(2,1)S(1)}, bf16[1536,128]{1,0:T(8,128)(2,1)}, u32[]{:S(2)}, u32[]{:S(2)}) collective-permute-start(bf16[1536,128]{1,0:T(8,128)(2,1)S(1)} %collective-permute-done.2.refs_7_), channel_id=1, source_target_pairs={{0,56},{8,0},{16,8},{24,16},{32,24},{40,32},{48,40},{56,48},{1,57}... | collective-permute-start | bytes 1179656 | tf_op jit(solution)/shard_map/ppermute | solution.py:217
  40.1 13.7 %collective-permute-start.14 = (bf16[1536,128]{1,0:T(8,128)(2,1)S(1)}, bf16[1536,128]{1,0:T(8,128)(2,1)}, u32[]{:S(2)}, u32[]{:S(2)}) collective-permute-start(bf16[1536,128]{1,0:T(8,128)(2,1)S(1)} %collective-permute-done.10.refs_7_), channel_id=1, source_target_pairs={{0,8},{8,16},{16,24},{24,32},{32,40},{40,48},{48,56},{56,0},{1,9},... | collective-permute-start | bytes 1179656 | tf_op jit(solution)/shard_map/ppermute | solution.py:219
  40.1 19.9 %collective-permute-start.7 = (bf16[1536,128]{1,0:T(8,128)(2,1)S(1)}, bf16[1536,128]{1,0:T(8,128)(2,1)}, u32[]{:S(2)}, u32[]{:S(2)}) collective-permute-start(bf16[1536,128]{1,0:T(8,128)(2,1)S(1)} %collective-permute-done.5.refs_8_), channel_id=1, source_target_pairs={{0,8},{8,16},{16,24},{24,32},{32,40},{40,48},{48,56},{56,0},{1,9},... | collective-permute-start | bytes 1179656 | tf_op jit(solution)/shard_map/ppermute | solution.py:218
  41.6 21.7 %collective-permute-start.11 = (bf16[1536,128]{1,0:T(8,128)(2,1)S(1)}, bf16[1536,128]{1,0:T(8,128)(2,1)}, u32[]{:S(2)}, u32[]{:S(2)}) collective-permute-start(bf16[1536,128]{1,0:T(8,128)(2,1)S(1)} %collective-permute-done.8.refs_4_), channel_id=1, source_target_pairs={{0,56},{8,0},{16,8},{24,16},{32,24},{40,32},{48,40},{56,48},{1,57}... | collective-permute-start | bytes 1179656 | tf_op jit(solution)/shard_map/ppermute | solution.py:216
  50.0 17.0 %collective-permute-start.12 = (bf16[1536,128]{1,0:T(8,128)(2,1)}, bf16[1536,128]{1,0:T(8,128)(2,1)}, u32[]{:S(2)}, u32[]{:S(2)}) collective-permute-start(bf16[1536,128]{1,0:T(8,128)(2,1)} %collective-permute-done.9.refs_5_), channel_id=1, source_target_pairs={{0,56},{8,0},{16,8},{24,16},{32,24},{40,32},{48,40},{56,48},{1,57}... | collective-permute-start | bytes 1179656 | tf_op jit(solution)/shard_map/ppermute | solution.py:217
  53.8 22.9 %collective-permute-start.16 = (bf16[1536,128]{1,0:T(8,128)(2,1)}, bf16[1536,128]{1,0:T(8,128)(2,1)}, u32[]{:S(2)}, u32[]{:S(2)}) collective-permute-start(bf16[1536,128]{1,0:T(8,128)(2,1)} %collective-permute-done.14.refs_7_), channel_id=1, source_target_pairs={{0,8},{8,16},{16,24},{24,32},{32,40},{40,48},{48,56},{56,0},{1,9},... | collective-permute-start | bytes 1179656 | tf_op jit(solution)/shard_map/ppermute | solution.py:234
  53.8 1.1 %copy-start = (bf16[3072,128]{1,0:T(8,128)(2,1)S(1)}, bf16[3072,128]{1,0:T(8,128)(2,1)}, u32[]{:S(2)}) copy-start(bf16[3072,128]{1,0:T(8,128)(2,1)} %get-tuple-element.14.refs_0_.refs_3_) | copy-start | bytes 2359300
  55.0 1.0 %copy-start.4 = (bf16[1536,128]{1,0:T(8,128)(2,1)S(1)}, bf16[1536,128]{1,0:T(8,128)(2,1)}, u32[]{:S(2)}) copy-start(bf16[1536,128]{1,0:T(8,128)(2,1)} %get-tuple-element.17.refs_4_) | copy-start | bytes 1179652
  56.0 1.0 %copy-start.5 = (bf16[1536,128]{1,0:T(8,128)(2,1)S(1)}, bf16[1536,128]{1,0:T(8,128)(2,1)}, u32[]{:S(2)}) copy-start(bf16[1536,128]{1,0:T(8,128)(2,1)} %get-tuple-element.15.refs_5_) | copy-start | bytes 1179652
  60.0 14.4 %copy-start.1 = (bf16[3072,128]{1,0:T(8,128)(2,1)S(1)}, bf16[3072,128]{1,0:T(8,128)(2,1)}, u32[]{:S(2)}) copy-start(bf16[3072,128]{1,0:T(8,128)(2,1)} %get-tuple-element.14.refs_0_.refs_3_) | copy-start | bytes 2359300
  60.0 14.4 %collective-permute-start.13 = (bf16[1536,128]{1,0:T(8,128)(2,1)}, bf16[1536,128]{1,0:T(8,128)(2,1)}, u32[]{:S(2)}, u32[]{:S(2)}) collective-permute-start(bf16[1536,128]{1,0:T(8,128)(2,1)} %collective-permute-done.7.refs_6_), channel_id=1, source_target_pairs={{0,8},{8,16},{16,24},{24,32},{32,40},{40,48},{48,56},{56,0},{1,9},... | collective-permute-start | bytes 1179656 | tf_op jit(solution)/shard_map/ppermute | solution.py:218
  62.5 0.7 copy-start.2
  63.3 13.5 %collective-permute-start.15 = (bf16[1536,128]{1,0:T(8,128)(2,1)}, bf16[1536,128]{1,0:T(8,128)(2,1)}, u32[]{:S(2)}, u32[]{:S(2)}) collective-permute-start(bf16[1536,128]{1,0:T(8,128)(2,1)} %collective-permute-done.11.refs_4_), channel_id=1, source_target_pairs={{0,56},{8,0},{16,8},{24,16},{32,24},{40,32},{48,40},{56,48},{1,57}... | collective-permute-start | bytes 1179656 | tf_op jit(solution)/shard_map/ppermute | solution.py:234
  66.5 10.3 %copy-start.3 = (bf16[2,128,512]{2,1,0:T(8,128)(2,1)S(1)}, bf16[2,128,512]{2,1,0:T(8,128)(2,1)}, u32[]{:S(2)}) copy-start(bf16[2,128,512]{2,1,0:T(8,128)(2,1)} %copy-done.2) | copy-start | bytes 786436

commit v3 on v2

v3 whole, which is shorter than its diff:
```python
import functools

import jax
import jax.numpy as jnp
from jax import lax
from jax.experimental import pallas as pl
from jax.experimental.pallas import tpu as pltpu
from jax.sharding import PartitionSpec as P

WIDE_LIMIT = 60 * 1024 * 1024
VMEM_LIMIT = 16 * 1024 * 1024
CHUNKS = 2


def half_kernel(mask_ref, slot_ref, orb_ref, int_ref, whole_ref,
                place_ref, weight_ref, orb_buf, int_buf, out_buf, int_sem, orb_sem, out_sem):
    chunks, capacity, block, lanes = int_buf.shape
    rows = out_buf.shape[1]
    occ = orb_buf.shape[0]
    row_blocks, block_count = mask_ref.shape
    low = lax.broadcasted_iota(jnp.int32, (occ, 2 * block), 1) < block

    def load(c):
        return pltpu.make_async_copy(int_ref.at[:, :, pl.ds(c * lanes, lanes)], int_buf.at[c], int_sem.at[c])

    orb_load = pltpu.make_async_copy(orb_ref, orb_buf, orb_sem)
    orb_load.start()
    for c in range(chunks):
        load(c).start()

    position = lax.broadcasted_iota(jnp.int32, mask_ref.shape, 0) * block_count + lax.broadcasted_iota(
        jnp.int32, mask_ref.shape, 1
    )
    slots = jnp.where(mask_ref[...] == 1, slot_ref[...], -1)
    for s in range(capacity):
        place_ref[s] = jnp.max(jnp.where(slots == s, position, -1))

    orb_load.wait()
    for pair in range(capacity // 2):
        parts = []
        for s in (2 * pair, 2 * pair + 1):
            place = place_ref[s]
            at = jnp.maximum(place, 0)
            home = at // block_count
            parity = lax.rem(at, 2)
            start = pl.multiple_of((lax.rem(at, block_count) // 2) * (2 * block), 2 * block)
            columns = orb_buf[:, pl.ds(start, 2 * block)].astype(jnp.float32)
            turned = pltpu.roll(columns, block, 1)
            value = jnp.where(parity == (s % 2), columns, turned)
            parts.append((place, home, value))
        for b in range(row_blocks):
            chosen = [jnp.where((place >= 0) & (home == b), value, 0.0) for place, home, value in parts]
            weight_ref[b * occ : (b + 1) * occ, pair * 2 * block : (pair + 1) * 2 * block] = jnp.where(
                low, chosen[0], chosen[1]
            ).astype(weight_ref.dtype)

    def store(c):
        return pltpu.make_async_copy(out_buf.at[c], whole_ref.at[pl.ds(c * rows, rows)], out_sem.at[c])

    for c in range(chunks):
        load(c).wait()
        packed = int_buf[c].reshape(capacity * block, lanes)
        product = jnp.dot(weight_ref[...], packed, preferred_element_type=jnp.float32)
        for pair in range(lanes // (2 * block)):
            first = product[:occ, pair * 2 * block : (pair + 1) * 2 * block]
            second = product[occ:, pair * 2 * block : (pair + 1) * 2 * block]
            out_buf[c, 2 * pair * occ : (2 * pair + 1) * occ, :] = jnp.where(
                low, first, pltpu.roll(second, block, 1)
            ).astype(out_buf.dtype)
            out_buf[c, (2 * pair + 1) * occ : (2 * pair + 2) * occ, :] = jnp.where(
                low, pltpu.roll(first, block, 1), second
            ).astype(out_buf.dtype)
        store(c).start()
    for c in range(chunks):
        store(c).wait()


def half_transform(mask, slots, packed, orbitals):
    capacity, block, width = packed.shape
    occ = orbitals.shape[0]
    lanes = width // CHUNKS
    rows = lanes // block * occ
    vmem = pl.BlockSpec(memory_space=pltpu.VMEM)
    anywhere = pl.BlockSpec(memory_space=pl.ANY)
    return pl.pallas_call(
        half_kernel,
        out_shape=jax.ShapeDtypeStruct((rows * CHUNKS, 2 * block), jnp.bfloat16),
        in_specs=[vmem, vmem, anywhere, anywhere],
        out_specs=anywhere,
        scratch_shapes=[
            pltpu.SMEM((capacity,), jnp.int32),
            pltpu.VMEM((2 * occ, capacity * block), jnp.bfloat16),
            pltpu.VMEM(orbitals.shape, jnp.bfloat16),
            pltpu.VMEM((CHUNKS, capacity, block, lanes), jnp.bfloat16),
            pltpu.VMEM((CHUNKS, rows, 2 * block), jnp.bfloat16),
            pltpu.SemaphoreType.DMA((CHUNKS,)),
            pltpu.SemaphoreType.DMA,
            pltpu.SemaphoreType.DMA((CHUNKS,)),
        ],
        compiler_params=pltpu.CompilerParams(vmem_limit_bytes=WIDE_LIMIT),
        cost_estimate=pl.CostEstimate(flops=2 * 2 * occ * capacity * block * width, bytes_accessed=5 << 20, transcendentals=0),
    )(mask, slots, orbitals, packed)


CONTRACT = (((0,), (0,)), ((), ()))


def tile_of(parts, col_refs):
    total, start = None, 0
    for ref in parts:
        rows = ref.shape[0]
        columns = jnp.concatenate([c[start : start + rows, :] for c in col_refs], axis=1)
        term = lax.dot_general(ref[...], columns, CONTRACT, preferred_element_type=jnp.float32)
        total = term if total is None else total + term
        start += rows
    return total


def early_kernel(orders, *refs):
    count = len(orders)
    col_refs, moved = refs[:4], refs[4 : 4 + count]
    out_refs = refs[4 + count : -2]
    held, sems = refs[-2:]
    copies = [pltpu.make_async_copy(ref, held.at[n], sems.at[n]) for n, ref in enumerate(moved)]
    for copy in copies:
        copy.start()
    filled = [0, 0]
    for n, (group, order) in enumerate(orders):
        copies[n].wait()
        tile = tile_of([held.at[n]], [col_refs[o] for o in order])
        out_refs[group][filled[group]] = tile.astype(out_refs[group].dtype)
        filled[group] += 1


def early_tiles(col_panels, kept, sent):
    depth, width = col_panels[0].shape
    orders = [(0, (0, 1, 2, 3))] * len(kept) + [(1, (1, 0, 3, 2))] * len(sent)
    vmem = pl.BlockSpec(memory_space=pltpu.VMEM)
    return pl.pallas_call(
        functools.partial(early_kernel, orders),
        out_shape=tuple(
            jax.ShapeDtypeStruct((len(group), width, 4 * width), jnp.bfloat16) for group in (kept, sent)
        ),
        in_specs=[vmem] * 4 + [pl.BlockSpec(memory_space=pl.ANY)] * len(orders),
        out_specs=(vmem, vmem),
        scratch_shapes=[
            pltpu.VMEM((len(orders), depth, width), jnp.bfloat16),
            pltpu.SemaphoreType.DMA((len(orders),)),
        ],
        compiler_params=pltpu.CompilerParams(vmem_limit_bytes=VMEM_LIMIT),
        cost_estimate=pl.CostEstimate(flops=8 * width * width * depth * len(orders), bytes_accessed=7 << 20, transcendentals=0),
    )(*col_panels, *kept, *sent)


def last_kernel(ring, *refs):
    col_refs, far_ref, out_ref = refs[4:8], refs[8], refs[9]
    near_ref, outer_ref, near_other_ref, outer_other_ref = refs[:4]
    col, core = lax.axis_index("col"), lax.rem(lax.axis_index("row"), 2)

    def origin(d):
        return lax.rem(col + jnp.where(core == 0, d, ring - d), ring)

    for d in range(3):
        out_ref[origin(d)] = near_ref[d]
    out_ref[origin(3)] = outer_ref[0]
    for d in range(1, 3):
        out_ref[origin(ring - d)] = near_other_ref[d - 1]
    out_ref[origin(ring - 3)] = outer_other_ref[0]
    out_ref[origin(4)] = tile_of([far_ref], col_refs).astype(out_ref.dtype)


def last_tile(done, col_panels, far, ring):
    depth, width = far.shape
    return pl.pallas_call(
        functools.partial(last_kernel, ring),
        out_shape=jax.ShapeDtypeStruct((ring, width, 4 * width), jnp.bfloat16),
        in_specs=[pl.BlockSpec(memory_space=pltpu.VMEM)] * 9,
        out_specs=pl.BlockSpec(memory_space=pltpu.VMEM),
        compiler_params=pltpu.CompilerParams(vmem_limit_bytes=VMEM_LIMIT),
        cost_estimate=pl.CostEstimate(flops=8 * width * width * depth, bytes_accessed=6 << 20, transcendentals=0),
    )(*done, *col_panels, far)


def sum_kernel(in_ref, out_ref):
    row = lax.axis_index("row")
    width = out_ref.shape[2]
    for rho in range(out_ref.shape[1]):
        total = None
        for a in range(in_ref.shape[0]):
            term = in_ref[a, :, rho * width : (rho + 1) * width].astype(jnp.float32)
            total = term if total is None else total + term
        out_ref[:, row ^ rho, :] = total


def sum_parts(received):
    count, width, wide = received.shape
    return pl.pallas_call(
        sum_kernel,
        out_shape=jax.ShapeDtypeStruct((width, wide // width, width), jnp.float32),
        in_specs=[pl.BlockSpec(memory_space=pltpu.VMEM)],
        out_specs=pl.BlockSpec(memory_space=pltpu.VMEM),
        compiler_params=pltpu.CompilerParams(vmem_limit_bytes=VMEM_LIMIT),
        cost_estimate=pl.CostEstimate(flops=count * width * wide, bytes_accessed=2 * count * width * wide, transcendentals=0),
    )(received)


def local(integrals, block_mask, block_slots, orbitals):
    ring, rows_n = lax.axis_size("col"), lax.axis_size("row")
    whole = half_transform(block_mask[0], block_slots[0], integrals[0], orbitals)

    along = [
        (r * ring + z, r * ring + (z + (ring - 1 if r % 2 == 0 else 1)) % ring)
        for r in range(rows_n)
        for z in range(ring)
    ]

    def hop(panel):
        return lax.ppermute(panel, ("row", "col"), along)

    def to_row(value, rho):
        return lax.ppermute(value, "row", [(i, i ^ rho) for i in range(rows_n)])

    kept = [whole, hop(whole)]
    beside = to_row(whole, 1)
    over = to_row(whole, 2)
    sent = [hop(beside)]
    kept.append(hop(kept[1]))
    sent.append(hop(sent[0]))
    over, kept[2] = lax.optimization_barrier((over, kept[2]))
    diagonal = to_row(over, 1)
    col_panels = [whole, beside, over, diagonal]
    near = early_tiles(col_panels, kept, sent)
    third = hop(kept[2])
    third_sent = hop(sent[1])
    near_kept, near_sent, third = lax.optimization_barrier((*near, third))
    far = hop(third)
    near_other = to_row(near_sent, 1)
    outer_kept, outer_sent = early_tiles(col_panels, [third], [third_sent])
    outer_other = to_row(outer_sent, 1)
    sums = last_tile([near_kept, outer_kept, near_other, outer_other], col_panels, far, ring)
    received = lax.all_to_all(sums, "aux", 0, 0, tiled=True)
    return sum_parts(received)


def solution(mesh):
    placed = (
        P("aux", ("row", "col"), None, None),
        P("aux", ("row", "col"), None),
        P("aux", ("row", "col"), None),
        P(),
    )
    return jax.shard_map(
        local, mesh=mesh, in_specs=placed, out_specs=P(("row", "aux"), None, "col"), check_vma=False
    )
```

time: 99.6 us -> 92.5 us (0.929)
  Pallas kernels: 16.3 us -> 10.3 us
  local copies, waits for them, and re-layouts: 3.82 us -> 1.14 us
  blocking collectives: 19.3 us -> 20.3 us
    pallas_call x4 -> x3, Pallas kernels: 13 us -> 8.79 us  [the longest x2 4.74 us: early_tiles(): pl.pallas_call(functools.partial(early_kernel, orders), out_shape=tuple((...]
    unnamed x12 -> x4, local copies, waits for them, and re-layouts: 3.82 us -> 1.14 us
    pallas_call x1, Pallas kernels: 1.74 us -> 0.61 us  [last_tile(): pl.pallas_call(functools.partial(last_kernel, ring), out_shape=jax.ShapeD...]
    all_to_all x1, blocking collectives: 19.3 us -> 20.3 us  [local(): received = lax.all_to_all(sums, 'aux', 0, 0, tiled=True)]
    ppermute x17 -> x12, starting transfers between devices: 26.3 us -> 27.2 us  [the longest x7 26.7 us: hop(): return lax.ppermute(panel, ('row', 'col'), along)]
    ppermute x17 -> x12, waiting for transfers between devices: 33.4 us -> 33.2 us  [the longest x7 33.2 us: hop(): return lax.ppermute(panel, ('row', 'col'), along)]
  transfers between devices with their start and end apart: 17 -> 12, of which waited for: 10 -> 7; matrix products, arithmetic and copies ran while one was open for 0% -> 0% of each run, Pallas kernels for 8% -> 5%
where the time goes in v3:
time: 92.5 us; the launch traced here: 92.3 us
  waiting for transfers between devices  33.2 us (36%)
  starting transfers between devices  27.2 us (29%)
  blocking collectives  20.3 us (22%)
  Pallas kernels  10.3 us (11%)
  local copies, waits for them, and re-layouts  1.14 us (1%)
    ppermute x7, waiting for transfers between devices, hop(): return lax.ppermute(panel, ('row', 'col'), along)  33.2 us
    ppermute x7, starting transfers between devices, hop(): return lax.ppermute(panel, ('row', 'col'), along)  26.7 us
    all_to_all x1, blocking collectives, local(): received = lax.all_to_all(sums, 'aux', 0, 0, tiled=True)  20.3 us
    pallas_call x2, Pallas kernels, early_tiles(): pl.pallas_call(functools.partial(early_kernel, orders), out_shape=tuple((...  4.74 us
    pallas_call x1, Pallas kernels, half_transform(): pl.pallas_call(half_kernel, out_shape=jax.ShapeDtypeStruct((rows * CHUNKS...  4.05 us
  transfers between devices with their start and end apart: 12, of which 7 were waited for; matrix products, arithmetic and copies ran while one was open for 0% of the time, Pallas kernels for 5%

profile of v3, /device:TPU:16, one launch (start us, length us, event | category | flops | bytes accessed | tf_op | source)
XLA Modules:
  0.0 92.3 jit_solution(8845427983412895345)
XLA Ops:
  0.0 4.0 %shard_map.46.refs_0_.refs_4_ = bf16[3072,128]{1,0:T(8,128)(2,1)} custom-call(s32[2,64]{1,0:T(2,128)} %bitcast.4, s32[2,64]{1,0:T(2,128)} %bitcast.5, bf16[64,4096]{1,0:T(8,128)(2,1)} %orb_ref.1, bf16[8,64,3072]{2,1,0:T(8,128)(2,1)} %bitcast.3), custom_call_target="tpu_custom_call" | custom-call | flops 402653184 | bytes 5242880 | tf_op jit(solution)/shard_map/pallas_call | solution.py:85
  4.1 0.1 collective-permute-start
  4.2 5.9 %collective-permute-start.2 = (bf16[3072,128]{1,0:T(8,128)(2,1)}, bf16[3072,128]{1,0:T(8,128)(2,1)S(1)}, u32[]{:S(2)}, u32[]{:S(2)}) collective-permute-start(bf16[3072,128]{1,0:T(8,128)(2,1)} %shard_map.46.refs_0_.refs_4_), channel_id=1, source_target_pairs={{0,56},{8,0},{16,8},{24,16},{32,24},{40,32},{48,40},{56,48},{64,72... | collective-permute-start | bytes 2359304 | tf_op jit(solution)/shard_map/ppermute | solution.py:218
  10.1 0.0 collective-permute-done.refs_1_.refs_5_
  10.1 2.4 %collective-permute-start.5 = (bf16[3072,128]{1,0:T(8,128)(2,1)S(1)}, bf16[3072,128]{1,0:T(8,128)(2,1)S(1)}, u32[]{:S(2)}, u32[]{:S(2)}) collective-permute-start(bf16[3072,128]{1,0:T(8,128)(2,1)S(1)} %collective-permute-done.refs_1_.refs_5_), channel_id=1, source_target_pairs={{0,56},{8,0},{16,8},{24,16},{32,24},{40,32},{48,40},{56,48},{64,72... | collective-permute-start | bytes 2359304 | tf_op jit(solution)/shard_map/ppermute | solution.py:218
  12.5 0.3 collective-permute-start.1
  12.8 7.1 %collective-permute-done.2.refs_5_ = bf16[3072,128]{1,0:T(8,128)(2,1)S(1)} collective-permute-done((bf16[3072,128]{1,0:T(8,128)(2,1)}, bf16[3072,128]{1,0:T(8,128)(2,1)S(1)}, u32[]{:S(2)}, u32[]{:S(2)}) %collective-permute-start.2) | collective-permute-done | bytes 786464 | tf_op jit(solution)/shard_map/ppermute | solution.py:218
  19.9 3.6 %collective-permute-start.3 = (bf16[3072,128]{1,0:T(8,128)(2,1)S(1)}, bf16[3072,128]{1,0:T(8,128)(2,1)S(1)}, u32[]{:S(2)}, u32[]{:S(2)}) collective-permute-start(bf16[3072,128]{1,0:T(8,128)(2,1)S(1)} %collective-permute-done.2.refs_5_), channel_id=1, source_target_pairs={{0,56},{8,0},{16,8},{24,16},{32,24},{40,32},{48,40},{56,48},{64,72... | collective-permute-start | bytes 2359304 | tf_op jit(solution)/shard_map/ppermute | solution.py:218
  23.5 4.7 %collective-permute-done.5.refs_7_ = bf16[3072,128]{1,0:T(8,128)(2,1)S(1)} collective-permute-done((bf16[3072,128]{1,0:T(8,128)(2,1)S(1)}, bf16[3072,128]{1,0:T(8,128)(2,1)S(1)}, u32[]{:S(2)}, u32[]{:S(2)}) %collective-permute-start.5) | collective-permute-done | bytes 786464 | tf_op jit(solution)/shard_map/ppermute | solution.py:218
  28.2 3.7 %collective-permute-start.6 = (bf16[3072,128]{1,0:T(8,128)(2,1)S(1)}, bf16[3072,128]{1,0:T(8,128)(2,1)S(1)}, u32[]{:S(2)}, u32[]{:S(2)}) collective-permute-start(bf16[3072,128]{1,0:T(8,128)(2,1)S(1)} %collective-permute-done.5.refs_7_), channel_id=1, source_target_pairs={{0,56},{8,0},{16,8},{24,16},{32,24},{40,32},{48,40},{56,48},{64,72... | collective-permute-start | bytes 2359304 | tf_op jit(solution)/shard_map/ppermute | solution.py:218
  31.9 0.0 collective-permute-done.1.refs_2_.refs_6_
  31.9 4.7 %collective-permute-done.3.refs_6_ = bf16[3072,128]{1,0:T(8,128)(2,1)S(1)} collective-permute-done((bf16[3072,128]{1,0:T(8,128)(2,1)S(1)}, bf16[3072,128]{1,0:T(8,128)(2,1)S(1)}, u32[]{:S(2)}, u32[]{:S(2)}) %collective-permute-start.3) | collective-permute-done | bytes 786464 | tf_op jit(solution)/shard_map/ppermute | solution.py:218
  36.7 0.0 collective-permute-start.4
  36.7 3.7 %collective-permute-start.7 = (bf16[3072,128]{1,0:T(8,128)(2,1)S(1)}, bf16[3072,128]{1,0:T(8,128)(2,1)S(1)}, u32[]{:S(2)}, u32[]{:S(2)}) collective-permute-start(bf16[3072,128]{1,0:T(8,128)(2,1)S(1)} %collective-permute-done.3.refs_6_), channel_id=1, source_target_pairs={{0,56},{8,0},{16,8},{24,16},{32,24},{40,32},{48,40},{56,48},{64,72... | collective-permute-start | bytes 2359304 | tf_op jit(solution)/shard_map/ppermute | solution.py:218
  40.4 4.7 %collective-permute-done.6.refs_8_ = bf16[3072,128]{1,0:T(8,128)(2,1)S(1)} collective-permute-done((bf16[3072,128]{1,0:T(8,128)(2,1)S(1)}, bf16[3072,128]{1,0:T(8,128)(2,1)S(1)}, u32[]{:S(2)}, u32[]{:S(2)}) %collective-permute-start.6) | collective-permute-done | bytes 786464 | tf_op jit(solution)/shard_map/ppermute | solution.py:218
  45.1 3.7 %collective-permute-start.8 = (bf16[3072,128]{1,0:T(8,128)(2,1)S(1)}, bf16[3072,128]{1,0:T(8,128)(2,1)S(1)}, u32[]{:S(2)}, u32[]{:S(2)}) collective-permute-start(bf16[3072,128]{1,0:T(8,128)(2,1)S(1)} %collective-permute-done.6.refs_8_), channel_id=1, source_target_pairs={{0,56},{8,0},{16,8},{24,16},{32,24},{40,32},{48,40},{56,48},{64,72... | collective-permute-start | bytes 2359304 | tf_op jit(solution)/shard_map/ppermute | solution.py:218
  48.8 0.0 collective-permute-done.4.refs_3_.refs_7_
  48.8 0.0 copy-start
  48.8 1.1 %copy-done = bf16[3072,128]{1,0:T(8,128)(2,1)S(1)} copy-done((bf16[3072,128]{1,0:T(8,128)(2,1)S(1)}, bf16[3072,128]{1,0:T(8,128)(2,1)}, u32[]{:S(2)}) %copy-start) | copy-done | bytes 786456
  49.9 3.4 %shard_map.47 = (bf16[3,128,512]{2,1,0:T(8,128)(2,1)S(1)}, bf16[2,128,512]{2,1,0:T(8,128)(2,1)S(1)}) custom-call(bf16[3072,128]{1,0:T(8,128)(2,1)S(1)} %copy-done, bf16[3072,128]{1,0:T(8,128)(2,1)S(1)} %collective-permute-done.refs_1_.refs_5_, bf16[3072,128]{1,0:T(8,128)(2,1)S(1)} %collective-permute-done.1.refs_2_.refs_6_, ...), custom_call_target="tpu_custom_call" | custom-call | flops 2013265920 | bytes 7340032 | tf_op jit(solution)/shard_map/pallas_call | solution.py:139
  53.3 0.0 copy-start.1
  53.3 0.2 collective-permute-done.7.refs_4_
  53.5 3.7 %collective-permute-start.11 = (bf16[3072,128]{1,0:T(8,128)(2,1)S(1)}, bf16[3072,128]{1,0:T(8,128)(2,1)S(1)}, u32[]{:S(2)}, u32[]{:S(2)}) collective-permute-start(bf16[3072,128]{1,0:T(8,128)(2,1)S(1)} %collective-permute-done.7.refs_4_), channel_id=1, source_target_pairs={{0,56},{8,0},{16,8},{24,16},{32,24},{40,32},{48,40},{56,48},{64,72... | collective-permute-start | bytes 2359304 | tf_op jit(solution)/shard_map/ppermute | solution.py:218
  57.2 0.0 collective-permute-start.9
  57.2 4.7 %collective-permute-done.8.refs_5_ = bf16[3072,128]{1,0:T(8,128)(2,1)S(1)} collective-permute-done((bf16[3072,128]{1,0:T(8,128)(2,1)S(1)}, bf16[3072,128]{1,0:T(8,128)(2,1)S(1)}, u32[]{:S(2)}, u32[]{:S(2)}) %collective-permute-start.8) | collective-permute-done | bytes 786464 | tf_op jit(solution)/shard_map/ppermute | solution.py:218
  62.0 1.4 %shard_map.48 = (bf16[1,128,512]{2,1,0:T(8,128)(2,1)S(1)}, bf16[1,128,512]{2,1,0:T(8,128)(2,1)S(1)}) custom-call(bf16[3072,128]{1,0:T(8,128)(2,1)S(1)} %copy-done, bf16[3072,128]{1,0:T(8,128)(2,1)S(1)} %collective-permute-done.refs_1_.refs_5_, bf16[3072,128]{1,0:T(8,128)(2,1)S(1)} %collective-permute-done.1.refs_2_.refs_6_, ...), custom_call_target="tpu_custom_call" | custom-call | flops 805306368 | bytes 7340032 | tf_op jit(solution)/shard_map/pallas_call | solution.py:139
  63.3 0.1 collective-permute-start.10
  63.4 0.0 collective-permute-done.9.refs_2_
  63.4 7.0 %collective-permute-done.11.refs_8_ = bf16[3072,128]{1,0:T(8,128)(2,1)S(1)} collective-permute-done((bf16[3072,128]{1,0:T(8,128)(2,1)S(1)}, bf16[3072,128]{1,0:T(8,128)(2,1)S(1)}, u32[]{:S(2)}, u32[]{:S(2)}) %collective-permute-start.11) | collective-permute-done | bytes 786464 | tf_op jit(solution)/shard_map/ppermute | solution.py:218
  70.4 0.0 collective-permute-done.10.refs_3_
  70.4 0.0 copy-done.1
  70.4 0.6 shard_map.49
  71.0 20.3 %all_to_all.5.in_ref = bf16[8,128,512]{2,1,0:T(8,128)(2,1)S(1)} all-to-all(bf16[8,128,512]{2,1,0:T(8,128)(2,1)S(1)} %shard_map.49), channel_id=1, replica_groups=mesh['row'=4,'col'=8,'aux'=8] {'aux'}, dimensions={0} | all-to-all | bytes 2097152 | tf_op jit(solution)/shard_map/all_to_all | solution.py:241
  91.3 1.0 %shard_map.50 = f32[128,4,128]{2,1,0:T(4,128)} custom-call(bf16[8,128,512]{2,1,0:T(8,128)(2,1)S(1)} %all_to_all.5.in_ref), custom_call_target="tpu_custom_call" | custom-call | flops 524288 | bytes 1048576 | tf_op jit(solution)/shard_map/pallas_call | solution.py:197
Async XLA Ops:
  4.1 6.0 %collective-permute-start = (bf16[3072,128]{1,0:T(8,128)(2,1)}, bf16[3072,128]{1,0:T(8,128)(2,1)S(1)}, u32[]{:S(2)}, u32[]{:S(2)}) collective-permute-start(bf16[3072,128]{1,0:T(8,128)(2,1)} %shard_map.46.refs_0_.refs_4_), channel_id=1, source_target_pairs={{0,64},{64,0},{128,192},{192,128},{1,65},{65,1},{129,193},{193,129... | collective-permute-start | bytes 2359304 | tf_op jit(solution)/shard_map/ppermute | solution.py:221
  4.2 15.8 %collective-permute-start.2 = (bf16[3072,128]{1,0:T(8,128)(2,1)}, bf16[3072,128]{1,0:T(8,128)(2,1)S(1)}, u32[]{:S(2)}, u32[]{:S(2)}) collective-permute-start(bf16[3072,128]{1,0:T(8,128)(2,1)} %shard_map.46.refs_0_.refs_4_), channel_id=1, source_target_pairs={{0,56},{8,0},{16,8},{24,16},{32,24},{40,32},{48,40},{56,48},{64,72... | collective-permute-start | bytes 2359304 | tf_op jit(solution)/shard_map/ppermute | solution.py:218
  10.1 18.1 %collective-permute-start.5 = (bf16[3072,128]{1,0:T(8,128)(2,1)S(1)}, bf16[3072,128]{1,0:T(8,128)(2,1)S(1)}, u32[]{:S(2)}, u32[]{:S(2)}) collective-permute-start(bf16[3072,128]{1,0:T(8,128)(2,1)S(1)} %collective-permute-done.refs_1_.refs_5_), channel_id=1, source_target_pairs={{0,56},{8,0},{16,8},{24,16},{32,24},{40,32},{48,40},{56,48},{64,72... | collective-permute-start | bytes 2359304 | tf_op jit(solution)/shard_map/ppermute | solution.py:218
  12.5 19.4 %collective-permute-start.1 = (bf16[3072,128]{1,0:T(8,128)(2,1)}, bf16[3072,128]{1,0:T(8,128)(2,1)S(1)}, u32[]{:S(2)}, u32[]{:S(2)}) collective-permute-start(bf16[3072,128]{1,0:T(8,128)(2,1)} %shard_map.46.refs_0_.refs_4_), channel_id=1, source_target_pairs={{0,128},{64,192},{128,0},{192,64},{1,129},{65,193},{129,1},{193,65... | collective-permute-start | bytes 2359304 | tf_op jit(solution)/shard_map/ppermute | solution.py:221
  19.9 16.7 %collective-permute-start.3 = (bf16[3072,128]{1,0:T(8,128)(2,1)S(1)}, bf16[3072,128]{1,0:T(8,128)(2,1)S(1)}, u32[]{:S(2)}, u32[]{:S(2)}) collective-permute-start(bf16[3072,128]{1,0:T(8,128)(2,1)S(1)} %collective-permute-done.2.refs_5_), channel_id=1, source_target_pairs={{0,56},{8,0},{16,8},{24,16},{32,24},{40,32},{48,40},{56,48},{64,72... | collective-permute-start | bytes 2359304 | tf_op jit(solution)/shard_map/ppermute | solution.py:218
  28.2 16.9 %collective-permute-start.6 = (bf16[3072,128]{1,0:T(8,128)(2,1)S(1)}, bf16[3072,128]{1,0:T(8,128)(2,1)S(1)}, u32[]{:S(2)}, u32[]{:S(2)}) collective-permute-start(bf16[3072,128]{1,0:T(8,128)(2,1)S(1)} %collective-permute-done.5.refs_7_), channel_id=1, source_target_pairs={{0,56},{8,0},{16,8},{24,16},{32,24},{40,32},{48,40},{56,48},{64,72... | collective-permute-start | bytes 2359304 | tf_op jit(solution)/shard_map/ppermute | solution.py:218
  36.7 12.1 %collective-permute-start.4 = (bf16[3072,128]{1,0:T(8,128)(2,1)S(1)}, bf16[3072,128]{1,0:T(8,128)(2,1)S(1)}, u32[]{:S(2)}, u32[]{:S(2)}) collective-permute-start(bf16[3072,128]{1,0:T(8,128)(2,1)S(1)} %collective-permute-done.1.refs_2_.refs_6_), channel_id=1, source_target_pairs={{0,64},{64,0},{128,192},{192,128},{1,65},{65,1},{129,193},{193,129... | collective-permute-start | bytes 2359304 | tf_op jit(solution)/shard_map/ppermute | solution.py:221
  36.7 16.8 %collective-permute-start.7 = (bf16[3072,128]{1,0:T(8,128)(2,1)S(1)}, bf16[3072,128]{1,0:T(8,128)(2,1)S(1)}, u32[]{:S(2)}, u32[]{:S(2)}) collective-permute-start(bf16[3072,128]{1,0:T(8,128)(2,1)S(1)} %collective-permute-done.3.refs_6_), channel_id=1, source_target_pairs={{0,56},{8,0},{16,8},{24,16},{32,24},{40,32},{48,40},{56,48},{64,72... | collective-permute-start | bytes 2359304 | tf_op jit(solution)/shard_map/ppermute | solution.py:218
  45.1 16.9 %collective-permute-start.8 = (bf16[3072,128]{1,0:T(8,128)(2,1)S(1)}, bf16[3072,128]{1,0:T(8,128)(2,1)S(1)}, u32[]{:S(2)}, u32[]{:S(2)}) collective-permute-start(bf16[3072,128]{1,0:T(8,128)(2,1)S(1)} %collective-permute-done.6.refs_8_), channel_id=1, source_target_pairs={{0,56},{8,0},{16,8},{24,16},{32,24},{40,32},{48,40},{56,48},{64,72... | collective-permute-start | bytes 2359304 | tf_op jit(solution)/shard_map/ppermute | solution.py:218
  48.8 1.1 %copy-start = (bf16[3072,128]{1,0:T(8,128)(2,1)S(1)}, bf16[3072,128]{1,0:T(8,128)(2,1)}, u32[]{:S(2)}) copy-start(bf16[3072,128]{1,0:T(8,128)(2,1)} %shard_map.46.refs_0_.refs_4_) | copy-start | bytes 2359300
  53.3 17.1 %copy-start.1 = (bf16[3072,128]{1,0:T(8,128)(2,1)S(1)}, bf16[3072,128]{1,0:T(8,128)(2,1)}, u32[]{:S(2)}) copy-start(bf16[3072,128]{1,0:T(8,128)(2,1)} %shard_map.46.refs_0_.refs_4_) | copy-start | bytes 2359300
  53.5 16.9 %collective-permute-start.11 = (bf16[3072,128]{1,0:T(8,128)(2,1)S(1)}, bf16[3072,128]{1,0:T(8,128)(2,1)S(1)}, u32[]{:S(2)}, u32[]{:S(2)}) collective-permute-start(bf16[3072,128]{1,0:T(8,128)(2,1)S(1)} %collective-permute-done.7.refs_4_), channel_id=1, source_target_pairs={{0,56},{8,0},{16,8},{24,16},{32,24},{40,32},{48,40},{56,48},{64,72... | collective-permute-start | bytes 2359304 | tf_op jit(solution)/shard_map/ppermute | solution.py:218
  57.2 6.2 %collective-permute-start.9 = (bf16[2,128,512]{2,1,0:T(8,128)(2,1)S(1)}, bf16[2,128,512]{2,1,0:T(8,128)(2,1)S(1)}, u32[]{:S(2)}, u32[]{:S(2)}) collective-permute-start(bf16[2,128,512]{2,1,0:T(8,128)(2,1)S(1)} %get-tuple-element.21), channel_id=1, source_target_pairs={{0,64},{64,0},{128,192},{192,128},{1,65},{65,1},{129,193},{193,129... | collective-permute-start | bytes 786440 | tf_op jit(solution)/shard_map/ppermute | solution.py:221
  63.3 7.1 %collective-permute-start.10 = (bf16[1,128,512]{2,1,0:T(8,128)(2,1)S(1)}, bf16[1,128,512]{2,1,0:T(8,128)(2,1)S(1)}, u32[]{:S(2)}, u32[]{:S(2)}) collective-permute-start(bf16[1,128,512]{2,1,0:T(8,128)(2,1)S(1)} %get-tuple-element.22), channel_id=1, source_target_pairs={{0,64},{64,0},{128,192},{192,128},{1,65},{65,1},{129,193},{193,129... | collective-permute-start | bytes 393224 | tf_op jit(solution)/shard_map/ppermute | solution.py:221

commit v4 on v3

--- a/solution.py
+++ b/solution.py
@@ -116,7 +116,30 @@
     return total
 
 
-def early_kernel(orders, *refs):
+def packed_diagonal(square):
+    size = square.shape[0]
+    row = lax.broadcasted_iota(jnp.int32, square.shape, 0)
+    column = lax.broadcasted_iota(jnp.int32, square.shape, 1)
+    left = square - square.astype(jnp.bfloat16).astype(jnp.float32)
+    left = jnp.sum(jnp.where(row == column, left, 0.0), axis=0, keepdims=True)
+    final = jnp.sum(jnp.where(column[:1] == size - 1, left, 0.0), axis=1, keepdims=True)
+    left = jnp.where((row == size - 1) & (column == 0), final, left)
+    return jnp.where(row > column, left, square)
+
+
+def unpacked_diagonal(square):
+    size = square.shape[0]
+    row = lax.broadcasted_iota(jnp.int32, square.shape, 0)
+    column = lax.broadcasted_iota(jnp.int32, square.shape, 1)
+    bottom = square[size - 1 :, :]
+    final = jnp.sum(jnp.where(column[:1] == 0, bottom, 0.0), axis=1, keepdims=True)
+    left = jnp.where(column[:1] == 0, square[size - 2 : size - 1, :], bottom)
+    left = jnp.where(column[:1] == size - 1, final, left)
+    whole = jnp.where(row > column, square.T, square)
+    return jnp.where(row == column, square + left, whole)
+
+
+def early_kernel(orders, own, *refs):
     count = len(orders)
     col_refs, moved = refs[:4], refs[4 : 4 + count]
     out_refs = refs[4 + count : -2]
@@ -128,16 +151,19 @@
     for n, (group, order) in enumerate(orders):
         copies[n].wait()
         tile = tile_of([held.at[n]], [col_refs[o] for o in order])
+        if own and n == 0:
+            size = tile.shape[0]
+            tile = jnp.concatenate([packed_diagonal(tile[:, :size]), tile[:, size:]], axis=1)
         out_refs[group][filled[group]] = tile.astype(out_refs[group].dtype)
         filled[group] += 1
 
 
-def early_tiles(col_panels, kept, sent):
+def early_tiles(col_panels, kept, sent, own):
     depth, width = col_panels[0].shape
     orders = [(0, (0, 1, 2, 3))] * len(kept) + [(1, (1, 0, 3, 2))] * len(sent)
     vmem = pl.BlockSpec(memory_space=pltpu.VMEM)
     return pl.pallas_call(
-        functools.partial(early_kernel, orders),
+        functools.partial(early_kernel, orders, own),
         out_shape=tuple(
             jax.ShapeDtypeStruct((len(group), width, 4 * width), jnp.bfloat16) for group in (kept, sent)
         ),
@@ -190,6 +216,10 @@
             term = in_ref[a, :, rho * width : (rho + 1) * width].astype(jnp.float32)
             total = term if total is None else total + term
         out_ref[:, row ^ rho, :] = total
+        if rho == 0:
+            @pl.when(lax.axis_index("aux") == lax.axis_index("col"))
+            def _(total=total):
+                out_ref[:, row, :] = unpacked_diagonal(total)
 
 
 def sum_parts(received):
@@ -229,13 +259,13 @@
     over, kept[2] = lax.optimization_barrier((over, kept[2]))
     diagonal = to_row(over, 1)
     col_panels = [whole, beside, over, diagonal]
-    near = early_tiles(col_panels, kept, sent)
+    near = early_tiles(col_panels, kept, sent, True)
     third = hop(kept[2])
     third_sent = hop(sent[1])
     near_kept, near_sent, third = lax.optimization_barrier((*near, third))
     far = hop(third)
     near_other = to_row(near_sent, 1)
-    outer_kept, outer_sent = early_tiles(col_panels, [third], [third_sent])
+    outer_kept, outer_sent = early_tiles(col_panels, [third], [third_sent], False)
     outer_other = to_row(outer_sent, 1)
     sums = last_tile([near_kept, outer_kept, near_other, outer_other], col_panels, far, ring)
     received = lax.all_to_all(sums, "aux", 0, 0, tiled=True)

time: 92.5 us -> 92.6 us (level)
  no operation moved by 1% of the time
where the time goes in v4:
time: 92.6 us; the launch traced here: 92.4 us
  waiting for transfers between devices  33.1 us (36%)
  starting transfers between devices  27.2 us (29%)
  blocking collectives  20.3 us (22%)
  Pallas kernels  10.6 us (11%)
  local copies, waits for them, and re-layouts  1.14 us (1%)
    ppermute x7, waiting for transfers between devices, hop(): return lax.ppermute(panel, ('row', 'col'), along)  33 us
    ppermute x7, starting transfers between devices, hop(): return lax.ppermute(panel, ('row', 'col'), along)  26.7 us
    all_to_all x1, blocking collectives, local(): received = lax.all_to_all(sums, 'aux', 0, 0, tiled=True)  20.3 us
    pallas_call x2, Pallas kernels, early_tiles(): pl.pallas_call(functools.partial(early_kernel, orders, own), out_shape=tu...  4.86 us
    pallas_call x1, Pallas kernels, half_transform(): pl.pallas_call(half_kernel, out_shape=jax.ShapeDtypeStruct((rows * CHUNKS...  4.05 us
  transfers between devices with their start and end apart: 12, of which 7 were waited for; matrix products, arithmetic and copies ran while one was open for 0% of the time, Pallas kernels for 5%

profile of v4, /device:TPU:16, one launch (start us, length us, event | category | flops | bytes accessed | tf_op | source)
XLA Modules:
  0.0 92.4 jit_solution(1658779356196667816)
XLA Ops:
  0.0 4.0 %shard_map.46.refs_0_.refs_4_ = bf16[3072,128]{1,0:T(8,128)(2,1)} custom-call(s32[2,64]{1,0:T(2,128)} %bitcast.4, s32[2,64]{1,0:T(2,128)} %bitcast.5, bf16[64,4096]{1,0:T(8,128)(2,1)} %orb_ref.1, bf16[8,64,3072]{2,1,0:T(8,128)(2,1)} %bitcast.3), custom_call_target="tpu_custom_call" | custom-call | flops 402653184 | bytes 5242880 | tf_op jit(solution)/shard_map/pallas_call | solution.py:85
  4.1 0.1 collective-permute-start
  4.2 5.9 %collective-permute-start.2 = (bf16[3072,128]{1,0:T(8,128)(2,1)}, bf16[3072,128]{1,0:T(8,128)(2,1)S(1)}, u32[]{:S(2)}, u32[]{:S(2)}) collective-permute-start(bf16[3072,128]{1,0:T(8,128)(2,1)} %shard_map.46.refs_0_.refs_4_), channel_id=1, source_target_pairs={{0,56},{8,0},{16,8},{24,16},{32,24},{40,32},{48,40},{56,48},{64,72... | collective-permute-start | bytes 2359304 | tf_op jit(solution)/shard_map/ppermute | solution.py:248
  10.1 0.0 collective-permute-done.refs_1_.refs_5_
  10.1 2.4 %collective-permute-start.5 = (bf16[3072,128]{1,0:T(8,128)(2,1)S(1)}, bf16[3072,128]{1,0:T(8,128)(2,1)S(1)}, u32[]{:S(2)}, u32[]{:S(2)}) collective-permute-start(bf16[3072,128]{1,0:T(8,128)(2,1)S(1)} %collective-permute-done.refs_1_.refs_5_), channel_id=1, source_target_pairs={{0,56},{8,0},{16,8},{24,16},{32,24},{40,32},{48,40},{56,48},{64,72... | collective-permute-start | bytes 2359304 | tf_op jit(solution)/shard_map/ppermute | solution.py:248
  12.5 0.3 collective-permute-start.1
  12.8 7.1 %collective-permute-done.2.refs_5_ = bf16[3072,128]{1,0:T(8,128)(2,1)S(1)} collective-permute-done((bf16[3072,128]{1,0:T(8,128)(2,1)}, bf16[3072,128]{1,0:T(8,128)(2,1)S(1)}, u32[]{:S(2)}, u32[]{:S(2)}) %collective-permute-start.2) | collective-permute-done | bytes 786464 | tf_op jit(solution)/shard_map/ppermute | solution.py:248
  19.9 3.6 %collective-permute-start.3 = (bf16[3072,128]{1,0:T(8,128)(2,1)S(1)}, bf16[3072,128]{1,0:T(8,128)(2,1)S(1)}, u32[]{:S(2)}, u32[]{:S(2)}) collective-permute-start(bf16[3072,128]{1,0:T(8,128)(2,1)S(1)} %collective-permute-done.2.refs_5_), channel_id=1, source_target_pairs={{0,56},{8,0},{16,8},{24,16},{32,24},{40,32},{48,40},{56,48},{64,72... | collective-permute-start | bytes 2359304 | tf_op jit(solution)/shard_map/ppermute | solution.py:248
  23.5 4.7 %collective-permute-done.5.refs_7_ = bf16[3072,128]{1,0:T(8,128)(2,1)S(1)} collective-permute-done((bf16[3072,128]{1,0:T(8,128)(2,1)S(1)}, bf16[3072,128]{1,0:T(8,128)(2,1)S(1)}, u32[]{:S(2)}, u32[]{:S(2)}) %collective-permute-start.5) | collective-permute-done | bytes 786464 | tf_op jit(solution)/shard_map/ppermute | solution.py:248
  28.2 3.7 %collective-permute-start.6 = (bf16[3072,128]{1,0:T(8,128)(2,1)S(1)}, bf16[3072,128]{1,0:T(8,128)(2,1)S(1)}, u32[]{:S(2)}, u32[]{:S(2)}) collective-permute-start(bf16[3072,128]{1,0:T(8,128)(2,1)S(1)} %collective-permute-done.5.refs_7_), channel_id=1, source_target_pairs={{0,56},{8,0},{16,8},{24,16},{32,24},{40,32},{48,40},{56,48},{64,72... | collective-permute-start | bytes 2359304 | tf_op jit(solution)/shard_map/ppermute | solution.py:248
  31.9 0.0 collective-permute-done.1.refs_2_.refs_6_
  31.9 4.7 %collective-permute-done.3.refs_6_ = bf16[3072,128]{1,0:T(8,128)(2,1)S(1)} collective-permute-done((bf16[3072,128]{1,0:T(8,128)(2,1)S(1)}, bf16[3072,128]{1,0:T(8,128)(2,1)S(1)}, u32[]{:S(2)}, u32[]{:S(2)}) %collective-permute-start.3) | collective-permute-done | bytes 786464 | tf_op jit(solution)/shard_map/ppermute | solution.py:248
  36.7 0.0 collective-permute-start.4
  36.7 3.7 %collective-permute-start.7 = (bf16[3072,128]{1,0:T(8,128)(2,1)S(1)}, bf16[3072,128]{1,0:T(8,128)(2,1)S(1)}, u32[]{:S(2)}, u32[]{:S(2)}) collective-permute-start(bf16[3072,128]{1,0:T(8,128)(2,1)S(1)} %collective-permute-done.3.refs_6_), channel_id=1, source_target_pairs={{0,56},{8,0},{16,8},{24,16},{32,24},{40,32},{48,40},{56,48},{64,72... | collective-permute-start | bytes 2359304 | tf_op jit(solution)/shard_map/ppermute | solution.py:248
  40.4 4.7 %collective-permute-done.6.refs_8_ = bf16[3072,128]{1,0:T(8,128)(2,1)S(1)} collective-permute-done((bf16[3072,128]{1,0:T(8,128)(2,1)S(1)}, bf16[3072,128]{1,0:T(8,128)(2,1)S(1)}, u32[]{:S(2)}, u32[]{:S(2)}) %collective-permute-start.6) | collective-permute-done | bytes 786464 | tf_op jit(solution)/shard_map/ppermute | solution.py:248
  45.1 3.7 %collective-permute-start.8 = (bf16[3072,128]{1,0:T(8,128)(2,1)S(1)}, bf16[3072,128]{1,0:T(8,128)(2,1)S(1)}, u32[]{:S(2)}, u32[]{:S(2)}) collective-permute-start(bf16[3072,128]{1,0:T(8,128)(2,1)S(1)} %collective-permute-done.6.refs_8_), channel_id=1, source_target_pairs={{0,56},{8,0},{16,8},{24,16},{32,24},{40,32},{48,40},{56,48},{64,72... | collective-permute-start | bytes 2359304 | tf_op jit(solution)/shard_map/ppermute | solution.py:248
  48.8 0.0 collective-permute-done.4.refs_3_.refs_7_
  48.8 0.0 copy-start
  48.8 1.1 %copy-done = bf16[3072,128]{1,0:T(8,128)(2,1)S(1)} copy-done((bf16[3072,128]{1,0:T(8,128)(2,1)S(1)}, bf16[3072,128]{1,0:T(8,128)(2,1)}, u32[]{:S(2)}) %copy-start) | copy-done | bytes 786456
  49.9 3.5 %shard_map.47 = (bf16[3,128,512]{2,1,0:T(8,128)(2,1)S(1)}, bf16[2,128,512]{2,1,0:T(8,128)(2,1)S(1)}) custom-call(bf16[3072,128]{1,0:T(8,128)(2,1)S(1)} %copy-done, bf16[3072,128]{1,0:T(8,128)(2,1)S(1)} %collective-permute-done.refs_1_.refs_5_, bf16[3072,128]{1,0:T(8,128)(2,1)S(1)} %collective-permute-done.1.refs_2_.refs_6_, ...), custom_call_target="tpu_custom_call" | custom-call | flops 2013265920 | bytes 7340032 | tf_op jit(solution)/shard_map/pallas_call | solution.py:165
  53.4 0.0 copy-start.1
  53.4 0.1 collective-permute-done.7.refs_4_
  53.5 3.7 %collective-permute-start.11 = (bf16[3072,128]{1,0:T(8,128)(2,1)S(1)}, bf16[3072,128]{1,0:T(8,128)(2,1)S(1)}, u32[]{:S(2)}, u32[]{:S(2)}) collective-permute-start(bf16[3072,128]{1,0:T(8,128)(2,1)S(1)} %collective-permute-done.7.refs_4_), channel_id=1, source_target_pairs={{0,56},{8,0},{16,8},{24,16},{32,24},{40,32},{48,40},{56,48},{64,72... | collective-permute-start | bytes 2359304 | tf_op jit(solution)/shard_map/ppermute | solution.py:248
  57.2 0.0 collective-permute-start.9
  57.2 4.7 %collective-permute-done.8.refs_5_ = bf16[3072,128]{1,0:T(8,128)(2,1)S(1)} collective-permute-done((bf16[3072,128]{1,0:T(8,128)(2,1)S(1)}, bf16[3072,128]{1,0:T(8,128)(2,1)S(1)}, u32[]{:S(2)}, u32[]{:S(2)}) %collective-permute-start.8) | collective-permute-done | bytes 786464 | tf_op jit(solution)/shard_map/ppermute | solution.py:248
  62.0 1.4 %shard_map.48 = (bf16[1,128,512]{2,1,0:T(8,128)(2,1)S(1)}, bf16[1,128,512]{2,1,0:T(8,128)(2,1)S(1)}) custom-call(bf16[3072,128]{1,0:T(8,128)(2,1)S(1)} %copy-done, bf16[3072,128]{1,0:T(8,128)(2,1)S(1)} %collective-permute-done.refs_1_.refs_5_, bf16[3072,128]{1,0:T(8,128)(2,1)S(1)} %collective-permute-done.1.refs_2_.refs_6_, ...), custom_call_target="tpu_custom_call" | custom-call | flops 805306368 | bytes 7340032 | tf_op jit(solution)/shard_map/pallas_call | solution.py:165
  63.3 0.1 collective-permute-start.10
  63.4 0.0 collective-permute-done.9.refs_2_
  63.4 7.0 %collective-permute-done.11.refs_8_ = bf16[3072,128]{1,0:T(8,128)(2,1)S(1)} collective-permute-done((bf16[3072,128]{1,0:T(8,128)(2,1)S(1)}, bf16[3072,128]{1,0:T(8,128)(2,1)S(1)}, u32[]{:S(2)}, u32[]{:S(2)}) %collective-permute-start.11) | collective-permute-done | bytes 786464 | tf_op jit(solution)/shard_map/ppermute | solution.py:248
  70.4 0.0 collective-permute-done.10.refs_3_
  70.4 0.0 copy-done.1
  70.4 0.6 shard_map.49
  71.0 20.3 %all_to_all.5.in_ref = bf16[8,128,512]{2,1,0:T(8,128)(2,1)S(1)} all-to-all(bf16[8,128,512]{2,1,0:T(8,128)(2,1)S(1)} %shard_map.49), channel_id=1, replica_groups=mesh['row'=4,'col'=8,'aux'=8] {'aux'}, dimensions={0} | all-to-all | bytes 2097152 | tf_op jit(solution)/shard_map/all_to_all | solution.py:271
  91.3 1.1 %shard_map.50 = f32[128,4,128]{2,1,0:T(4,128)} custom-call(bf16[8,128,512]{2,1,0:T(8,128)(2,1)S(1)} %all_to_all.5.in_ref), custom_call_target="tpu_custom_call" | custom-call | flops 524288 | bytes 1048576 | tf_op jit(solution)/shard_map/pallas_call | solution.py:227
Async XLA Ops:
  4.1 6.0 %collective-permute-start = (bf16[3072,128]{1,0:T(8,128)(2,1)}, bf16[3072,128]{1,0:T(8,128)(2,1)S(1)}, u32[]{:S(2)}, u32[]{:S(2)}) collective-permute-start(bf16[3072,128]{1,0:T(8,128)(2,1)} %shard_map.46.refs_0_.refs_4_), channel_id=1, source_target_pairs={{0,64},{64,0},{128,192},{192,128},{1,65},{65,1},{129,193},{193,129... | collective-permute-start | bytes 2359304 | tf_op jit(solution)/shard_map/ppermute | solution.py:251
  4.2 15.8 %collective-permute-start.2 = (bf16[3072,128]{1,0:T(8,128)(2,1)}, bf16[3072,128]{1,0:T(8,128)(2,1)S(1)}, u32[]{:S(2)}, u32[]{:S(2)}) collective-permute-start(bf16[3072,128]{1,0:T(8,128)(2,1)} %shard_map.46.refs_0_.refs_4_), channel_id=1, source_target_pairs={{0,56},{8,0},{16,8},{24,16},{32,24},{40,32},{48,40},{56,48},{64,72... | collective-permute-start | bytes 2359304 | tf_op jit(solution)/shard_map/ppermute | solution.py:248
  10.1 18.1 %collective-permute-start.5 = (bf16[3072,128]{1,0:T(8,128)(2,1)S(1)}, bf16[3072,128]{1,0:T(8,128)(2,1)S(1)}, u32[]{:S(2)}, u32[]{:S(2)}) collective-permute-start(bf16[3072,128]{1,0:T(8,128)(2,1)S(1)} %collective-permute-done.refs_1_.refs_5_), channel_id=1, source_target_pairs={{0,56},{8,0},{16,8},{24,16},{32,24},{40,32},{48,40},{56,48},{64,72... | collective-permute-start | bytes 2359304 | tf_op jit(solution)/shard_map/ppermute | solution.py:248
  12.5 19.4 %collective-permute-start.1 = (bf16[3072,128]{1,0:T(8,128)(2,1)}, bf16[3072,128]{1,0:T(8,128)(2,1)S(1)}, u32[]{:S(2)}, u32[]{:S(2)}) collective-permute-start(bf16[3072,128]{1,0:T(8,128)(2,1)} %shard_map.46.refs_0_.refs_4_), channel_id=1, source_target_pairs={{0,128},{64,192},{128,0},{192,64},{1,129},{65,193},{129,1},{193,65... | collective-permute-start | bytes 2359304 | tf_op jit(solution)/shard_map/ppermute | solution.py:251
  19.9 16.7 %collective-permute-start.3 = (bf16[3072,128]{1,0:T(8,128)(2,1)S(1)}, bf16[3072,128]{1,0:T(8,128)(2,1)S(1)}, u32[]{:S(2)}, u32[]{:S(2)}) collective-permute-start(bf16[3072,128]{1,0:T(8,128)(2,1)S(1)} %collective-permute-done.2.refs_5_), channel_id=1, source_target_pairs={{0,56},{8,0},{16,8},{24,16},{32,24},{40,32},{48,40},{56,48},{64,72... | collective-permute-start | bytes 2359304 | tf_op jit(solution)/shard_map/ppermute | solution.py:248
  28.2 16.9 %collective-permute-start.6 = (bf16[3072,128]{1,0:T(8,128)(2,1)S(1)}, bf16[3072,128]{1,0:T(8,128)(2,1)S(1)}, u32[]{:S(2)}, u32[]{:S(2)}) collective-permute-start(bf16[3072,128]{1,0:T(8,128)(2,1)S(1)} %collective-permute-done.5.refs_7_), channel_id=1, source_target_pairs={{0,56},{8,0},{16,8},{24,16},{32,24},{40,32},{48,40},{56,48},{64,72... | collective-permute-start | bytes 2359304 | tf_op jit(solution)/shard_map/ppermute | solution.py:248
  36.7 12.1 %collective-permute-start.4 = (bf16[3072,128]{1,0:T(8,128)(2,1)S(1)}, bf16[3072,128]{1,0:T(8,128)(2,1)S(1)}, u32[]{:S(2)}, u32[]{:S(2)}) collective-permute-start(bf16[3072,128]{1,0:T(8,128)(2,1)S(1)} %collective-permute-done.1.refs_2_.refs_6_), channel_id=1, source_target_pairs={{0,64},{64,0},{128,192},{192,128},{1,65},{65,1},{129,193},{193,129... | collective-permute-start | bytes 2359304 | tf_op jit(solution)/shard_map/ppermute | solution.py:251
  36.7 16.8 %collective-permute-start.7 = (bf16[3072,128]{1,0:T(8,128)(2,1)S(1)}, bf16[3072,128]{1,0:T(8,128)(2,1)S(1)}, u32[]{:S(2)}, u32[]{:S(2)}) collective-permute-start(bf16[3072,128]{1,0:T(8,128)(2,1)S(1)} %collective-permute-done.3.refs_6_), channel_id=1, source_target_pairs={{0,56},{8,0},{16,8},{24,16},{32,24},{40,32},{48,40},{56,48},{64,72... | collective-permute-start | bytes 2359304 | tf_op jit(solution)/shard_map/ppermute | solution.py:248
  45.1 16.9 %collective-permute-start.8 = (bf16[3072,128]{1,0:T(8,128)(2,1)S(1)}, bf16[3072,128]{1,0:T(8,128)(2,1)S(1)}, u32[]{:S(2)}, u32[]{:S(2)}) collective-permute-start(bf16[3072,128]{1,0:T(8,128)(2,1)S(1)} %collective-permute-done.6.refs_8_), channel_id=1, source_target_pairs={{0,56},{8,0},{16,8},{24,16},{32,24},{40,32},{48,40},{56,48},{64,72... | collective-permute-start | bytes 2359304 | tf_op jit(solution)/shard_map/ppermute | solution.py:248
  48.8 1.1 %copy-start = (bf16[3072,128]{1,0:T(8,128)(2,1)S(1)}, bf16[3072,128]{1,0:T(8,128)(2,1)}, u32[]{:S(2)}) copy-start(bf16[3072,128]{1,0:T(8,128)(2,1)} %shard_map.46.refs_0_.refs_4_) | copy-start | bytes 2359300
  53.4 16.9 %copy-start.1 = (bf16[3072,128]{1,0:T(8,128)(2,1)S(1)}, bf16[3072,128]{1,0:T(8,128)(2,1)}, u32[]{:S(2)}) copy-start(bf16[3072,128]{1,0:T(8,128)(2,1)} %shard_map.46.refs_0_.refs_4_) | copy-start | bytes 2359300
  53.5 16.9 %collective-permute-start.11 = (bf16[3072,128]{1,0:T(8,128)(2,1)S(1)}, bf16[3072,128]{1,0:T(8,128)(2,1)S(1)}, u32[]{:S(2)}, u32[]{:S(2)}) collective-permute-start(bf16[3072,128]{1,0:T(8,128)(2,1)S(1)} %collective-permute-done.7.refs_4_), channel_id=1, source_target_pairs={{0,56},{8,0},{16,8},{24,16},{32,24},{40,32},{48,40},{56,48},{64,72... | collective-permute-start | bytes 2359304 | tf_op jit(solution)/shard_map/ppermute | solution.py:248
  57.2 6.2 %collective-permute-start.9 = (bf16[2,128,512]{2,1,0:T(8,128)(2,1)S(1)}, bf16[2,128,512]{2,1,0:T(8,128)(2,1)S(1)}, u32[]{:S(2)}, u32[]{:S(2)}) collective-permute-start(bf16[2,128,512]{2,1,0:T(8,128)(2,1)S(1)} %get-tuple-element.21), channel_id=1, source_target_pairs={{0,64},{64,0},{128,192},{192,128},{1,65},{65,1},{129,193},{193,129... | collective-permute-start | bytes 786440 | tf_op jit(solution)/shard_map/ppermute | solution.py:251
  63.3 7.1 %collective-permute-start.10 = (bf16[1,128,512]{2,1,0:T(8,128)(2,1)S(1)}, bf16[1,128,512]{2,1,0:T(8,128)(2,1)S(1)}, u32[]{:S(2)}, u32[]{:S(2)}) collective-permute-start(bf16[1,128,512]{2,1,0:T(8,128)(2,1)S(1)} %get-tuple-element.22), channel_id=1, source_target_pairs={{0,64},{64,0},{128,192},{192,128},{1,65},{65,1},{129,193},{193,129... | collective-permute-start | bytes 393224 | tf_op jit(solution)/shard_map/ppermute | solution.py:251

commit v5 on v4

--- a/solution.py
+++ b/solution.py
@@ -9,23 +9,25 @@
 
 WIDE_LIMIT = 60 * 1024 * 1024
 VMEM_LIMIT = 16 * 1024 * 1024
-CHUNKS = 2
+CHUNKS = ((0, 2), (2, 1))
+THIRDS = 3
 
 
 def half_kernel(mask_ref, slot_ref, orb_ref, int_ref, whole_ref,
                 place_ref, weight_ref, orb_buf, int_buf, out_buf, int_sem, orb_sem, out_sem):
-    chunks, capacity, block, lanes = int_buf.shape
-    rows = out_buf.shape[1]
+    capacity, block, width = int_buf.shape
+    lanes, rows = width // THIRDS, out_buf.shape[0] // THIRDS
     occ = orb_buf.shape[0]
     row_blocks, block_count = mask_ref.shape
     low = lax.broadcasted_iota(jnp.int32, (occ, 2 * block), 1) < block
 
     def load(c):
-        return pltpu.make_async_copy(int_ref.at[:, :, pl.ds(c * lanes, lanes)], int_buf.at[c], int_sem.at[c])
+        part = pl.ds(CHUNKS[c][0] * lanes, CHUNKS[c][1] * lanes)
+        return pltpu.make_async_copy(int_ref.at[:, :, part], int_buf.at[:, :, part], int_sem.at[c])
 
     orb_load = pltpu.make_async_copy(orb_ref, orb_buf, orb_sem)
     orb_load.start()
-    for c in range(chunks):
+    for c in range(len(CHUNKS)):
         load(c).start()
 
     position = lax.broadcasted_iota(jnp.int32, mask_ref.shape, 0) * block_count + lax.broadcasted_iota(
@@ -54,48 +56,48 @@
                 low, chosen[0], chosen[1]
             ).astype(weight_ref.dtype)
 
-    def store(c):
-        return pltpu.make_async_copy(out_buf.at[c], whole_ref.at[pl.ds(c * rows, rows)], out_sem.at[c])
-
-    for c in range(chunks):
+    def store(n):
+        part = pl.ds(n * rows, rows)
+        return pltpu.make_async_copy(out_buf.at[part], whole_ref.at[part], out_sem.at[n])
+
+    for c, (begin, count) in enumerate(CHUNKS):
         load(c).wait()
-        packed = int_buf[c].reshape(capacity * block, lanes)
-        product = jnp.dot(weight_ref[...], packed, preferred_element_type=jnp.float32)
-        for pair in range(lanes // (2 * block)):
-            first = product[:occ, pair * 2 * block : (pair + 1) * 2 * block]
-            second = product[occ:, pair * 2 * block : (pair + 1) * 2 * block]
-            out_buf[c, 2 * pair * occ : (2 * pair + 1) * occ, :] = jnp.where(
-                low, first, pltpu.roll(second, block, 1)
-            ).astype(out_buf.dtype)
-            out_buf[c, (2 * pair + 1) * occ : (2 * pair + 2) * occ, :] = jnp.where(
-                low, pltpu.roll(first, block, 1), second
-            ).astype(out_buf.dtype)
-        store(c).start()
-    for c in range(chunks):
-        store(c).wait()
+        for n in range(begin, begin + count):
+            packed = int_buf[:, :, n * lanes : (n + 1) * lanes].reshape(capacity * block, lanes)
+            product = jnp.dot(weight_ref[...], packed, preferred_element_type=jnp.float32)
+            for pair in range(lanes // (2 * block)):
+                first = product[:occ, pair * 2 * block : (pair + 1) * 2 * block]
+                second = product[occ:, pair * 2 * block : (pair + 1) * 2 * block]
+                at = n * rows + 2 * pair * occ
+                out_buf[at : at + occ, :] = jnp.where(low, first, pltpu.roll(second, block, 1)).astype(out_buf.dtype)
+                out_buf[at + occ : at + 2 * occ, :] = jnp.where(
+                    low, pltpu.roll(first, block, 1), second
+                ).astype(out_buf.dtype)
+            store(n).start()
+    for n in range(THIRDS):
+        store(n).wait()
 
 
 def half_transform(mask, slots, packed, orbitals):
     capacity, block, width = packed.shape
     occ = orbitals.shape[0]
-    lanes = width // CHUNKS
-    rows = lanes // block * occ
+    rows = width // block * occ
     vmem = pl.BlockSpec(memory_space=pltpu.VMEM)
     anywhere = pl.BlockSpec(memory_space=pl.ANY)
     return pl.pallas_call(
         half_kernel,
-        out_shape=jax.ShapeDtypeStruct((rows * CHUNKS, 2 * block), jnp.bfloat16),
+        out_shape=jax.ShapeDtypeStruct((rows, 2 * block), jnp.bfloat16),
         in_specs=[vmem, vmem, anywhere, anywhere],
         out_specs=anywhere,
         scratch_shapes=[
             pltpu.SMEM((capacity,), jnp.int32),
             pltpu.VMEM((2 * occ, capacity * block), jnp.bfloat16),
             pltpu.VMEM(orbitals.shape, jnp.bfloat16),
-            pltpu.VMEM((CHUNKS, capacity, block, lanes), jnp.bfloat16),
-            pltpu.VMEM((CHUNKS, rows, 2 * block), jnp.bfloat16),
-            pltpu.SemaphoreType.DMA((CHUNKS,)),
+            pltpu.VMEM(packed.shape, jnp.bfloat16),
+            pltpu.VMEM((rows, 2 * block), jnp.bfloat16),
+            pltpu.SemaphoreType.DMA((len(CHUNKS),)),
             pltpu.SemaphoreType.DMA,
-            pltpu.SemaphoreType.DMA((CHUNKS,)),
+            pltpu.SemaphoreType.DMA((THIRDS,)),
         ],
         compiler_params=pltpu.CompilerParams(vmem_limit_bytes=WIDE_LIMIT),
         cost_estimate=pl.CostEstimate(flops=2 * 2 * occ * capacity * block * width, bytes_accessed=5 << 20, transcendentals=0),

time: 92.6 us -> 92.7 us (level)
  no operation moved by 1% of the time
where the time goes in v5:
time: 92.7 us; the launch traced here: 92.6 us
  waiting for transfers between devices  33 us (36%)
  starting transfers between devices  27.2 us (29%)
  blocking collectives  20.3 us (22%)
  Pallas kernels  10.7 us (12%)
  local copies, waits for them, and re-layouts  1.14 us (1%)
    ppermute x7, waiting for transfers between devices, hop(): return lax.ppermute(panel, ('row', 'col'), along)  33 us
    ppermute x7, starting transfers between devices, hop(): return lax.ppermute(panel, ('row', 'col'), along)  26.7 us
    all_to_all x1, blocking collectives, local(): received = lax.all_to_all(sums, 'aux', 0, 0, tiled=True)  20.3 us
    pallas_call x2, Pallas kernels, early_tiles(): pl.pallas_call(functools.partial(early_kernel, orders, own), out_shape=tu...  4.85 us
    pallas_call x1, Pallas kernels, half_transform(): pl.pallas_call(half_kernel, out_shape=jax.ShapeDtypeStruct((rows, 2 * blo...  4.2 us
  transfers between devices with their start and end apart: 12, of which 7 were waited for; matrix products, arithmetic and copies ran while one was open for 0% of the time, Pallas kernels for 5%

profile of v5, /device:TPU:16, one launch (start us, length us, event | category | flops | bytes accessed | tf_op | source)
XLA Modules:
  0.0 92.6 jit_solution(1948745019717201946)
XLA Ops:
  0.0 4.2 %shard_map.46.refs_0_.refs_4_ = bf16[3072,128]{1,0:T(8,128)(2,1)} custom-call(s32[2,64]{1,0:T(2,128)} %bitcast.4, s32[2,64]{1,0:T(2,128)} %bitcast.5, bf16[64,4096]{1,0:T(8,128)(2,1)} %orb_ref.1, bf16[8,64,3072]{2,1,0:T(8,128)(2,1)} %bitcast.3), custom_call_target="tpu_custom_call" | custom-call | flops 402653184 | bytes 5242880 | tf_op jit(solution)/shard_map/pallas_call | solution.py:87
  4.2 0.1 collective-permute-start
  4.3 5.9 %collective-permute-start.2 = (bf16[3072,128]{1,0:T(8,128)(2,1)}, bf16[3072,128]{1,0:T(8,128)(2,1)S(1)}, u32[]{:S(2)}, u32[]{:S(2)}) collective-permute-start(bf16[3072,128]{1,0:T(8,128)(2,1)} %shard_map.46.refs_0_.refs_4_), channel_id=1, source_target_pairs={{0,56},{8,0},{16,8},{24,16},{32,24},{40,32},{48,40},{56,48},{64,72... | collective-permute-start | bytes 2359304 | tf_op jit(solution)/shard_map/ppermute | solution.py:250
  10.2 0.0 collective-permute-done.refs_1_.refs_5_
  10.2 2.4 %collective-permute-start.5 = (bf16[3072,128]{1,0:T(8,128)(2,1)S(1)}, bf16[3072,128]{1,0:T(8,128)(2,1)S(1)}, u32[]{:S(2)}, u32[]{:S(2)}) collective-permute-start(bf16[3072,128]{1,0:T(8,128)(2,1)S(1)} %collective-permute-done.refs_1_.refs_5_), channel_id=1, source_target_pairs={{0,56},{8,0},{16,8},{24,16},{32,24},{40,32},{48,40},{56,48},{64,72... | collective-permute-start | bytes 2359304 | tf_op jit(solution)/shard_map/ppermute | solution.py:250
  12.6 0.3 collective-permute-start.1
  13.0 7.1 %collective-permute-done.2.refs_5_ = bf16[3072,128]{1,0:T(8,128)(2,1)S(1)} collective-permute-done((bf16[3072,128]{1,0:T(8,128)(2,1)}, bf16[3072,128]{1,0:T(8,128)(2,1)S(1)}, u32[]{:S(2)}, u32[]{:S(2)}) %collective-permute-start.2) | collective-permute-done | bytes 786464 | tf_op jit(solution)/shard_map/ppermute | solution.py:250
  20.1 3.6 %collective-permute-start.3 = (bf16[3072,128]{1,0:T(8,128)(2,1)S(1)}, bf16[3072,128]{1,0:T(8,128)(2,1)S(1)}, u32[]{:S(2)}, u32[]{:S(2)}) collective-permute-start(bf16[3072,128]{1,0:T(8,128)(2,1)S(1)} %collective-permute-done.2.refs_5_), channel_id=1, source_target_pairs={{0,56},{8,0},{16,8},{24,16},{32,24},{40,32},{48,40},{56,48},{64,72... | collective-permute-start | bytes 2359304 | tf_op jit(solution)/shard_map/ppermute | solution.py:250
  23.6 4.7 %collective-permute-done.5.refs_7_ = bf16[3072,128]{1,0:T(8,128)(2,1)S(1)} collective-permute-done((bf16[3072,128]{1,0:T(8,128)(2,1)S(1)}, bf16[3072,128]{1,0:T(8,128)(2,1)S(1)}, u32[]{:S(2)}, u32[]{:S(2)}) %collective-permute-start.5) | collective-permute-done | bytes 786464 | tf_op jit(solution)/shard_map/ppermute | solution.py:250
  28.4 3.7 %collective-permute-start.6 = (bf16[3072,128]{1,0:T(8,128)(2,1)S(1)}, bf16[3072,128]{1,0:T(8,128)(2,1)S(1)}, u32[]{:S(2)}, u32[]{:S(2)}) collective-permute-start(bf16[3072,128]{1,0:T(8,128)(2,1)S(1)} %collective-permute-done.5.refs_7_), channel_id=1, source_target_pairs={{0,56},{8,0},{16,8},{24,16},{32,24},{40,32},{48,40},{56,48},{64,72... | collective-permute-start | bytes 2359304 | tf_op jit(solution)/shard_map/ppermute | solution.py:250
  32.1 0.0 collective-permute-done.1.refs_2_.refs_6_
  32.1 4.7 %collective-permute-done.3.refs_6_ = bf16[3072,128]{1,0:T(8,128)(2,1)S(1)} collective-permute-done((bf16[3072,128]{1,0:T(8,128)(2,1)S(1)}, bf16[3072,128]{1,0:T(8,128)(2,1)S(1)}, u32[]{:S(2)}, u32[]{:S(2)}) %collective-permute-start.3) | collective-permute-done | bytes 786464 | tf_op jit(solution)/shard_map/ppermute | solution.py:250
  36.8 0.0 collective-permute-start.4
  36.8 3.7 %collective-permute-start.7 = (bf16[3072,128]{1,0:T(8,128)(2,1)S(1)}, bf16[3072,128]{1,0:T(8,128)(2,1)S(1)}, u32[]{:S(2)}, u32[]{:S(2)}) collective-permute-start(bf16[3072,128]{1,0:T(8,128)(2,1)S(1)} %collective-permute-done.3.refs_6_), channel_id=1, source_target_pairs={{0,56},{8,0},{16,8},{24,16},{32,24},{40,32},{48,40},{56,48},{64,72... | collective-permute-start | bytes 2359304 | tf_op jit(solution)/shard_map/ppermute | solution.py:250
  40.5 4.7 %collective-permute-done.6.refs_8_ = bf16[3072,128]{1,0:T(8,128)(2,1)S(1)} collective-permute-done((bf16[3072,128]{1,0:T(8,128)(2,1)S(1)}, bf16[3072,128]{1,0:T(8,128)(2,1)S(1)}, u32[]{:S(2)}, u32[]{:S(2)}) %collective-permute-start.6) | collective-permute-done | bytes 786464 | tf_op jit(solution)/shard_map/ppermute | solution.py:250
  45.2 3.7 %collective-permute-start.8 = (bf16[3072,128]{1,0:T(8,128)(2,1)S(1)}, bf16[3072,128]{1,0:T(8,128)(2,1)S(1)}, u32[]{:S(2)}, u32[]{:S(2)}) collective-permute-start(bf16[3072,128]{1,0:T(8,128)(2,1)S(1)} %collective-permute-done.6.refs_8_), channel_id=1, source_target_pairs={{0,56},{8,0},{16,8},{24,16},{32,24},{40,32},{48,40},{56,48},{64,72... | collective-permute-start | bytes 2359304 | tf_op jit(solution)/shard_map/ppermute | solution.py:250
  48.9 0.0 collective-permute-done.4.refs_3_.refs_7_
  48.9 0.0 copy-start
  48.9 1.1 %copy-done = bf16[3072,128]{1,0:T(8,128)(2,1)S(1)} copy-done((bf16[3072,128]{1,0:T(8,128)(2,1)S(1)}, bf16[3072,128]{1,0:T(8,128)(2,1)}, u32[]{:S(2)}) %copy-start) | copy-done | bytes 786456
  50.1 3.5 %shard_map.47 = (bf16[3,128,512]{2,1,0:T(8,128)(2,1)S(1)}, bf16[2,128,512]{2,1,0:T(8,128)(2,1)S(1)}) custom-call(bf16[3072,128]{1,0:T(8,128)(2,1)S(1)} %copy-done, bf16[3072,128]{1,0:T(8,128)(2,1)S(1)} %collective-permute-done.refs_1_.refs_5_, bf16[3072,128]{1,0:T(8,128)(2,1)S(1)} %collective-permute-done.1.refs_2_.refs_6_, ...), custom_call_target="tpu_custom_call" | custom-call | flops 2013265920 | bytes 7340032 | tf_op jit(solution)/shard_map/pallas_call | solution.py:167
  53.6 0.0 copy-start.1
  53.6 0.1 collective-permute-done.7.refs_4_
  53.7 3.7 %collective-permute-start.11 = (bf16[3072,128]{1,0:T(8,128)(2,1)S(1)}, bf16[3072,128]{1,0:T(8,128)(2,1)S(1)}, u32[]{:S(2)}, u32[]{:S(2)}) collective-permute-start(bf16[3072,128]{1,0:T(8,128)(2,1)S(1)} %collective-permute-done.7.refs_4_), channel_id=1, source_target_pairs={{0,56},{8,0},{16,8},{24,16},{32,24},{40,32},{48,40},{56,48},{64,72... | collective-permute-start | bytes 2359304 | tf_op jit(solution)/shard_map/ppermute | solution.py:250
  57.4 0.0 collective-permute-start.9
  57.4 4.7 %collective-permute-done.8.refs_5_ = bf16[3072,128]{1,0:T(8,128)(2,1)S(1)} collective-permute-done((bf16[3072,128]{1,0:T(8,128)(2,1)S(1)}, bf16[3072,128]{1,0:T(8,128)(2,1)S(1)}, u32[]{:S(2)}, u32[]{:S(2)}) %collective-permute-start.8) | collective-permute-done | bytes 786464 | tf_op jit(solution)/shard_map/ppermute | solution.py:250
  62.1 1.3 %shard_map.48 = (bf16[1,128,512]{2,1,0:T(8,128)(2,1)S(1)}, bf16[1,128,512]{2,1,0:T(8,128)(2,1)S(1)}) custom-call(bf16[3072,128]{1,0:T(8,128)(2,1)S(1)} %copy-done, bf16[3072,128]{1,0:T(8,128)(2,1)S(1)} %collective-permute-done.refs_1_.refs_5_, bf16[3072,128]{1,0:T(8,128)(2,1)S(1)} %collective-permute-done.1.refs_2_.refs_6_, ...), custom_call_target="tpu_custom_call" | custom-call | flops 805306368 | bytes 7340032 | tf_op jit(solution)/shard_map/pallas_call | solution.py:167
  63.4 0.1 collective-permute-start.10
  63.5 0.0 collective-permute-done.9.refs_2_
  63.6 7.0 %collective-permute-done.11.refs_8_ = bf16[3072,128]{1,0:T(8,128)(2,1)S(1)} collective-permute-done((bf16[3072,128]{1,0:T(8,128)(2,1)S(1)}, bf16[3072,128]{1,0:T(8,128)(2,1)S(1)}, u32[]{:S(2)}, u32[]{:S(2)}) %collective-permute-start.11) | collective-permute-done | bytes 786464 | tf_op jit(solution)/shard_map/ppermute | solution.py:250
  70.5 0.0 collective-permute-done.10.refs_3_
  70.5 0.0 copy-done.1
  70.5 0.6 shard_map.49
  71.1 20.3 %all_to_all.5.in_ref = bf16[8,128,512]{2,1,0:T(8,128)(2,1)S(1)} all-to-all(bf16[8,128,512]{2,1,0:T(8,128)(2,1)S(1)} %shard_map.49), channel_id=1, replica_groups=mesh['row'=4,'col'=8,'aux'=8] {'aux'}, dimensions={0} | all-to-all | bytes 2097152 | tf_op jit(solution)/shard_map/all_to_all | solution.py:273
  91.5 1.1 %shard_map.50 = f32[128,4,128]{2,1,0:T(4,128)} custom-call(bf16[8,128,512]{2,1,0:T(8,128)(2,1)S(1)} %all_to_all.5.in_ref), custom_call_target="tpu_custom_call" | custom-call | flops 524288 | bytes 1048576 | tf_op jit(solution)/shard_map/pallas_call | solution.py:229
Async XLA Ops:
  4.2 6.0 %collective-permute-start = (bf16[3072,128]{1,0:T(8,128)(2,1)}, bf16[3072,128]{1,0:T(8,128)(2,1)S(1)}, u32[]{:S(2)}, u32[]{:S(2)}) collective-permute-start(bf16[3072,128]{1,0:T(8,128)(2,1)} %shard_map.46.refs_0_.refs_4_), channel_id=1, source_target_pairs={{0,64},{64,0},{128,192},{192,128},{1,65},{65,1},{129,193},{193,129... | collective-permute-start | bytes 2359304 | tf_op jit(solution)/shard_map/ppermute | solution.py:253
  4.3 15.8 %collective-permute-start.2 = (bf16[3072,128]{1,0:T(8,128)(2,1)}, bf16[3072,128]{1,0:T(8,128)(2,1)S(1)}, u32[]{:S(2)}, u32[]{:S(2)}) collective-permute-start(bf16[3072,128]{1,0:T(8,128)(2,1)} %shard_map.46.refs_0_.refs_4_), channel_id=1, source_target_pairs={{0,56},{8,0},{16,8},{24,16},{32,24},{40,32},{48,40},{56,48},{64,72... | collective-permute-start | bytes 2359304 | tf_op jit(solution)/shard_map/ppermute | solution.py:250
  10.2 18.1 %collective-permute-start.5 = (bf16[3072,128]{1,0:T(8,128)(2,1)S(1)}, bf16[3072,128]{1,0:T(8,128)(2,1)S(1)}, u32[]{:S(2)}, u32[]{:S(2)}) collective-permute-start(bf16[3072,128]{1,0:T(8,128)(2,1)S(1)} %collective-permute-done.refs_1_.refs_5_), channel_id=1, source_target_pairs={{0,56},{8,0},{16,8},{24,16},{32,24},{40,32},{48,40},{56,48},{64,72... | collective-permute-start | bytes 2359304 | tf_op jit(solution)/shard_map/ppermute | solution.py:250
  12.6 19.4 %collective-permute-start.1 = (bf16[3072,128]{1,0:T(8,128)(2,1)}, bf16[3072,128]{1,0:T(8,128)(2,1)S(1)}, u32[]{:S(2)}, u32[]{:S(2)}) collective-permute-start(bf16[3072,128]{1,0:T(8,128)(2,1)} %shard_map.46.refs_0_.refs_4_), channel_id=1, source_target_pairs={{0,128},{64,192},{128,0},{192,64},{1,129},{65,193},{129,1},{193,65... | collective-permute-start | bytes 2359304 | tf_op jit(solution)/shard_map/ppermute | solution.py:253
  20.1 16.7 %collective-permute-start.3 = (bf16[3072,128]{1,0:T(8,128)(2,1)S(1)}, bf16[3072,128]{1,0:T(8,128)(2,1)S(1)}, u32[]{:S(2)}, u32[]{:S(2)}) collective-permute-start(bf16[3072,128]{1,0:T(8,128)(2,1)S(1)} %collective-permute-done.2.refs_5_), channel_id=1, source_target_pairs={{0,56},{8,0},{16,8},{24,16},{32,24},{40,32},{48,40},{56,48},{64,72... | collective-permute-start | bytes 2359304 | tf_op jit(solution)/shard_map/ppermute | solution.py:250
  28.4 16.9 %collective-permute-start.6 = (bf16[3072,128]{1,0:T(8,128)(2,1)S(1)}, bf16[3072,128]{1,0:T(8,128)(2,1)S(1)}, u32[]{:S(2)}, u32[]{:S(2)}) collective-permute-start(bf16[3072,128]{1,0:T(8,128)(2,1)S(1)} %collective-permute-done.5.refs_7_), channel_id=1, source_target_pairs={{0,56},{8,0},{16,8},{24,16},{32,24},{40,32},{48,40},{56,48},{64,72... | collective-permute-start | bytes 2359304 | tf_op jit(solution)/shard_map/ppermute | solution.py:250
  36.8 12.1 %collective-permute-start.4 = (bf16[3072,128]{1,0:T(8,128)(2,1)S(1)}, bf16[3072,128]{1,0:T(8,128)(2,1)S(1)}, u32[]{:S(2)}, u32[]{:S(2)}) collective-permute-start(bf16[3072,128]{1,0:T(8,128)(2,1)S(1)} %collective-permute-done.1.refs_2_.refs_6_), channel_id=1, source_target_pairs={{0,64},{64,0},{128,192},{192,128},{1,65},{65,1},{129,193},{193,129... | collective-permute-start | bytes 2359304 | tf_op jit(solution)/shard_map/ppermute | solution.py:253
  36.8 16.8 %collective-permute-start.7 = (bf16[3072,128]{1,0:T(8,128)(2,1)S(1)}, bf16[3072,128]{1,0:T(8,128)(2,1)S(1)}, u32[]{:S(2)}, u32[]{:S(2)}) collective-permute-start(bf16[3072,128]{1,0:T(8,128)(2,1)S(1)} %collective-permute-done.3.refs_6_), channel_id=1, source_target_pairs={{0,56},{8,0},{16,8},{24,16},{32,24},{40,32},{48,40},{56,48},{64,72... | collective-permute-start | bytes 2359304 | tf_op jit(solution)/shard_map/ppermute | solution.py:250
  45.2 16.9 %collective-permute-start.8 = (bf16[3072,128]{1,0:T(8,128)(2,1)S(1)}, bf16[3072,128]{1,0:T(8,128)(2,1)S(1)}, u32[]{:S(2)}, u32[]{:S(2)}) collective-permute-start(bf16[3072,128]{1,0:T(8,128)(2,1)S(1)} %collective-permute-done.6.refs_8_), channel_id=1, source_target_pairs={{0,56},{8,0},{16,8},{24,16},{32,24},{40,32},{48,40},{56,48},{64,72... | collective-permute-start | bytes 2359304 | tf_op jit(solution)/shard_map/ppermute | solution.py:250
  48.9 1.1 %copy-start = (bf16[3072,128]{1,0:T(8,128)(2,1)S(1)}, bf16[3072,128]{1,0:T(8,128)(2,1)}, u32[]{:S(2)}) copy-start(bf16[3072,128]{1,0:T(8,128)(2,1)} %shard_map.46.refs_0_.refs_4_) | copy-start | bytes 2359300
  53.6 16.9 %copy-start.1 = (bf16[3072,128]{1,0:T(8,128)(2,1)S(1)}, bf16[3072,128]{1,0:T(8,128)(2,1)}, u32[]{:S(2)}) copy-start(bf16[3072,128]{1,0:T(8,128)(2,1)} %shard_map.46.refs_0_.refs_4_) | copy-start | bytes 2359300
  53.7 16.9 %collective-permute-start.11 = (bf16[3072,128]{1,0:T(8,128)(2,1)S(1)}, bf16[3072,128]{1,0:T(8,128)(2,1)S(1)}, u32[]{:S(2)}, u32[]{:S(2)}) collective-permute-start(bf16[3072,128]{1,0:T(8,128)(2,1)S(1)} %collective-permute-done.7.refs_4_), channel_id=1, source_target_pairs={{0,56},{8,0},{16,8},{24,16},{32,24},{40,32},{48,40},{56,48},{64,72... | collective-permute-start | bytes 2359304 | tf_op jit(solution)/shard_map/ppermute | solution.py:250
  57.4 6.2 %collective-permute-start.9 = (bf16[2,128,512]{2,1,0:T(8,128)(2,1)S(1)}, bf16[2,128,512]{2,1,0:T(8,128)(2,1)S(1)}, u32[]{:S(2)}, u32[]{:S(2)}) collective-permute-start(bf16[2,128,512]{2,1,0:T(8,128)(2,1)S(1)} %get-tuple-element.21), channel_id=1, source_target_pairs={{0,64},{64,0},{128,192},{192,128},{1,65},{65,1},{129,193},{193,129... | collective-permute-start | bytes 786440 | tf_op jit(solution)/shard_map/ppermute | solution.py:253
  63.4 7.1 %collective-permute-start.10 = (bf16[1,128,512]{2,1,0:T(8,128)(2,1)S(1)}, bf16[1,128,512]{2,1,0:T(8,128)(2,1)S(1)}, u32[]{:S(2)}, u32[]{:S(2)}) collective-permute-start(bf16[1,128,512]{2,1,0:T(8,128)(2,1)S(1)} %get-tuple-element.22), channel_id=1, source_target_pairs={{0,64},{64,0},{128,192},{192,128},{1,65},{65,1},{129,193},{193,129... | collective-permute-start | bytes 393224 | tf_op jit(solution)/shard_map/ppermute | solution.py:253

commit v6 on v4

--- a/solution.py
+++ b/solution.py
@@ -262,7 +262,7 @@
     near = early_tiles(col_panels, kept, sent, True)
     third = hop(kept[2])
     third_sent = hop(sent[1])
-    near_kept, near_sent, third = lax.optimization_barrier((*near, third))
+    near_kept, near_sent = near
     far = hop(third)
     near_other = to_row(near_sent, 1)
     outer_kept, outer_sent = early_tiles(col_panels, [third], [third_sent], False)

time: 92.6 us -> 92.6 us (level)
  transfers between devices with their start and end apart: 12 -> 12, of which waited for: 7 -> 6; matrix products, arithmetic and copies ran while one was open for 0% -> 0% of each run, Pallas kernels for 5% -> 5%
where the time goes in v6:
time: 92.6 us; the launch traced here: 92.4 us
  waiting for transfers between devices  32.5 us (35%)
  starting transfers between devices  27.8 us (30%)
  blocking collectives  20.3 us (22%)
  Pallas kernels  10.6 us (11%)
  local copies, waits for them, and re-layouts  1.14 us (1%)
    ppermute x7, waiting for transfers between devices, hop(): return lax.ppermute(panel, ('row', 'col'), along)  32.5 us
    ppermute x7, starting transfers between devices, hop(): return lax.ppermute(panel, ('row', 'col'), along)  26.7 us
    all_to_all x1, blocking collectives, local(): received = lax.all_to_all(sums, 'aux', 0, 0, tiled=True)  20.3 us
    pallas_call x2, Pallas kernels, early_tiles(): pl.pallas_call(functools.partial(early_kernel, orders, own), out_shape=tu...  4.84 us
    pallas_call x1, Pallas kernels, half_transform(): pl.pallas_call(half_kernel, out_shape=jax.ShapeDtypeStruct((rows * CHUNKS...  4.05 us
  transfers between devices with their start and end apart: 12, of which 6 were waited for; matrix products, arithmetic and copies ran while one was open for 0% of the time, Pallas kernels for 5%

profile of v6, /device:TPU:16, one launch (start us, length us, event | category | flops | bytes accessed | tf_op | source)
XLA Modules:
  0.0 92.4 jit_solution(2611980145133310619)
XLA Ops:
  0.0 4.0 %shard_map.46.refs_0_.refs_4_ = bf16[3072,128]{1,0:T(8,128)(2,1)} custom-call(s32[2,64]{1,0:T(2,128)} %bitcast.4, s32[2,64]{1,0:T(2,128)} %bitcast.5, bf16[64,4096]{1,0:T(8,128)(2,1)} %orb_ref.1, bf16[8,64,3072]{2,1,0:T(8,128)(2,1)} %bitcast.3), custom_call_target="tpu_custom_call" | custom-call | flops 402653184 | bytes 5242880 | tf_op jit(solution)/shard_map/pallas_call | solution.py:85
  4.1 0.1 collective-permute-start
  4.2 5.9 %collective-permute-start.2 = (bf16[3072,128]{1,0:T(8,128)(2,1)}, bf16[3072,128]{1,0:T(8,128)(2,1)S(1)}, u32[]{:S(2)}, u32[]{:S(2)}) collective-permute-start(bf16[3072,128]{1,0:T(8,128)(2,1)} %shard_map.46.refs_0_.refs_4_), channel_id=1, source_target_pairs={{0,56},{8,0},{16,8},{24,16},{32,24},{40,32},{48,40},{56,48},{64,72... | collective-permute-start | bytes 2359304 | tf_op jit(solution)/shard_map/ppermute | solution.py:248
  10.1 0.0 collective-permute-done.refs_1_.refs_5_
  10.1 2.4 %collective-permute-start.5 = (bf16[3072,128]{1,0:T(8,128)(2,1)S(1)}, bf16[3072,128]{1,0:T(8,128)(2,1)S(1)}, u32[]{:S(2)}, u32[]{:S(2)}) collective-permute-start(bf16[3072,128]{1,0:T(8,128)(2,1)S(1)} %collective-permute-done.refs_1_.refs_5_), channel_id=1, source_target_pairs={{0,56},{8,0},{16,8},{24,16},{32,24},{40,32},{48,40},{56,48},{64,72... | collective-permute-start | bytes 2359304 | tf_op jit(solution)/shard_map/ppermute | solution.py:248
  12.5 0.3 collective-permute-start.1
  12.8 7.1 %collective-permute-done.2.refs_5_ = bf16[3072,128]{1,0:T(8,128)(2,1)S(1)} collective-permute-done((bf16[3072,128]{1,0:T(8,128)(2,1)}, bf16[3072,128]{1,0:T(8,128)(2,1)S(1)}, u32[]{:S(2)}, u32[]{:S(2)}) %collective-permute-start.2) | collective-permute-done | bytes 786464 | tf_op jit(solution)/shard_map/ppermute | solution.py:248
  19.9 3.6 %collective-permute-start.3 = (bf16[3072,128]{1,0:T(8,128)(2,1)S(1)}, bf16[3072,128]{1,0:T(8,128)(2,1)S(1)}, u32[]{:S(2)}, u32[]{:S(2)}) collective-permute-start(bf16[3072,128]{1,0:T(8,128)(2,1)S(1)} %collective-permute-done.2.refs_5_), channel_id=1, source_target_pairs={{0,56},{8,0},{16,8},{24,16},{32,24},{40,32},{48,40},{56,48},{64,72... | collective-permute-start | bytes 2359304 | tf_op jit(solution)/shard_map/ppermute | solution.py:248
  23.5 4.7 %collective-permute-done.5.refs_7_ = bf16[3072,128]{1,0:T(8,128)(2,1)S(1)} collective-permute-done((bf16[3072,128]{1,0:T(8,128)(2,1)S(1)}, bf16[3072,128]{1,0:T(8,128)(2,1)S(1)}, u32[]{:S(2)}, u32[]{:S(2)}) %collective-permute-start.5) | collective-permute-done | bytes 786464 | tf_op jit(solution)/shard_map/ppermute | solution.py:248
  28.2 3.7 %collective-permute-start.6 = (bf16[3072,128]{1,0:T(8,128)(2,1)S(1)}, bf16[3072,128]{1,0:T(8,128)(2,1)S(1)}, u32[]{:S(2)}, u32[]{:S(2)}) collective-permute-start(bf16[3072,128]{1,0:T(8,128)(2,1)S(1)} %collective-permute-done.5.refs_7_), channel_id=1, source_target_pairs={{0,56},{8,0},{16,8},{24,16},{32,24},{40,32},{48,40},{56,48},{64,72... | collective-permute-start | bytes 2359304 | tf_op jit(solution)/shard_map/ppermute | solution.py:248
  31.9 0.0 collective-permute-done.1.refs_2_.refs_6_
  31.9 4.7 %collective-permute-done.3.refs_6_ = bf16[3072,128]{1,0:T(8,128)(2,1)S(1)} collective-permute-done((bf16[3072,128]{1,0:T(8,128)(2,1)S(1)}, bf16[3072,128]{1,0:T(8,128)(2,1)S(1)}, u32[]{:S(2)}, u32[]{:S(2)}) %collective-permute-start.3) | collective-permute-done | bytes 786464 | tf_op jit(solution)/shard_map/ppermute | solution.py:248
  36.7 3.7 %collective-permute-start.7 = (bf16[3072,128]{1,0:T(8,128)(2,1)S(1)}, bf16[3072,128]{1,0:T(8,128)(2,1)S(1)}, u32[]{:S(2)}, u32[]{:S(2)}) collective-permute-start(bf16[3072,128]{1,0:T(8,128)(2,1)S(1)} %collective-permute-done.3.refs_6_), channel_id=1, source_target_pairs={{0,56},{8,0},{16,8},{24,16},{32,24},{40,32},{48,40},{56,48},{64,72... | collective-permute-start | bytes 2359304 | tf_op jit(solution)/shard_map/ppermute | solution.py:248
  40.4 0.0 collective-permute-start.4
  40.4 4.7 %collective-permute-done.6.refs_8_ = bf16[3072,128]{1,0:T(8,128)(2,1)S(1)} collective-permute-done((bf16[3072,128]{1,0:T(8,128)(2,1)S(1)}, bf16[3072,128]{1,0:T(8,128)(2,1)S(1)}, u32[]{:S(2)}, u32[]{:S(2)}) %collective-permute-start.6) | collective-permute-done | bytes 786464 | tf_op jit(solution)/shard_map/ppermute | solution.py:248
  45.1 3.7 %collective-permute-start.8 = (bf16[3072,128]{1,0:T(8,128)(2,1)S(1)}, bf16[3072,128]{1,0:T(8,128)(2,1)S(1)}, u32[]{:S(2)}, u32[]{:S(2)}) collective-permute-start(bf16[3072,128]{1,0:T(8,128)(2,1)S(1)} %collective-permute-done.6.refs_8_), channel_id=1, source_target_pairs={{0,56},{8,0},{16,8},{24,16},{32,24},{40,32},{48,40},{56,48},{64,72... | collective-permute-start | bytes 2359304 | tf_op jit(solution)/shard_map/ppermute | solution.py:248
  48.8 4.7 %collective-permute-done.7.refs_4_ = bf16[3072,128]{1,0:T(8,128)(2,1)S(1)} collective-permute-done((bf16[3072,128]{1,0:T(8,128)(2,1)S(1)}, bf16[3072,128]{1,0:T(8,128)(2,1)S(1)}, u32[]{:S(2)}, u32[]{:S(2)}) %collective-permute-start.7) | collective-permute-done | bytes 786464 | tf_op jit(solution)/shard_map/ppermute | solution.py:248
  53.5 3.7 %collective-permute-start.11 = (bf16[3072,128]{1,0:T(8,128)(2,1)S(1)}, bf16[3072,128]{1,0:T(8,128)(2,1)S(1)}, u32[]{:S(2)}, u32[]{:S(2)}) collective-permute-start(bf16[3072,128]{1,0:T(8,128)(2,1)S(1)} %collective-permute-done.7.refs_4_), channel_id=1, source_target_pairs={{0,56},{8,0},{16,8},{24,16},{32,24},{40,32},{48,40},{56,48},{64,72... | collective-permute-start | bytes 2359304 | tf_op jit(solution)/shard_map/ppermute | solution.py:248
  57.2 0.0 collective-permute-done.4.refs_3_.refs_7_
  57.2 0.0 copy-start
  57.2 1.1 %copy-done = bf16[3072,128]{1,0:T(8,128)(2,1)S(1)} copy-done((bf16[3072,128]{1,0:T(8,128)(2,1)S(1)}, bf16[3072,128]{1,0:T(8,128)(2,1)}, u32[]{:S(2)}) %copy-start) | copy-done | bytes 786456
  58.4 3.5 %shard_map.47 = (bf16[3,128,512]{2,1,0:T(8,128)(2,1)S(1)}, bf16[2,128,512]{2,1,0:T(8,128)(2,1)S(1)}) custom-call(bf16[3072,128]{1,0:T(8,128)(2,1)S(1)} %copy-done, bf16[3072,128]{1,0:T(8,128)(2,1)S(1)} %collective-permute-done.refs_1_.refs_5_, bf16[3072,128]{1,0:T(8,128)(2,1)S(1)} %collective-permute-done.1.refs_2_.refs_6_, ...), custom_call_target="tpu_custom_call" | custom-call | flops 2013265920 | bytes 7340032 | tf_op jit(solution)/shard_map/pallas_call | solution.py:165
  61.9 0.0 copy-start.1
  61.9 0.1 collective-permute-start.9
  62.0 0.0 collective-permute-done.8.refs_5_
  62.0 1.4 %shard_map.48 = (bf16[1,128,512]{2,1,0:T(8,128)(2,1)S(1)}, bf16[1,128,512]{2,1,0:T(8,128)(2,1)S(1)}) custom-call(bf16[3072,128]{1,0:T(8,128)(2,1)S(1)} %copy-done, bf16[3072,128]{1,0:T(8,128)(2,1)S(1)} %collective-permute-done.refs_1_.refs_5_, bf16[3072,128]{1,0:T(8,128)(2,1)S(1)} %collective-permute-done.1.refs_2_.refs_6_, ...), custom_call_target="tpu_custom_call" | custom-call | flops 805306368 | bytes 7340032 | tf_op jit(solution)/shard_map/pallas_call | solution.py:165
  63.3 0.6 collective-permute-start.10
  63.9 0.0 collective-permute-done.9.refs_2_
  63.9 6.5 %collective-permute-done.11.refs_8_ = bf16[3072,128]{1,0:T(8,128)(2,1)S(1)} collective-permute-done((bf16[3072,128]{1,0:T(8,128)(2,1)S(1)}, bf16[3072,128]{1,0:T(8,128)(2,1)S(1)}, u32[]{:S(2)}, u32[]{:S(2)}) %collective-permute-start.11) | collective-permute-done | bytes 786464 | tf_op jit(solution)/shard_map/ppermute | solution.py:248
  70.4 0.0 collective-permute-done.10.refs_3_
  70.4 0.0 copy-done.1
  70.4 0.6 shard_map.49
  71.0 20.3 %all_to_all.5.in_ref = bf16[8,128,512]{2,1,0:T(8,128)(2,1)S(1)} all-to-all(bf16[8,128,512]{2,1,0:T(8,128)(2,1)S(1)} %shard_map.49), channel_id=1, replica_groups=mesh['row'=4,'col'=8,'aux'=8] {'aux'}, dimensions={0} | all-to-all | bytes 2097152 | tf_op jit(solution)/shard_map/all_to_all | solution.py:271
  91.3 1.1 %shard_map.50 = f32[128,4,128]{2,1,0:T(4,128)} custom-call(bf16[8,128,512]{2,1,0:T(8,128)(2,1)S(1)} %all_to_all.5.in_ref), custom_call_target="tpu_custom_call" | custom-call | flops 524288 | bytes 1048576 | tf_op jit(solution)/shard_map/pallas_call | solution.py:227
Async XLA Ops:
  4.1 6.0 %collective-permute-start = (bf16[3072,128]{1,0:T(8,128)(2,1)}, bf16[3072,128]{1,0:T(8,128)(2,1)S(1)}, u32[]{:S(2)}, u32[]{:S(2)}) collective-permute-start(bf16[3072,128]{1,0:T(8,128)(2,1)} %shard_map.46.refs_0_.refs_4_), channel_id=1, source_target_pairs={{0,64},{64,0},{128,192},{192,128},{1,65},{65,1},{129,193},{193,129... | collective-permute-start | bytes 2359304 | tf_op jit(solution)/shard_map/ppermute | solution.py:251
  4.2 15.8 %collective-permute-start.2 = (bf16[3072,128]{1,0:T(8,128)(2,1)}, bf16[3072,128]{1,0:T(8,128)(2,1)S(1)}, u32[]{:S(2)}, u32[]{:S(2)}) collective-permute-start(bf16[3072,128]{1,0:T(8,128)(2,1)} %shard_map.46.refs_0_.refs_4_), channel_id=1, source_target_pairs={{0,56},{8,0},{16,8},{24,16},{32,24},{40,32},{48,40},{56,48},{64,72... | collective-permute-start | bytes 2359304 | tf_op jit(solution)/shard_map/ppermute | solution.py:248
  10.1 18.1 %collective-permute-start.5 = (bf16[3072,128]{1,0:T(8,128)(2,1)S(1)}, bf16[3072,128]{1,0:T(8,128)(2,1)S(1)}, u32[]{:S(2)}, u32[]{:S(2)}) collective-permute-start(bf16[3072,128]{1,0:T(8,128)(2,1)S(1)} %collective-permute-done.refs_1_.refs_5_), channel_id=1, source_target_pairs={{0,56},{8,0},{16,8},{24,16},{32,24},{40,32},{48,40},{56,48},{64,72... | collective-permute-start | bytes 2359304 | tf_op jit(solution)/shard_map/ppermute | solution.py:248
  12.5 19.4 %collective-permute-start.1 = (bf16[3072,128]{1,0:T(8,128)(2,1)}, bf16[3072,128]{1,0:T(8,128)(2,1)S(1)}, u32[]{:S(2)}, u32[]{:S(2)}) collective-permute-start(bf16[3072,128]{1,0:T(8,128)(2,1)} %shard_map.46.refs_0_.refs_4_), channel_id=1, source_target_pairs={{0,128},{64,192},{128,0},{192,64},{1,129},{65,193},{129,1},{193,65... | collective-permute-start | bytes 2359304 | tf_op jit(solution)/shard_map/ppermute | solution.py:251
  19.9 16.7 %collective-permute-start.3 = (bf16[3072,128]{1,0:T(8,128)(2,1)S(1)}, bf16[3072,128]{1,0:T(8,128)(2,1)S(1)}, u32[]{:S(2)}, u32[]{:S(2)}) collective-permute-start(bf16[3072,128]{1,0:T(8,128)(2,1)S(1)} %collective-permute-done.2.refs_5_), channel_id=1, source_target_pairs={{0,56},{8,0},{16,8},{24,16},{32,24},{40,32},{48,40},{56,48},{64,72... | collective-permute-start | bytes 2359304 | tf_op jit(solution)/shard_map/ppermute | solution.py:248
  28.2 16.9 %collective-permute-start.6 = (bf16[3072,128]{1,0:T(8,128)(2,1)S(1)}, bf16[3072,128]{1,0:T(8,128)(2,1)S(1)}, u32[]{:S(2)}, u32[]{:S(2)}) collective-permute-start(bf16[3072,128]{1,0:T(8,128)(2,1)S(1)} %collective-permute-done.5.refs_7_), channel_id=1, source_target_pairs={{0,56},{8,0},{16,8},{24,16},{32,24},{40,32},{48,40},{56,48},{64,72... | collective-permute-start | bytes 2359304 | tf_op jit(solution)/shard_map/ppermute | solution.py:248
  36.7 16.9 %collective-permute-start.7 = (bf16[3072,128]{1,0:T(8,128)(2,1)S(1)}, bf16[3072,128]{1,0:T(8,128)(2,1)S(1)}, u32[]{:S(2)}, u32[]{:S(2)}) collective-permute-start(bf16[3072,128]{1,0:T(8,128)(2,1)S(1)} %collective-permute-done.3.refs_6_), channel_id=1, source_target_pairs={{0,56},{8,0},{16,8},{24,16},{32,24},{40,32},{48,40},{56,48},{64,72... | collective-permute-start | bytes 2359304 | tf_op jit(solution)/shard_map/ppermute | solution.py:248
  40.4 16.9 %collective-permute-start.4 = (bf16[3072,128]{1,0:T(8,128)(2,1)S(1)}, bf16[3072,128]{1,0:T(8,128)(2,1)S(1)}, u32[]{:S(2)}, u32[]{:S(2)}) collective-permute-start(bf16[3072,128]{1,0:T(8,128)(2,1)S(1)} %collective-permute-done.1.refs_2_.refs_6_), channel_id=1, source_target_pairs={{0,64},{64,0},{128,192},{192,128},{1,65},{65,1},{129,193},{193,129... | collective-permute-start | bytes 2359304 | tf_op jit(solution)/shard_map/ppermute | solution.py:251
  45.1 16.9 %collective-permute-start.8 = (bf16[3072,128]{1,0:T(8,128)(2,1)S(1)}, bf16[3072,128]{1,0:T(8,128)(2,1)S(1)}, u32[]{:S(2)}, u32[]{:S(2)}) collective-permute-start(bf16[3072,128]{1,0:T(8,128)(2,1)S(1)} %collective-permute-done.6.refs_8_), channel_id=1, source_target_pairs={{0,56},{8,0},{16,8},{24,16},{32,24},{40,32},{48,40},{56,48},{64,72... | collective-permute-start | bytes 2359304 | tf_op jit(solution)/shard_map/ppermute | solution.py:248
  53.5 16.9 %collective-permute-start.11 = (bf16[3072,128]{1,0:T(8,128)(2,1)S(1)}, bf16[3072,128]{1,0:T(8,128)(2,1)S(1)}, u32[]{:S(2)}, u32[]{:S(2)}) collective-permute-start(bf16[3072,128]{1,0:T(8,128)(2,1)S(1)} %collective-permute-done.7.refs_4_), channel_id=1, source_target_pairs={{0,56},{8,0},{16,8},{24,16},{32,24},{40,32},{48,40},{56,48},{64,72... | collective-permute-start | bytes 2359304 | tf_op jit(solution)/shard_map/ppermute | solution.py:248
  57.2 1.1 %copy-start = (bf16[3072,128]{1,0:T(8,128)(2,1)S(1)}, bf16[3072,128]{1,0:T(8,128)(2,1)}, u32[]{:S(2)}) copy-start(bf16[3072,128]{1,0:T(8,128)(2,1)} %shard_map.46.refs_0_.refs_4_) | copy-start | bytes 2359300
  61.9 8.5 %copy-start.1 = (bf16[3072,128]{1,0:T(8,128)(2,1)S(1)}, bf16[3072,128]{1,0:T(8,128)(2,1)}, u32[]{:S(2)}) copy-start(bf16[3072,128]{1,0:T(8,128)(2,1)} %shard_map.46.refs_0_.refs_4_) | copy-start | bytes 2359300
  61.9 2.1 %collective-permute-start.9 = (bf16[2,128,512]{2,1,0:T(8,128)(2,1)S(1)}, bf16[2,128,512]{2,1,0:T(8,128)(2,1)S(1)}, u32[]{:S(2)}, u32[]{:S(2)}) collective-permute-start(bf16[2,128,512]{2,1,0:T(8,128)(2,1)S(1)} %get-tuple-element.15), channel_id=1, source_target_pairs={{0,64},{64,0},{128,192},{192,128},{1,65},{65,1},{129,193},{193,129... | collective-permute-start | bytes 786440 | tf_op jit(solution)/shard_map/ppermute | solution.py:251
  63.3 7.0 %collective-permute-start.10 = (bf16[1,128,512]{2,1,0:T(8,128)(2,1)S(1)}, bf16[1,128,512]{2,1,0:T(8,128)(2,1)S(1)}, u32[]{:S(2)}, u32[]{:S(2)}) collective-permute-start(bf16[1,128,512]{2,1,0:T(8,128)(2,1)S(1)} %get-tuple-element.16), channel_id=1, source_target_pairs={{0,64},{64,0},{128,192},{192,128},{1,65},{65,1},{129,193},{193,129... | collective-permute-start | bytes 393224 | tf_op jit(solution)/shard_map/ppermute | solution.py:251
